TPU v7x, 32 devices: a whole 2x2x4 slice. The times are simulated.
32 devices in a mesh: dp: 8 (over z, x), blk: 4 (over y, core).
Axes of the slice: x: 2, y: 2, z: 4, core: 2. Of those that a mesh axis runs over, the one named last changes fastest.
Arguments:
- inputs: bfloat16 [8, 512, 768], P('dp', 'blk'), may hold values from -6 to 6
- doc_lengths: int32 [8, 8], P('dp'), may hold values from 1 to 505, as said below
- project_in: bfloat16 [768, 2304], P(('dp', 'blk')), may hold values from -0.3125 to 0.3125
- project_out: bfloat16 [768, 768], P(('dp', 'blk')), may hold values from -0.875 to 0.875
- gate_weight: bfloat16 [768, 3072], P(('dp', 'blk')), may hold values from -0.21875 to 0.21875
- up_weight: bfloat16 [768, 3072], P(('dp', 'blk')), may hold values from -0.21875 to 0.21875
- down_weight: bfloat16 [3072, 768], P(('dp', 'blk')), may hold values from -0.15625 to 0.15625
- first_gain: bfloat16 [768], P(('dp', 'blk')), may hold values from 0.099609375 to 1.8984375
- first_bias: bfloat16 [768], P(('dp', 'blk')), may hold values from -1.5 to 1.5
- second_gain: bfloat16 [768], P(('dp', 'blk')), may hold values from 0.099609375 to 1.8984375
- second_bias: bfloat16 [768], P(('dp', 'blk')), may hold values from -1.5 to 1.5
- cotangent: bfloat16 [8, 512, 768], P('dp', 'blk'), may hold values from -6 to 6
Outputs:
- outputs: bfloat16 [8, 512, 768], P('dp', 'blk')
- input_grad: bfloat16 [8, 512, 768], P('dp', 'blk')
- project_in_grad: float32 [768, 2304], P(('dp', 'blk'))
- project_out_grad: float32 [768, 768], P(('dp', 'blk'))
- gate_grad: float32 [768, 3072], P(('dp', 'blk'))
- up_grad: float32 [768, 3072], P(('dp', 'blk'))
- down_grad: float32 [3072, 768], P(('dp', 'blk'))
- first_gain_grad: float32 [768], P(('dp', 'blk'))
- first_bias_grad: float32 [768], P(('dp', 'blk'))
- second_gain_grad: float32 [768], P(('dp', 'blk'))
- second_bias_grad: float32 [768], P(('dp', 'blk'))
Inputs may be any that keep to these rules, and one draw needn't show every extreme that they name: `doc_lengths`: each row's entries sum to 512; entries 0 to 6 are document lengths in order and entry 7 counts padding at the row's end, 1 or more; document 1 starts within the row's first 128 positions and ends within its last 128; in some row every entry but document 1 is 1.
All inputs are finite; a program needn't handle non-finite values.
Results may differ from a plain program's by a relative error of at most 0.024.
Values may be sent and summed in bfloat16 or wider, within the bound.
A program may use at most 128 MiB of HBM per device.

v0:
```python
import jax
import jax.numpy as jnp
from jax import lax
from jax.sharding import PartitionSpec as P

HEADS = 12


NEG = -1e30
EPS = 1e-05
BASE = 1000.0


def doc_layout(lengths_row, positions):
    bounds = jnp.cumsum(lengths_row)
    passed = positions[:, None] >= bounds[None, :]
    segment = jnp.sum(passed.astype(jnp.int32), axis=1)
    begins = jnp.sum(jnp.where(passed, lengths_row[None, :], 0), axis=1)
    return (segment, positions - begins)


def rotary(vectors, offsets):
    half_size = vectors.shape[-1] // 2
    frequency = BASE ** (-2.0 * jnp.arange(half_size, dtype=jnp.float32) / vectors.shape[-1])
    angles = offsets.astype(jnp.float32)[:, None] * frequency[None, :]
    cosine = jnp.concatenate([jnp.cos(angles), jnp.cos(angles)], axis=1)[:, None, :]
    sine_rows = jnp.concatenate([jnp.sin(angles), jnp.sin(angles)], axis=1)[:, None, :]
    first_half = vectors[..., :half_size]
    second_half = vectors[..., half_size:]
    turned = jnp.concatenate([-second_half, first_half], axis=-1)
    return vectors * cosine + turned * sine_rows


def layer_norm(residual, gain_row, bias_row):
    row_mean = jnp.mean(residual, axis=-1, keepdims=True)
    centered = residual - row_mean
    variance = jnp.mean(centered * centered, axis=-1, keepdims=True)
    return centered * lax.rsqrt(variance + EPS) * gain_row + bias_row


def contract_rows(left, right):
    return lax.dot_general(
        left, right, (((0,), (0,)), ((), ())), preferred_element_type=jnp.float32
    )


def contract_cols(left, right):
    return lax.dot_general(
        left, right, (((1,), (1,)), ((), ())), preferred_element_type=jnp.float32
    )


def tile_scores(query_tile, key_tile, seg_query, seg_key, score_scale):
    scores = (
        jnp.einsum("qhd,khd->hqk", query_tile, key_tile, preferred_element_type=jnp.float32)
        * score_scale
    )
    allowed = (seg_query[:, None] == seg_key[None, :])[None, :, :]
    return (jnp.where(allowed, scores, NEG), allowed)


def run_groups(pieces, group, lengths_row, seg_query, carried, tile_fn, extra_shape):
    group_count = pieces[0].shape[0] // group

    def group_step(carried_in, number):
        offset = number * group
        tile_set = tuple(
            (lax.dynamic_slice_in_dim(piece_rows, offset, group, 0) for piece_rows in pieces)
        )
        positions = offset + jnp.arange(group, dtype=jnp.int32)
        seg_key, unused_offsets = doc_layout(lengths_row, positions)
        touches = (seg_key[0] <= seg_query[-1]) & (seg_query[0] <= seg_key[-1])

        def active(state_in):
            return tile_fn(state_in, tile_set, seg_key)

        def skipped(state_in):
            return (state_in, jnp.zeros(extra_shape, jnp.float32))

        return lax.cond(touches, active, skipped, carried_in)

    return lax.scan(group_step, carried, jnp.arange(group_count, dtype=jnp.int32))


def shards(
    inputs,
    doc_lengths,
    project_in,
    project_out,
    gate_weight,
    up_weight,
    down_weight,
    first_gain,
    first_bias,
    second_gain,
    second_bias,
    cotangent,
):
    group = inputs.shape[1]
    width = inputs.shape[2]
    head_count = HEADS
    head_size = width // head_count
    score_scale = head_size ** (-0.5)
    cycle_rank = lax.axis_index("blk")
    positions = cycle_rank * group + jnp.arange(group, dtype=jnp.int32)
    lengths_row = doc_lengths[0]
    seg_query, offsets = doc_layout(lengths_row, positions)
    keep_mask = seg_query < lengths_row.shape[0] - 1
    keep_float = keep_mask.astype(jnp.float32)
    fetched = (
        lax.all_gather(project_in, ("dp", "blk"), axis=0, tiled=True),
        lax.all_gather(project_out, ("dp", "blk"), axis=0, tiled=True),
        lax.all_gather(gate_weight, ("dp", "blk"), axis=0, tiled=True),
        lax.all_gather(up_weight, ("dp", "blk"), axis=0, tiled=True),
        lax.all_gather(down_weight, ("dp", "blk"), axis=0, tiled=True),
        lax.all_gather(first_gain, ("dp", "blk"), axis=0, tiled=True),
        lax.all_gather(first_bias, ("dp", "blk"), axis=0, tiled=True),
        lax.all_gather(second_gain, ("dp", "blk"), axis=0, tiled=True),
        lax.all_gather(second_bias, ("dp", "blk"), axis=0, tiled=True),
    )
    full_in, full_out, full_gate, full_up, full_down = (
        fetched[0],
        fetched[1],
        fetched[2],
        fetched[3],
        fetched[4],
    )
    gain_one = fetched[5].astype(jnp.float32)
    bias_one = fetched[6].astype(jnp.float32)
    gain_two = fetched[7].astype(jnp.float32)
    bias_two = fetched[8].astype(jnp.float32)
    tokens_low = inputs[0]
    tokens_f = tokens_low.astype(jnp.float32)
    joined = jnp.dot(tokens_low, full_in, preferred_element_type=jnp.float32)
    query_raw = joined[:, :width].reshape(group, head_count, head_size)
    key_raw = joined[:, width : 2 * width].reshape(group, head_count, head_size)
    value_low = joined[:, 2 * width :].astype(jnp.bfloat16)
    query_rot, query_pull = jax.vjp(lambda vectors: rotary(vectors, offsets), query_raw)
    key_rot, key_pull = jax.vjp(lambda vectors: rotary(vectors, offsets), key_raw)
    query_low = query_rot.astype(jnp.bfloat16)
    key_low = key_rot.reshape(group, width).astype(jnp.bfloat16)

    def stats_tile(carried, tile_set, seg_key):
        row_top, row_total = carried
        key_tile = tile_set[0].reshape(group, head_count, head_size)
        scores, allowed = tile_scores(query_low, key_tile, seg_query, seg_key, score_scale)
        new_top = jnp.maximum(row_top, jnp.max(scores, axis=2))
        shrink = jnp.exp(row_top - new_top)
        added = jnp.sum(jnp.where(allowed, jnp.exp(scores - new_top[:, :, None]), 0.0), axis=2)
        return ((new_top, row_total * shrink + added), jnp.zeros((1,), jnp.float32))

    init_stats = (
        jnp.full((head_count, group), NEG, jnp.float32),
        jnp.zeros((head_count, group), jnp.float32),
    )
    carried = init_stats
    carried, unused = run_groups(
        (lax.all_gather(key_low, "blk", axis=0, tiled=True),),
        group,
        lengths_row,
        seg_query,
        carried,
        stats_tile,
        (1,),
    )
    row_top, row_total = carried
    log_total = row_top + jnp.log(row_total)

    def output_tile(accum, tile_set, seg_key):
        key_tile = tile_set[0].reshape(group, head_count, head_size)
        value_tile = tile_set[1].reshape(group, head_count, head_size)
        scores, allowed = tile_scores(query_low, key_tile, seg_query, seg_key, score_scale)
        prob_low = jnp.where(allowed, jnp.exp(scores - log_total[:, :, None]), 0.0).astype(
            jnp.bfloat16
        )
        accum = accum + jnp.einsum(
            "hqk,khd->qhd", prob_low, value_tile, preferred_element_type=jnp.float32
        )
        return (accum, jnp.zeros((1,), jnp.float32))

    zero_accum = jnp.zeros((group, head_count, head_size), jnp.float32)
    accum = zero_accum
    accum, unused = run_groups(
        (
            lax.all_gather(key_low, "blk", axis=0, tiled=True),
            lax.all_gather(value_low, "blk", axis=0, tiled=True),
        ),
        group,
        lengths_row,
        seg_query,
        accum,
        output_tile,
        (1,),
    )
    attend_low = (accum * keep_float[:, None, None]).reshape(group, width).astype(jnp.bfloat16)
    branch = jnp.dot(attend_low, full_out, preferred_element_type=jnp.float32)
    residual_one = tokens_f + branch
    hidden, norm_one_pull = jax.vjp(layer_norm, residual_one, gain_one, bias_one)
    hidden_low = hidden.astype(jnp.bfloat16)
    gate_pre = jnp.dot(hidden_low, full_gate, preferred_element_type=jnp.float32)
    up_pre = jnp.dot(hidden_low, full_up, preferred_element_type=jnp.float32)
    activated, swiglu_pull = jax.vjp(
        lambda gate_in, up_in: jax.nn.silu(gate_in) * up_in, gate_pre, up_pre
    )
    active_low = activated.astype(jnp.bfloat16)
    mlp_out = jnp.dot(active_low, full_down, preferred_element_type=jnp.float32)
    outputs_f, norm_two_pull = jax.vjp(layer_norm, hidden + mlp_out, gain_two, bias_two)
    refetched = (
        lax.all_gather(project_in, ("dp", "blk"), axis=0, tiled=True),
        lax.all_gather(project_out, ("dp", "blk"), axis=0, tiled=True),
        lax.all_gather(gate_weight, ("dp", "blk"), axis=0, tiled=True),
        lax.all_gather(up_weight, ("dp", "blk"), axis=0, tiled=True),
        lax.all_gather(down_weight, ("dp", "blk"), axis=0, tiled=True),
    )
    full_in, full_out, full_gate, full_up, full_down = (
        refetched[0],
        refetched[1],
        refetched[2],
        refetched[3],
        refetched[4],
    )
    d_res_two, second_gain_part, second_bias_part = norm_two_pull(cotangent[0].astype(jnp.float32))
    d_mlp_low = d_res_two.astype(jnp.bfloat16)
    down_part = contract_rows(active_low, d_mlp_low)
    d_active = contract_cols(d_mlp_low, full_down)
    d_gate, d_up = swiglu_pull(d_active)
    d_gate_low = d_gate.astype(jnp.bfloat16)
    d_up_low = d_up.astype(jnp.bfloat16)
    gate_part = contract_rows(hidden_low, d_gate_low)
    up_part = contract_rows(hidden_low, d_up_low)
    d_hidden = d_res_two + contract_cols(d_gate_low, full_gate) + contract_cols(d_up_low, full_up)
    d_res_one, first_gain_part, first_bias_part = norm_one_pull(d_hidden)
    d_branch_low = d_res_one.astype(jnp.bfloat16)
    out_part = contract_rows(attend_low, d_branch_low)
    d_attend = contract_cols(d_branch_low, full_out).astype(jnp.bfloat16)
    d_attend_low = (d_attend * keep_mask[:, None].astype(jnp.bfloat16)).reshape(
        group, head_count, head_size
    )
    delta = jnp.einsum("qhd,qhd->hq", d_attend_low.astype(jnp.float32), accum)

    def back_tile(grad_query, tile_set, seg_key):
        key_tile = tile_set[0].reshape(group, head_count, head_size)
        value_tile = tile_set[1].reshape(group, head_count, head_size)
        scores, allowed = tile_scores(query_low, key_tile, seg_query, seg_key, score_scale)
        prob_rows = jnp.where(allowed, jnp.exp(scores - log_total[:, :, None]), 0.0)
        d_probs = jnp.einsum(
            "qhd,khd->hqk", d_attend_low, value_tile, preferred_element_type=jnp.float32
        )
        d_score_low = (prob_rows * (d_probs - delta[:, :, None])).astype(jnp.bfloat16)
        grad_query = (
            grad_query
            + jnp.einsum("hqk,khd->qhd", d_score_low, key_tile, preferred_element_type=jnp.float32)
            * score_scale
        )
        grad_key = (
            jnp.einsum("hqk,qhd->khd", d_score_low, query_low, preferred_element_type=jnp.float32)
            * score_scale
        )
        grad_value = jnp.einsum(
            "hqk,qhd->khd",
            prob_rows.astype(jnp.bfloat16),
            d_attend_low,
            preferred_element_type=jnp.float32,
        )
        return (
            grad_query,
            jnp.concatenate(
                [grad_key.reshape(group, width), grad_value.reshape(group, width)], axis=1
            ),
        )

    grad_query = zero_accum
    grad_query, blocks = run_groups(
        (
            lax.all_gather(key_low, "blk", axis=0, tiled=True),
            lax.all_gather(value_low, "blk", axis=0, tiled=True),
        ),
        group,
        lengths_row,
        seg_query,
        grad_query,
        back_tile,
        (group, 2 * width),
    )
    blocks = blocks.reshape(-1, 2 * width)
    back_result = (grad_query, blocks)
    grad_query = back_result[0]
    owned_pairs = lax.psum_scatter(
        back_result[1].astype(jnp.bfloat16), "blk", scatter_dimension=0, tiled=True
    ).astype(jnp.float32)
    key_sum = owned_pairs[:, :width]
    value_sum = owned_pairs[:, width:]
    d_query_pre = query_pull(grad_query.astype(jnp.bfloat16).astype(jnp.float32))[0]
    d_key_low = key_sum.astype(jnp.bfloat16).astype(jnp.float32)
    d_key_pre = key_pull(d_key_low.reshape(group, head_count, head_size))[0]
    d_value_low = value_sum.astype(jnp.bfloat16).astype(jnp.float32)
    d_joined_low = jnp.concatenate(
        [d_query_pre.reshape(group, width), d_key_pre.reshape(group, width), d_value_low], axis=1
    ).astype(jnp.bfloat16)
    in_part = contract_rows(tokens_low, d_joined_low)
    input_grad = (d_res_one + contract_cols(d_joined_low, full_in)).astype(jnp.bfloat16)
    by_rows = (
        lax.psum_scatter(
            in_part.astype(jnp.bfloat16), "dp", scatter_dimension=0, tiled=True
        ).astype(jnp.float32),
        lax.psum_scatter(
            out_part.astype(jnp.bfloat16), "dp", scatter_dimension=0, tiled=True
        ).astype(jnp.float32),
        lax.psum_scatter(
            gate_part.astype(jnp.bfloat16), "dp", scatter_dimension=0, tiled=True
        ).astype(jnp.float32),
        lax.psum_scatter(
            up_part.astype(jnp.bfloat16), "dp", scatter_dimension=0, tiled=True
        ).astype(jnp.float32),
        lax.psum_scatter(
            down_part.astype(jnp.bfloat16), "dp", scatter_dimension=0, tiled=True
        ).astype(jnp.float32),
        lax.psum_scatter(
            first_gain_part.astype(jnp.bfloat16), "dp", scatter_dimension=0, tiled=True
        ).astype(jnp.float32),
        lax.psum_scatter(
            first_bias_part.astype(jnp.bfloat16), "dp", scatter_dimension=0, tiled=True
        ).astype(jnp.float32),
        lax.psum_scatter(
            second_gain_part.astype(jnp.bfloat16), "dp", scatter_dimension=0, tiled=True
        ).astype(jnp.float32),
        lax.psum_scatter(
            second_bias_part.astype(jnp.bfloat16), "dp", scatter_dimension=0, tiled=True
        ).astype(jnp.float32),
    )
    summed = (
        lax.psum_scatter(
            by_rows[0].astype(jnp.bfloat16), "blk", scatter_dimension=0, tiled=True
        ).astype(jnp.float32),
        lax.psum_scatter(
            by_rows[1].astype(jnp.bfloat16), "blk", scatter_dimension=0, tiled=True
        ).astype(jnp.float32),
        lax.psum_scatter(
            by_rows[2].astype(jnp.bfloat16), "blk", scatter_dimension=0, tiled=True
        ).astype(jnp.float32),
        lax.psum_scatter(
            by_rows[3].astype(jnp.bfloat16), "blk", scatter_dimension=0, tiled=True
        ).astype(jnp.float32),
        lax.psum_scatter(
            by_rows[4].astype(jnp.bfloat16), "blk", scatter_dimension=0, tiled=True
        ).astype(jnp.float32),
        lax.psum_scatter(
            by_rows[5].astype(jnp.bfloat16), "blk", scatter_dimension=0, tiled=True
        ).astype(jnp.float32),
        lax.psum_scatter(
            by_rows[6].astype(jnp.bfloat16), "blk", scatter_dimension=0, tiled=True
        ).astype(jnp.float32),
        lax.psum_scatter(
            by_rows[7].astype(jnp.bfloat16), "blk", scatter_dimension=0, tiled=True
        ).astype(jnp.float32),
        lax.psum_scatter(
            by_rows[8].astype(jnp.bfloat16), "blk", scatter_dimension=0, tiled=True
        ).astype(jnp.float32),
    )
    return (
        outputs_f.astype(jnp.bfloat16)[None],
        input_grad[None],
        summed[0],
        summed[1],
        summed[2],
        summed[3],
        summed[4],
        summed[5],
        summed[6],
        summed[7],
        summed[8],
    )


def solution(mesh):
    placed = (
        P("dp", "blk", None),
        P("dp", None),
        P(("dp", "blk"), None),
        P(("dp", "blk"), None),
        P(("dp", "blk"), None),
        P(("dp", "blk"), None),
        P(("dp", "blk"), None),
        P(("dp", "blk")),
        P(("dp", "blk")),
        P(("dp", "blk")),
        P(("dp", "blk")),
        P("dp", "blk", None),
    )
    return jax.shard_map(
        shards,
        mesh=mesh,
        in_specs=placed,
        out_specs=(
            P("dp", "blk", None),
            P("dp", "blk", None),
            P(("dp", "blk"), None),
            P(("dp", "blk"), None),
            P(("dp", "blk"), None),
            P(("dp", "blk"), None),
            P(("dp", "blk"), None),
            P(("dp", "blk")),
            P(("dp", "blk")),
            P(("dp", "blk")),
            P(("dp", "blk")),
        ),
        check_vma=False,
    )
```

profile of v0, /device:TPU:0, one launch (start us, length us, event | category | flops | bytes accessed | tf_op | source)
XLA Modules:
  0.0 977.8 jit_solution(17894344299859333463)
XLA Ops:
  15.0 42.3 %all-reduce.16 = (bf16[768]{0:T(1024)(128)(2,1)S(1)}, bf16[768]{0:T(1024)(128)(2,1)S(1)}, bf16[768]{0:T(1024)(128)(2,1)S(1)}, bf16[768]{0:T(1024)(128)(2,1)S(1)}) all-reduce(bf16[768]{0:T(1024)(128)(2,1)S(1)} %dynamic-update-slice.1, bf16[768]{0:T(1024)(128)(2,1)S(1)} %dynamic-update-slice, ...), channel_id=1, replica_groups=mesh['dp'=8,'blk'=4] {'dp','blk'}, use_global_device_ids=true, to_apply=%add.5 | all-reduce | flops 3072 | bytes 12288
  58.4 15.5 %all-gather.6.cloned.1.call-done = bf16[768,2304]{1,0:T(8,128)(2,1)} async-done(((bf16[24,2304]{1,0:T(8,128)(2,1)}), bf16[768,2304]{1,0:T(8,128)(2,1)}) %all-gather.6.cloned.1.call-update) | async-done | bytes 3538960 | tf_op jit(solution)/shard_map/all_gather | solution.py:111
  77.1 8.6 all_gather.42
  86.2 8.7 all_gather.43
  96.1 24.2 %while.46 = (s32[]{:T(128)}, f32[12,128]{1,0:T(8,128)S(1)}, f32[12,128]{1,0:T(8,128)S(1)}, s32[4]{0:T(128)S(1)}, s32[1,8]{1,0:T(1,128)}, /*index=5*/s32[128]{0:T...) while((s32[]{:T(128)}, f32[12,128]{1,0:T(8,128)S(1)}, ...), condition=%wide.region_10.11_spmd, body=%wide.region_4.10_spmd.sunk | while | flops 26368012 | bytes 2491241 | solution.py:82
  120.9 27.1 %while.47 = (s32[]{:T(128)}, f32[128,12,64]{0,2,1:T(8,128)S(1)}, s32[4]{0:T(128)S(1)}, s32[1,8]{1,0:T(1,128)}, s32[128]{0:T(128)S(1)}, /*index=5*/bf16[512,768]{...) while((s32[]{:T(128)}, f32[128,12,64]{0,2,1:T(8,128)S(1)}, ...), condition=%wide.region_15.16_spmd, body=%wide.region_11.15_spmd.sunk | while | flops 51432456 | bytes 2204505 | solution.py:82
  150.3 44.9 %all-gather.10.cloned.1.call-done = bf16[768,3072]{1,0:T(8,128)(2,1)} async-done(((bf16[24,3072]{1,0:T(8,128)(2,1)}), bf16[768,3072]{1,0:T(8,128)(2,1)}) %all-gather.10.cloned.1.call-update) | async-done | bytes 4718608 | tf_op jit(solution)/shard_map/all_gather | solution.py:113
  195.2 4.3 fusion.71
  199.5 60.9 %all-gather.12.cloned.1.call-done = bf16[768,3072]{1,0:T(8,128)(2,1)} async-done(((bf16[24,3072]{1,0:T(8,128)(2,1)}), bf16[768,3072]{1,0:T(8,128)(2,1)}) %all-gather.12.cloned.1.call-update) | async-done | bytes 4718608 | tf_op jit(solution)/shard_map/all_gather | solution.py:114
  260.4 5.0 multiply_convert_fusion.1
  265.4 60.1 %all-gather.14.cloned.1.call-done = bf16[3072,768]{1,0:T(8,128)(2,1)} async-done(((bf16[96,768]{1,0:T(8,128)(2,1)}), bf16[3072,768]{1,0:T(8,128)(2,1)}) %all-gather.14.cloned.1.call-update) | async-done | bytes 4718608 | tf_op jit(solution)/shard_map/all_gather | solution.py:115
  325.6 3.4 fusion.70
  339.7 35.3 %while.48 = (s32[]{:T(128)}, f32[128,12,64]{0,2,1:T(8,128)S(1)}, bf16[4,128,1536]{2,1,0:T(8,128)(2,1)}, s32[4]{0:T(128)S(1)}, s32[1,8]{1,0:T(1,128)}, /*index=5*...) while((s32[]{:T(128)}, f32[128,12,64]{0,2,1:T(8,128)S(1)}, ...), condition=%wide.region_28.29_spmd, body=%wide.region_24.28_spmd.sunk | while | flops 128601096 | bytes 9288589 | solution.py:82
  344.8 2.8 conditional.8
  353.6 2.8 conditional.8
  371.3 2.8 conditional.8
  377.9 3.6 convolution_convert_fusion.2
  382.7 3.6 convolution_convert_fusion.1
  387.5 3.7 convolution_convert_fusion
  391.3 10.9 %reduce-scatter.16.cloned.1.call-done = bf16[128,1536]{1,0:T(8,128)(2,1)} async-done(((bf16[512,1536]{1,0:T(8,128)(2,1)}), bf16[128,1536]{1,0:T(8,128)(2,1)}) %reduce-scatter.16.cloned.1.call-update) | async-done | bytes 393232 | tf_op jit(solution)/shard_map/reduce_scatter | solution.py:288
  409.0 4.0 copy.109
  413.1 57.0 %reduce-scatter.18.cloned.1.call-done = bf16[96,768]{1,0:T(8,128)(2,1)} async-done(((bf16[768,768]{1,0:T(8,128)(2,1)}), bf16[96,768]{1,0:T(8,128)(2,1)}) %reduce-scatter.18.cloned.1.call-update) | async-done | bytes 147472 | tf_op jit(solution)/shard_map/reduce_scatter | solution.py:306
  470.1 98.4 %reduce-scatter.22.cloned.1.call-done = bf16[96,3072]{1,0:T(8,128)(2,1)} async-done(((bf16[768,3072]{1,0:T(8,128)(2,1)}), bf16[96,3072]{1,0:T(8,128)(2,1)}) %reduce-scatter.22.cloned.1.call-update) | async-done | bytes 589840 | tf_op jit(solution)/shard_map/reduce_scatter | solution.py:309
  568.6 99.2 %reduce-scatter.26.cloned.1.call-done = bf16[96,3072]{1,0:T(8,128)(2,1)} async-done(((bf16[768,3072]{1,0:T(8,128)(2,1)}), bf16[96,3072]{1,0:T(8,128)(2,1)}) %reduce-scatter.26.cloned.1.call-update) | async-done | bytes 589840 | tf_op jit(solution)/shard_map/reduce_scatter | solution.py:312
  667.9 98.9 %reduce-scatter.30.cloned.1.call-done = bf16[384,768]{1,0:T(8,128)(2,1)} async-done(((bf16[3072,768]{1,0:T(8,128)(2,1)}), bf16[384,768]{1,0:T(8,128)(2,1)}) %reduce-scatter.30.cloned.1.call-update) | async-done | bytes 589840 | tf_op jit(solution)/shard_map/reduce_scatter | solution.py:315
  766.9 83.0 %reduce-scatter.34.cloned.1.call-done = bf16[96,2304]{1,0:T(8,128)(2,1)} async-done(((bf16[768,2304]{1,0:T(8,128)(2,1)}), bf16[96,2304]{1,0:T(8,128)(2,1)}) %reduce-scatter.34.cloned.1.call-update) | async-done | bytes 442384
  854.6 20.8 %all-reduce.17 = (bf16[768]{0:T(1024)(128)(2,1)}, bf16[768]{0:T(1024)(128)(2,1)}, bf16[768]{0:T(1024)(128)(2,1)}, bf16[768]{0:T(1024)(128)(2,1)}) all-reduce(bf16[768]{0:T(1024)(128)(2,1)S(1)} %copy-done.26, bf16[768]{0:T(1024)(128)(2,1)S(1)} %copy-done.27, ...), channel_id=13, replica_groups=mesh['dp'=8,'blk'=4] {'dp'}, use_global_device_ids=true, to_apply=%region_41.42.clone | all-reduce | flops 3072 | bytes 12288
  878.5 6.2 all-reduce.18
  891.0 3.2 fusion.35
  897.9 22.9 %reduce-scatter.28.cloned.1.call-done = bf16[24,3072]{1,0:T(8,128)(2,1)} async-done(((bf16[96,3072]{1,0:T(8,128)(2,1)}), bf16[24,3072]{1,0:T(8,128)(2,1)}) %reduce-scatter.28.cloned.1.call-update) | async-done | bytes 147472 | tf_op jit(solution)/shard_map/reduce_scatter | solution.py:341
  922.5 22.9 %reduce-scatter.32.cloned.1.call-done = bf16[96,768]{1,0:T(8,128)(2,1)} async-done(((bf16[384,768]{1,0:T(8,128)(2,1)}), bf16[96,768]{1,0:T(8,128)(2,1)}) %reduce-scatter.32.cloned.1.call-update) | async-done | bytes 147472 | tf_op jit(solution)/shard_map/reduce_scatter | solution.py:344
  947.1 22.0 %reduce-scatter.36.cloned.1.call-done = bf16[24,2304]{1,0:T(8,128)(2,1)} async-done(((bf16[96,2304]{1,0:T(8,128)(2,1)}), bf16[24,2304]{1,0:T(8,128)(2,1)}) %reduce-scatter.36.cloned.1.call-update) | async-done | bytes 110608
  (363 shorter events, 120.6 us)
Async XLA Ops:
  7.2 6.8 copy-start.36
  7.2 7.1 copy-start.37
  7.2 7.3 copy-start.38
  7.2 7.5 copy-start.39
  7.2 66.6 %copy-start.12 = (bf16[1,128,768]{2,1,0:T(8,128)(2,1)S(1)}, bf16[1,128,768]{2,1,0:T(8,128)(2,1)}, u32[]{:S(2)}) copy-start(bf16[1,128,768]{2,1,0:T(8,128)(2,1)} %param.24) | copy-start | bytes 589828
  7.2 66.6 %all-gather.6.cloned.1.call-start = ((), (), s32[]{:S(2)}) async-start(), calls=%async_computation.11 | async-start | bytes 3649536 | tf_op jit(solution)/shard_map/all_gather | solution.py:111
  8.0 140.2 %all-gather.8.cloned.1.call-start = ((), (), s32[]{:S(2)}) async-start(), calls=%async_computation.12 | async-start | bytes 1216512 | tf_op jit(solution)/shard_map/all_gather | solution.py:112
  8.7 186.5 %all-gather.10.cloned.1.call-start = ((), (), s32[]{:S(2)}) async-start(), calls=%async_computation.13 | async-start | bytes 4866048 | tf_op jit(solution)/shard_map/all_gather | solution.py:113
  9.4 250.9 %all-gather.12.cloned.1.call-start = ((), (), s32[]{:S(2)}) async-start(), calls=%async_computation.14 | async-start | bytes 4866048 | tf_op jit(solution)/shard_map/all_gather | solution.py:114
  10.0 315.6 %all-gather.14.cloned.1.call-start = ((), (), s32[]{:S(2)}) async-start(), calls=%async_computation.15 | async-start | bytes 4866048 | tf_op jit(solution)/shard_map/all_gather | solution.py:115
  10.6 391.6 %reduce-scatter.16.cloned.1.call-start = ((), (), s32[]{:S(2)}) async-start(), calls=%async_computation.16 | async-start | bytes 1966080 | tf_op jit(solution)/shard_map/reduce_scatter | solution.py:288
  13.8 62.7 %copy-start.17 = (f32[128,64]{0,1:T(8,128)}, f32[128,64]{0,1:T(8,128)S(1)}, u32[]{:S(2)}) copy-start(f32[128,64]{0,1:T(8,128)S(1)} %get-tuple-element.927) | copy-start | bytes 98308
  13.8 63.0 %copy-start.19 = (f32[128,64]{0,1:T(8,128)}, f32[128,64]{0,1:T(8,128)S(1)}, u32[]{:S(2)}) copy-start(f32[128,64]{0,1:T(8,128)S(1)} %get-tuple-element.928) | copy-start | bytes 98308
  120.9 27.2 %copy-start.35 = (f32[128]{0:T(128)S(1)}, f32[128]{0:T(128)}, u32[]{:S(2)}) copy-start(f32[128]{0:T(128)} %get-tuple-element.919) | copy-start | bytes 1540
  150.0 49.5 %copy-start.22 = (f32[128]{0:T(128)}, f32[128]{0:T(128)S(1)}, u32[]{:S(2)}) copy-start(f32[128]{0:T(128)S(1)} %broadcast_multiply_fusion.2) | copy-start | bytes 1540
  150.2 49.3 %copy-start.33 = (f32[128]{0:T(128)}, f32[128]{0:T(128)S(1)}, u32[]{:S(2)}) copy-start(f32[128]{0:T(128)S(1)} %multiply_reduce_fusion.3) | copy-start | bytes 1540
  150.2 49.3 %copy-start.24 = (f32[128]{0:T(128)}, f32[128]{0:T(128)S(1)}, u32[]{:S(2)}) copy-start(f32[128]{0:T(128)S(1)} %fusion.54) | copy-start | bytes 1540
  265.4 63.5 %copy-start = (bf16[128,3072]{1,0:T(8,128)(2,1)}, bf16[128,3072]{1,0:T(8,128)(2,1)S(1)}, u32[]{:S(2)}) copy-start(bf16[128,3072]{1,0:T(8,128)(2,1)S(1)} %get-tuple-element.922) | copy-start | bytes 2359300
  375.1 95.0 %reduce-scatter.18.cloned.1.call-start = ((), (), s32[]{:S(2)}) async-start(), calls=%async_computation.17 | async-start | bytes 1327104 | tf_op jit(solution)/shard_map/reduce_scatter | solution.py:306
  377.7 190.9 %reduce-scatter.22.cloned.1.call-start = ((), (), s32[]{:S(2)}) async-start(), calls=%async_computation.19 | async-start | bytes 5308416 | tf_op jit(solution)/shard_map/reduce_scatter | solution.py:309
  381.5 286.3 %reduce-scatter.26.cloned.1.call-start = ((), (), s32[]{:S(2)}) async-start(), calls=%async_computation.21 | async-start | bytes 5308416 | tf_op jit(solution)/shard_map/reduce_scatter | solution.py:312
  386.3 380.5 %reduce-scatter.30.cloned.1.call-start = ((), (), s32[]{:S(2)}) async-start(), calls=%async_computation.23 | async-start | bytes 5308416 | tf_op jit(solution)/shard_map/reduce_scatter | solution.py:315
  391.3 12.8 %copy-start.20 = (f32[128,64]{0,1:T(8,128)S(1)}, f32[128,64]{0,1:T(8,128)}, u32[]{:S(2)}) copy-start(f32[128,64]{0,1:T(8,128)} %copy-done.19) | copy-start | bytes 98308
  391.3 458.6 %reduce-scatter.34.cloned.1.call-start = ((), (), s32[]{:S(2)}) async-start(), calls=%async_computation.25 | async-start | bytes 3981312
  413.0 478.0 %copy-start.5 = (bf16[768,2304]{1,0:T(8,128)(2,1)S(1)}, bf16[768,2304]{1,0:T(8,128)(2,1)}, u32[]{:S(2)}) copy-start(bf16[768,2304]{1,0:T(8,128)(2,1)} %all-gather.6.cloned.1.call-done) | copy-start | bytes 10616836
  413.0 441.6 %copy-start.26 = (bf16[768]{0:T(1024)(128)(2,1)S(1)}, bf16[768]{0:T(1024)(128)(2,1)}, u32[]{:S(2)}) copy-start(bf16[768]{0:T(1024)(128)(2,1)} %get-tuple-element.792) | copy-start | bytes 4612
  413.0 441.6 %copy-start.27 = (bf16[768]{0:T(1024)(128)(2,1)S(1)}, bf16[768]{0:T(1024)(128)(2,1)}, u32[]{:S(2)}) copy-start(bf16[768]{0:T(1024)(128)(2,1)} %get-tuple-element.796) | copy-start | bytes 4612
  413.0 476.6 %reduce-scatter.20.cloned.1.call-start = ((), (), s32[]{:S(2)}) async-start(), calls=%async_computation.18 | async-start | bytes 184320 | tf_op jit(solution)/shard_map/reduce_scatter | solution.py:335
  470.1 426.2 %reduce-scatter.24.cloned.1.call-start = ((), (), s32[]{:S(2)}) async-start(), calls=%async_computation.20 | async-start | bytes 737280 | tf_op jit(solution)/shard_map/reduce_scatter | solution.py:338
  568.6 352.3 %reduce-scatter.28.cloned.1.call-start = ((), (), s32[]{:S(2)}) async-start(), calls=%async_computation.22 | async-start | bytes 737280 | tf_op jit(solution)/shard_map/reduce_scatter | solution.py:341
  667.9 277.6 %reduce-scatter.32.cloned.1.call-start = ((), (), s32[]{:S(2)}) async-start(), calls=%async_computation.24 | async-start | bytes 737280 | tf_op jit(solution)/shard_map/reduce_scatter | solution.py:344
  766.8 202.3 %reduce-scatter.36.cloned.1.call-start = ((), (), s32[]{:S(2)}) async-start(), calls=%async_computation.26 | async-start | bytes 552960
  (31 other events, 75.6 us)
Sparse Core Ops, SparseCore 0:
  11.0 62.8 all-gather.5
  76.8 52.9 all-gather.7
  132.6 62.5 all-gather.9
  198.0 62.3 all-gather.11
  263.2 62.3 all-gather.13
  375.2 26.9 reduce-scatter.15
  406.0 64.0 reduce-scatter.17
  474.2 94.3 reduce-scatter.21
  572.6 95.1 reduce-scatter.25
  671.8 94.9 reduce-scatter.29
  770.9 78.9 reduce-scatter.33
  852.3 19.2 reduce-scatter.19
  874.2 22.1 reduce-scatter.23
  898.8 22.0 reduce-scatter.27
  923.4 22.0 reduce-scatter.31
  948.0 21.0 reduce-scatter.35
where the time goes:
time: 980 us; the launch traced here: 978 us
  waiting for transfers between devices  702 us (72%)
  blocking collectives  86.6 us (9%)
  matrix products  57.5 us (6%)
  local copies, waits for them, and re-layouts  42.7 us (4%)
  loops' own time  39.2 us (4%)
  other arithmetic  32.8 us (3%)
  between operations  16.1 us (2%)
    unnamed x18, waiting for transfers between devices  108 us
    reduce_scatter x1, waiting for transfers between devices, shards(): lax.psum_scatter(up_part.astype(jnp.bfloat16), 'dp', scatter_dimension=0,...  99.2 us
    reduce_scatter x1, waiting for transfers between devices, shards(): lax.psum_scatter(down_part.astype(jnp.bfloat16), 'dp', scatter_dimension=...  98.9 us
    reduce_scatter x1, waiting for transfers between devices, shards(): lax.psum_scatter(gate_part.astype(jnp.bfloat16), 'dp', scatter_dimension=...  98.4 us
    unnamed x3, blocking collectives  69.2 us
    all_gather x1, waiting for transfers between devices, shards(): lax.all_gather(up_weight, ('dp', 'blk'), axis=0, tiled=True)  60.9 us
    all_gather x1, waiting for transfers between devices, shards(): lax.all_gather(down_weight, ('dp', 'blk'), axis=0, tiled=True)  60.1 us
    reduce_scatter x1, waiting for transfers between devices, shards(): lax.psum_scatter(out_part.astype(jnp.bfloat16), 'dp', scatter_dimension=0...  57 us
  transfers between devices with their start and end apart: 16, of which 14 were waited for; matrix products, arithmetic and copies ran while one was open for 9% of the time, Pallas kernels for 0%

commit v1 on v0

--- a/solution.py
+++ b/solution.py
@@ -1,6 +1,11 @@
+import functools
+
 import jax
 import jax.numpy as jnp
+import numpy as np
 from jax import lax
+from jax.experimental import pallas as pl
+from jax.experimental.pallas import tpu as pltpu
 from jax.sharding import PartitionSpec as P
 
 HEADS = 12
@@ -372,6 +377,876 @@
     )
 
 
+MESH_IDS = pl.DeviceIdType.MESH
+LANES = 128
+HALF = 64
+QUART = 32
+
+
+def mm(left, right):
+    return lax.dot_general(
+        left, right, (((1,), (0,)), ((), ())), preferred_element_type=jnp.float32
+    )
+
+
+def mt(left, right):
+    return lax.dot_general(
+        left, right, (((1,), (1,)), ((), ())), preferred_element_type=jnp.float32
+    )
+
+
+def tm(left, right):
+    return lax.dot_general(
+        left, right, (((0,), (0,)), ((), ())), preferred_element_type=jnp.float32
+    )
+
+
+class Wire:
+    def __init__(self, send_sem, recv_sem):
+        self.send_sem, self.recv_sem = send_sem, recv_sem
+        self.count, self.sent = 0, []
+
+    def push(self, src, dst, peer):
+        slot = self.count
+        self.count += 1
+        copy = pltpu.make_async_remote_copy(
+            src_ref=src,
+            dst_ref=dst,
+            send_sem=self.send_sem.at[slot],
+            recv_sem=self.recv_sem.at[slot],
+            device_id=peer,
+            device_id_type=MESH_IDS,
+        )
+        copy.start()
+        self.sent.append(copy)
+        return slot
+
+    def arrive(self, slot, dst, peer):
+        pltpu.make_async_remote_copy(
+            src_ref=dst,
+            dst_ref=dst,
+            send_sem=self.send_sem.at[slot],
+            recv_sem=self.recv_sem.at[slot],
+            device_id=peer,
+            device_id_type=MESH_IDS,
+        ).wait_recv()
+
+    def finish(self):
+        for copy in self.sent:
+            copy.wait_send()
+
+
+def fused(
+    depth,
+    lens,
+    freq,
+    xin,
+    cot,
+    p_in,
+    p_mlp,
+    p_out,
+    p_down,
+    outputs,
+    input_grad,
+    g_in,
+    g_mlp,
+    g_out,
+    g_down,
+    xs,
+    r_in,
+    r_mlp,
+    s_out,
+    w_in,
+    w_gate,
+    w_up,
+    w_down,
+    w_out,
+    params,
+    cos_tab,
+    sin_tab,
+    seg_tab,
+    qm,
+    kw,
+    vw,
+    prob,
+    att,
+    s_att,
+    r_att,
+    norm_one,
+    hid,
+    hs,
+    gate_pre,
+    up_pre,
+    act,
+    s_mix,
+    r_mix,
+    dres_two,
+    dms,
+    dgate,
+    dup,
+    s_dh,
+    r_dh,
+    dres_one,
+    s_da,
+    r_da,
+    acc_q,
+    acc_k,
+    acc_v,
+    dj,
+    s_ig,
+    r_ig,
+    pr_in,
+    rx_in,
+    sz_in,
+    rz_in,
+    pr_gate,
+    rx_gate,
+    sz_gate,
+    rz_gate,
+    pr_up,
+    rx_up,
+    sz_up,
+    rz_up,
+    pr_down,
+    rx_down,
+    sz_down,
+    rz_down,
+    b_out,
+    rb_out,
+    pr_out,
+    rx_out,
+    sz_out,
+    rz_out,
+    f_gate,
+    s_gmlp,
+    r_gmlp,
+    s_gin,
+    r_gin,
+    send_sem,
+    recv_sem,
+):
+    planes, cols = depth, 4
+    tok = xin.shape[0]
+    row_len = tok * cols
+    dp = lax.axis_index("dp")
+    blk = lax.axis_index("blk")
+    z, x = dp // 2, dp % 2
+    bf16, f32 = jnp.bfloat16, jnp.float32
+
+    def side():
+        return (z * 2 + (1 - x), blk)
+
+    def tier(k):
+        return (((z + k) % planes) * 2 + x, blk)
+
+    def tier_from(k):
+        return (z + planes - k) % planes
+
+    def lane(k):
+        return (dp, (blk + k) % cols)
+
+    def lane_from(k):
+        return (blk + cols - k) % cols
+
+    tiers, lanes = range(1, planes), range(1, cols)
+    wire = Wire(send_sem, recv_sem)
+    barrier = pltpu.get_barrier_semaphore()
+    peers = [side()] + [tier(k) for k in tiers] + [lane(k) for k in lanes]
+    for peer in peers:
+        pl.semaphore_signal(barrier, inc=1, device_id=peer, device_id_type=MESH_IDS)
+    pl.semaphore_wait(barrier, len(peers))
+
+    def to_lanes(source_of, target):
+        return [wire.push(source_of((blk + k) % cols), target.at[blk], lane(k)) for k in lanes]
+
+    def from_lanes(slots, target):
+        for k, slot in zip(lanes, slots):
+            wire.arrive(slot, target.at[lane_from(k)], lane(k))
+
+    def spread_tiers(source, target):
+        return [wire.push(source, target.at[dp], tier(k)) for k in tiers]
+
+    def from_tier(slots, target, k):
+        wire.arrive(slots[k - 1], target.at[tier_from(k) * 2 + x], tier(k))
+
+    def spread_side(source, target, plane):
+        return wire.push(source, target.at[plane * 2 + x], side())
+
+    def from_side(slot, target, plane):
+        wire.arrive(slot, target.at[plane * 2 + (1 - x)], side())
+
+    own_out = s_out.at[blk]
+    in_slots = to_lanes(lambda to: p_in.at[to], r_in)
+    out_tiers = spread_tiers(p_out, own_out)
+    out_sides = [spread_side(p_out, own_out, z)]
+    x_slots = to_lanes(lambda to: xin, xs)
+    mlp_slots = to_lanes(lambda to: p_mlp.at[to], r_mlp)
+    xs[blk] = xin[...]
+    r_in[blk] = p_in[blk]
+    r_mlp[blk] = p_mlp[blk]
+    s_out[blk, dp] = p_out[...]
+    w_down[dp] = p_down[...]
+
+    lengths = [lens[0, j] for j in range(lens.shape[1])]
+
+    def layout(positions):
+        segment = jnp.zeros_like(positions)
+        begins = jnp.zeros_like(positions)
+        bound = jnp.int32(0)
+        for length in lengths:
+            bound = bound + length
+            passed = positions >= bound
+            segment = segment + jnp.where(passed, 1, 0)
+            begins = begins + jnp.where(passed, length, 0)
+        return segment, positions - begins
+
+    seg_rows, offsets = layout(lax.broadcasted_iota(jnp.int32, (row_len, LANES), 0))
+    seg_tab[...] = seg_rows
+    seg_key = layout(lax.broadcasted_iota(jnp.int32, (8, row_len), 1))[0][0:1]
+    lane_ids = lax.broadcasted_iota(jnp.int32, (1, LANES), 1)
+    low_half = lane_ids < HALF
+    front = lane_ids % HALF < QUART
+    angles = offsets.astype(f32) * freq[0:1]
+    cos_tab[...] = jnp.cos(angles)
+    sin_tab[...] = jnp.where(front, -1.0, 1.0) * jnp.sin(angles)
+
+    def turn(window):
+        return jnp.where(
+            front, pltpu.roll(window, LANES - QUART, 1), pltpu.roll(window, QUART, 1)
+        )
+
+    from_lanes(in_slots, r_in)
+    rows = 24
+    w_in[dp] = jnp.concatenate(
+        [r_in[j, 0:rows, :].astype(f32) for j in range(cols)], axis=0
+    ).astype(bf16)
+    in_tiers = spread_tiers(w_in.at[dp], w_in)
+    in_sides = [spread_side(w_in.at[dp], w_in, z)]
+    from_lanes(mlp_slots, r_mlp)
+    mlp_own = [r_mlp[j].astype(f32) for j in range(cols)]
+    w_gate[dp] = jnp.concatenate([part[0:rows] for part in mlp_own], axis=0).astype(bf16)
+    w_up[dp] = jnp.concatenate([part[rows:] for part in mlp_own], axis=0).astype(bf16)
+    gate_tiers = spread_tiers(w_gate.at[dp], w_gate)
+    up_tiers = spread_tiers(w_up.at[dp], w_up)
+    down_tiers = spread_tiers(p_down, w_down)
+
+    def relay(tier_slots, side_slots, target):
+        for k in tiers:
+            from_tier(tier_slots, target, k)
+            plane = tier_from(k)
+            side_slots.append(spread_side(target.at[plane * 2 + x], target, plane))
+
+    def settle(side_slots, target):
+        for k in range(planes):
+            from_side(side_slots[k], target, tier_from(k))
+
+    relay(out_tiers, out_sides, own_out)
+    relay(in_tiers, in_sides, w_in)
+    gate_sides = [spread_side(w_gate.at[dp], w_gate, z)]
+    settle(out_sides, own_out)
+    out_lanes = to_lanes(lambda to: own_out, s_out)
+    from_lanes(x_slots, xs)
+    settle(in_sides, w_in)
+
+    width = xin.shape[1]
+    group = 2
+    chunk = group * tok
+
+    def project(step, carry):
+        start = pl.multiple_of(step * chunk, chunk)
+        here = pl.ds(start, chunk)
+        tokens = xs[pl.ds(step * group, group)].reshape(chunk, width)
+        joined = mm(tokens, w_in[...].reshape(width, w_in.shape[2]))
+        cosine, sine = cos_tab[here, :], sin_tab[here, :]
+
+        def rotate(number):
+            window = joined[:, number * LANES : (number + 1) * LANES]
+            return window * cosine + turn(window) * sine
+
+        scale = HALF ** -0.5
+        queries = rotate(0).astype(bf16).astype(f32) * scale
+        qm[0, here, :] = jnp.where(low_half, queries, 0.0).astype(bf16)
+        qm[1, here, :] = jnp.where(low_half, 0.0, queries).astype(bf16)
+        kw[0, here, :] = rotate(1).astype(bf16)
+        vw[0, here, :] = joined[:, 2 * LANES : 3 * LANES].astype(bf16)
+        both = rotate(3)
+        qm[2, here, :] = jnp.where(low_half, both.astype(bf16).astype(f32) * scale, 0.0).astype(bf16)
+        kw[1, here, :] = jnp.where(low_half, pltpu.roll(both, HALF, 1), 0.0).astype(bf16)
+        vw[1, here, :] = joined[:, 4 * LANES : 5 * LANES].astype(bf16)
+        return carry
+
+    lax.fori_loop(0, cols // group, project, 0)
+
+    def attend(head):
+        window = head // 2
+
+        def step_fn(step, carry):
+            here = pl.ds(pl.multiple_of(step * chunk, chunk), chunk)
+            scores = mt(qm[head, here, :], kw[window])
+            allowed = seg_tab[here, :][:, 0:1] == seg_key
+            scores = jnp.where(allowed, scores, NEG)
+            top = jnp.max(scores, axis=1, keepdims=True)
+            raised = jnp.exp(scores - top)
+            total = jnp.sum(raised, axis=1, keepdims=True)
+            prob_low = (raised * (1.0 / total)).astype(bf16)
+            prob[head, here, :] = prob_low
+            mixed = mm(prob_low, vw[window])
+            if head == 1:
+                mixed = jnp.where(low_half, att[0, here, :], mixed)
+            att[window, here, :] = mixed
+            return carry
+
+        lax.fori_loop(0, row_len // chunk, step_fn, 0)
+
+    attend(0)
+    relay(gate_tiers, gate_sides, w_gate)
+    up_sides = [spread_side(w_up.at[dp], w_up, z)]
+    attend(1)
+    relay(up_tiers, up_sides, w_up)
+    down_sides = [spread_side(p_down, w_down, z)]
+    attend(2)
+
+    last_segment = lens.shape[1] - 1
+    for j in range(cols):
+        here = slice(j * tok, (j + 1) * tok)
+        kept = seg_tab[here, :] < last_segment
+        s_att[j, :, 0:LANES] = jnp.where(kept, att[0, here, :], 0.0).astype(bf16)
+        s_att[j, :, LANES : 2 * LANES] = jnp.where(kept, att[1, here, :], 0.0).astype(bf16)
+    att_slots = to_lanes(lambda to: s_att.at[to], r_att)
+    r_att[blk] = s_att[blk]
+
+    from_lanes(out_lanes, s_out)
+    shards = planes * 2 * cols
+    per_quarter = shards // cols
+    head_rows = per_quarter * rows
+    for quarter in range(cols):
+        w_out[quarter, 0:head_rows, :] = jnp.concatenate(
+            [
+                s_out[s % cols, s // cols, 0:rows, :].astype(f32)
+                for s in range(quarter * per_quarter, (quarter + 1) * per_quarter)
+            ],
+            axis=0,
+        ).astype(bf16)
+        w_out[quarter, head_rows:, :] = jnp.zeros(
+            (w_out.shape[1] - head_rows, width), bf16
+        )
+    column = lax.broadcasted_iota(jnp.int32, (LANES, width), 1).astype(f32)
+    owner = jnp.floor((column + 0.5) * (1.0 / rows))
+    inside = column - owner * rows
+    unit = (
+        inside == lax.broadcasted_iota(jnp.int32, (LANES, width), 0).astype(f32)
+    ).astype(bf16)
+    tails = jnp.concatenate(
+        [
+            s_out[s % cols, s // cols, rows : rows + 8, 0:LANES].astype(f32)
+            for s in range(shards)
+        ],
+        axis=0,
+    ).astype(bf16)
+    shard_ids = lax.broadcasted_iota(jnp.int32, (shards, 8, width), 0).astype(f32)
+    shard_hit = (shard_ids == owner[0:1].reshape(1, 1, width)).astype(f32)
+    params[...] = jnp.sum(mm(tails, unit).reshape(shards, 8, width) * shard_hit, axis=0)
+    gain_one, bias_one = params[0:1, :], params[1:2, :]
+    gain_two, bias_two = params[2:3, :], params[3:4, :]
+
+    def normalize(residual):
+        centered = residual - jnp.mean(residual, axis=1, keepdims=True)
+        variance = jnp.mean(centered * centered, axis=1, keepdims=True)
+        spread = lax.rsqrt(variance + EPS)
+        return centered * spread, spread
+
+    def normalize_back(grad, normal, spread, gain):
+        inner = grad * gain
+        mean_inner = jnp.mean(inner, axis=1, keepdims=True)
+        mean_both = jnp.mean(inner * normal, axis=1, keepdims=True)
+        return (inner - mean_inner - normal * mean_both) * spread
+
+    def column_sum(value):
+        return jnp.sum(value, axis=0, keepdims=True)
+
+    from_lanes(att_slots, r_att)
+    branch = mm(r_att[0], w_out[0])
+    for quarter in range(1, cols):
+        branch = branch + mm(r_att[quarter], w_out[quarter])
+    normal, spread_one = normalize(xin[...].astype(f32) + branch)
+    norm_one[...] = normal
+    hidden = normal * gain_one + bias_one
+    hid[...] = hidden
+    hs[blk] = hidden.astype(bf16)
+    hid_slots = to_lanes(lambda to: hs.at[blk], hs)
+    relay(down_tiers, down_sides, w_down)
+    settle(gate_sides, w_gate)
+    settle(up_sides, w_up)
+    from_lanes(hid_slots, hs)
+
+    units = w_gate.shape[2]
+    wide = 256
+    strips = units // wide
+
+    def expand(step, carry):
+        here = pl.ds(pl.multiple_of(step * wide, wide), wide)
+        tokens = hs[...].reshape(row_len, width)
+        gate = mm(tokens, w_gate[:, :, here].reshape(width, wide))
+        up = mm(tokens, w_up[:, :, here].reshape(width, wide))
+        gate_pre[:, here] = gate
+        up_pre[:, here] = up
+        act[:, here] = (gate / (1.0 + jnp.exp(-gate)) * up).astype(bf16)
+        return carry
+
+    lax.fori_loop(0, strips, expand, 0)
+    settle(down_sides, w_down)
+
+    def contract(step, carry):
+        here = pl.ds(pl.multiple_of(step * wide, wide), wide)
+        mixed = mm(act[...], w_down[:, :, here].reshape(units, wide))
+        s_mix[:, :, here] = mixed.reshape(cols, tok, wide).astype(bf16)
+        return carry
+
+    lax.fori_loop(0, width // wide, contract, 0)
+    mix_slots = to_lanes(lambda to: s_mix.at[to], r_mix)
+    r_mix[blk] = s_mix[blk]
+    from_lanes(mix_slots, r_mix)
+    mlp_out = r_mix[0].astype(f32)
+    for j in range(1, cols):
+        mlp_out = mlp_out + r_mix[j].astype(f32)
+    normal, spread_two = normalize(hid[...] + mlp_out)
+    outputs[...] = (normal * gain_two + bias_two).astype(bf16)
+    grad = cot[...].astype(f32)
+    second_gain = column_sum(grad * normal)
+    second_bias = column_sum(grad)
+    d_two = normalize_back(grad, normal, spread_two, gain_two)
+    dres_two[...] = d_two
+    dms[blk] = d_two.astype(bf16)
+    dm_slots = to_lanes(lambda to: dms.at[blk], dms)
+    from_lanes(dm_slots, dms)
+
+    def send_side(part, inbox):
+        order = [(z + k) % planes for k in list(tiers) + [0]]
+        return [wire.push(part.at[1 - x, to], inbox.at[to], side()) for to in order]
+
+    def pass_on(part, inbox, staged, landing, side_slots):
+        tier_slots = []
+        for k in tiers:
+            to = (z + k) % planes
+            wire.arrive(side_slots[k - 1], inbox.at[to], side())
+            staged[to] = (part[x, to].astype(f32) + inbox[to].astype(f32)).astype(bf16)
+            tier_slots.append(wire.push(staged.at[to], landing.at[k], tier(k)))
+        wire.arrive(side_slots[planes - 1], inbox.at[z], side())
+        return tier_slots
+
+    def total_of(part, inbox, landing, tier_slots):
+        total = part[x, z].astype(f32) + inbox[z].astype(f32)
+        for k in tiers:
+            wire.arrive(tier_slots[k - 1], landing.at[k], tier(k))
+            total = total + landing[k].astype(f32)
+        return total
+
+    half = 4
+
+    def fill_parts(part, left_of, right):
+        height = part.shape[2]
+
+        def step_fn(step, carry):
+            here = pl.ds(pl.multiple_of(step * half * height, LANES), half * height)
+            product = tm(left_of(here), right())
+            for j in range(half):
+                part[j % 2, step * (half // 2) + j // 2] = product[
+                    j * height : (j + 1) * height
+                ].astype(bf16)
+            return carry
+
+        lax.fori_loop(0, planes * 2 // half, step_fn, 0)
+
+    fill_parts(pr_down, lambda here: act[:, here], lambda: dms[...].reshape(row_len, width))
+    down_x = send_side(pr_down, rx_down)
+
+    block = w_down.shape[1]
+
+    def active_grads(step, carry):
+        here = pl.ds(pl.multiple_of(step * half * block, LANES), half * block)
+        d_active = mt(
+            dms[...].reshape(row_len, width),
+            w_down[pl.ds(step * half, half)].reshape(half * block, width),
+        )
+        gate, up = gate_pre[:, here], up_pre[:, here]
+        sg = 1.0 / (1.0 + jnp.exp(-gate))
+        dgate[:, here] = (d_active * up * sg * (1.0 + gate * (1.0 - sg))).astype(bf16)
+        dup[:, here] = (d_active * gate * sg).astype(bf16)
+        return carry
+
+    lax.fori_loop(0, planes * 2 // half, active_grads, 0)
+    block = w_gate.shape[1]
+
+    def hidden_grads(step, carry):
+        here = pl.ds(pl.multiple_of(step * half * block, LANES), half * block)
+        those = pl.ds(step * half, half)
+        mixed = mt(dgate[...], w_gate[those].reshape(half * block, units)) + mt(
+            dup[...], w_up[those].reshape(half * block, units)
+        )
+        s_dh[:, :, here] = mixed.reshape(cols, tok, half * block).astype(bf16)
+        return carry
+
+    lax.fori_loop(0, planes * 2 // half, hidden_grads, 0)
+    dh_slots = to_lanes(lambda to: s_dh.at[to], r_dh)
+    r_dh[blk] = s_dh[blk]
+
+    def hidden_rows(here):
+        return hs[:, :, here].reshape(row_len, half * block)
+
+    fill_parts(pr_gate, hidden_rows, lambda: dgate[...])
+    gate_x = send_side(pr_gate, rx_gate)
+    fill_parts(pr_up, hidden_rows, lambda: dup[...])
+    up_x = send_side(pr_up, rx_up)
+
+    from_lanes(dh_slots, r_dh)
+    d_hidden = dres_two[...]
+    for j in range(cols):
+        d_hidden = d_hidden + r_dh[j].astype(f32)
+    normal = norm_one[...]
+    first_gain = column_sum(d_hidden * normal)
+    first_bias = column_sum(d_hidden)
+    d_one = normalize_back(d_hidden, normal, spread_one, gain_one)
+    dres_one[...] = d_one
+    d_branch = d_one.astype(bf16)
+    mine = pl.ds(pl.multiple_of(blk * tok, tok), tok)
+    kept = seg_tab[mine, :][:, 0:1] < last_segment
+    for quarter in range(cols):
+        pulled = mt(d_branch, w_out[quarter]).astype(bf16).astype(f32)
+        s_da[quarter] = jnp.where(kept, pulled, 0.0).astype(bf16)
+    da_slots = to_lanes(lambda to: s_da.at[to], r_da)
+    r_da[blk] = s_da[blk]
+
+    vectors = jnp.concatenate(
+        [first_gain, first_bias, second_gain, second_bias, jnp.zeros((4, width), f32)], axis=0
+    )
+    tails = mt(
+        (shard_hit * vectors.reshape(1, 8, width)).reshape(shards * 8, width).astype(bf16), unit
+    )
+    for quarter in range(cols):
+        product = tm(r_att[quarter], d_branch)
+        for t in range(per_quarter):
+            s = quarter * per_quarter + t
+            owner_dp = s // cols
+            lower = jnp.concatenate(
+                [tails[s * 8 : s * 8 + 8], jnp.zeros((8, width - LANES), f32)], axis=1
+            )
+            b_out[s % cols, owner_dp % 2, owner_dp // 2] = jnp.concatenate(
+                [product[t * rows : (t + 1) * rows], lower], axis=0
+            ).astype(bf16)
+    out_blk = to_lanes(lambda to: b_out.at[to], rb_out)
+    rb_out[blk] = b_out[blk]
+
+    down_z = pass_on(pr_down, rx_down, sz_down, rz_down, down_x)
+    from_lanes(da_slots, r_da)
+
+    def attend_back(head):
+        window = head // 2
+        fresh = head != 1
+
+        def step_fn(step, carry):
+            here = pl.ds(pl.multiple_of(step * chunk, chunk), chunk)
+            d_out = r_da[pl.ds(step * group, group), :, window * LANES : (window + 1) * LANES]
+            d_out = d_out.reshape(chunk, LANES).astype(f32)
+            if head == 0:
+                d_out = jnp.where(low_half, d_out, 0.0)
+            if head == 1:
+                d_out = jnp.where(low_half, 0.0, d_out)
+            d_low = d_out.astype(bf16)
+            delta = jnp.sum(d_out * att[window, here, :], axis=1, keepdims=True)
+            prob_low = prob[head, here, :]
+            d_prob = mt(d_low, vw[window])
+            d_score = (prob_low.astype(f32) * (d_prob - delta)).astype(bf16)
+            d_query = mm(d_score, kw[window]) * (HALF ** -0.5)
+            if head == 1:
+                d_query = jnp.where(low_half, acc_q[0, here, :], d_query)
+            acc_q[window, here, :] = d_query
+            d_key = tm(d_score, qm[head, here, :])
+            d_value = tm(prob_low, d_low)
+            if fresh:
+
+                @pl.when(step == 0)
+                def _():
+                    acc_k[window] = d_key
+                    acc_v[window] = d_value
+
+                @pl.when(step != 0)
+                def _():
+                    acc_k[window] = acc_k[window] + d_key
+                    acc_v[window] = acc_v[window] + d_value
+            else:
+                acc_k[window] = acc_k[window] + d_key
+                acc_v[window] = acc_v[window] + d_value
+            return carry
+
+        lax.fori_loop(0, row_len // chunk, step_fn, 0)
+
+    attend_back(0)
+    attend_back(1)
+    attend_back(2)
+
+    cosine, sine = cos_tab[...], sin_tab[...]
+
+    def rotate_back(vector):
+        vector = vector.astype(bf16).astype(f32)
+        return (vector * cosine - turn(vector) * sine).astype(bf16)
+
+    dj[:, 0:LANES] = rotate_back(acc_q[0])
+    dj[:, LANES : 2 * LANES] = rotate_back(acc_k[0])
+    dj[:, 2 * LANES : 3 * LANES] = acc_v[0].astype(bf16)
+    dj[:, 3 * LANES : 4 * LANES] = rotate_back(acc_q[1] + pltpu.roll(acc_k[1], HALF, 1))
+    dj[:, 4 * LANES : 5 * LANES] = acc_v[1].astype(bf16)
+
+    from_lanes(out_blk, rb_out)
+    for side_at in range(2):
+        gathered = rb_out[0, side_at].astype(f32)
+        for j in range(1, cols):
+            gathered = gathered + rb_out[j, side_at].astype(f32)
+        pr_out[side_at] = gathered.astype(bf16)
+    out_x = send_side(pr_out, rx_out)
+
+    fill_parts(pr_in, lambda here: xs[:, :, here].reshape(row_len, half * block), lambda: dj[...])
+    in_x = send_side(pr_in, rx_in)
+
+    def input_grads(step, carry):
+        here = pl.ds(pl.multiple_of(step * half * block, LANES), half * block)
+        mixed = mt(dj[...], w_in[pl.ds(step * half, half)].reshape(half * block, w_in.shape[2]))
+        s_ig[:, :, here] = mixed.reshape(cols, tok, half * block).astype(bf16)
+        return carry
+
+    lax.fori_loop(0, planes * 2 // half, input_grads, 0)
+    ig_slots = to_lanes(lambda to: s_ig.at[to], r_ig)
+    r_ig[blk] = s_ig[blk]
+
+    gate_z = pass_on(pr_gate, rx_gate, sz_gate, rz_gate, gate_x)
+    g_down[...] = total_of(pr_down, rx_down, rz_down, down_z)
+    up_z = pass_on(pr_up, rx_up, sz_up, rz_up, up_x)
+    gate_total = total_of(pr_gate, rx_gate, rz_gate, gate_z)
+    f_gate[...] = gate_total
+    out_z = pass_on(pr_out, rx_out, sz_out, rz_out, out_x)
+    from_lanes(ig_slots, r_ig)
+    grad_in = dres_one[...]
+    for j in range(cols):
+        grad_in = grad_in + r_ig[j].astype(f32)
+    input_grad[...] = grad_in.astype(bf16)
+    up_total = total_of(pr_up, rx_up, rz_up, up_z)
+    gate_total = f_gate[...]
+    for j in range(cols):
+        here = slice(j * rows, (j + 1) * rows)
+        s_gmlp[j] = jnp.concatenate([gate_total[here], up_total[here]], axis=0).astype(bf16)
+    gmlp_slots = to_lanes(lambda to: s_gmlp.at[to], r_gmlp)
+    r_gmlp[blk] = s_gmlp[blk]
+    in_z = pass_on(pr_in, rx_in, sz_in, rz_in, in_x)
+    g_out[...] = total_of(pr_out, rx_out, rz_out, out_z)
+    from_lanes(gmlp_slots, r_gmlp)
+    g_mlp[...] = r_gmlp[...]
+    in_total = total_of(pr_in, rx_in, rz_in, in_z)
+    for j in range(cols):
+        s_gin[j] = jnp.concatenate(
+            [in_total[j * rows : (j + 1) * rows], jnp.zeros((8, in_total.shape[1]), f32)], axis=0
+        ).astype(bf16)
+    gin_slots = to_lanes(lambda to: s_gin.at[to], r_gin)
+    r_gin[blk] = s_gin[blk]
+    from_lanes(gin_slots, r_gin)
+    g_in[...] = r_gin[...]
+    wire.finish()
+
+
+def fast_shards(
+    depth,
+    inputs,
+    doc_lengths,
+    project_in,
+    project_out,
+    gate_weight,
+    up_weight,
+    down_weight,
+    first_gain,
+    first_bias,
+    second_gain,
+    second_bias,
+    cotangent,
+):
+    cols = 4
+    tok, width = inputs.shape[1:]
+    rows = project_in.shape[0]
+    ff = gate_weight.shape[1]
+    ring = depth * 2
+    row_len = tok * cols
+    units = ff // cols
+    block = units // ring
+    head_width = width // cols
+    in_width = 5 * LANES
+    bf16, f32 = jnp.bfloat16, jnp.float32
+
+    kinds = project_in.reshape(rows, 3, cols, head_width)
+    pairs, singles = kinds[..., :LANES], kinds[..., LANES:]
+    p_in = jnp.concatenate(
+        [pairs[:, 0], pairs[:, 1], pairs[:, 2], singles[:, 0], singles[:, 1], singles[:, 2]],
+        axis=-1,
+    ).transpose(1, 0, 2)
+    p_in = jnp.pad(p_in, ((0, 0), (0, 32 - rows), (0, in_width - p_in.shape[2])))
+
+    def by_owner(weight):
+        return weight.reshape(rows, ring, cols, block).transpose(2, 0, 1, 3).reshape(cols, rows, units)
+
+    p_mlp = jnp.concatenate([by_owner(gate_weight), by_owner(up_weight)], axis=1)
+    vectors = jnp.stack([first_gain, first_bias, second_gain, second_bias])
+    p_out = jnp.concatenate(
+        [project_out, jnp.pad(vectors, ((0, 4), (0, width - rows)))], axis=0
+    )
+    lane_ids = np.arange(LANES) % QUART
+    freq = jnp.asarray(
+        np.broadcast_to(BASE ** (-2.0 * lane_ids / HALF), (8, LANES)).astype(np.float32)
+    )
+
+    def scratch(*shape, kind=bf16):
+        return pltpu.VMEM(shape, kind)
+
+    def sums(height, across):
+        return [
+            scratch(2, depth, height, across),
+            scratch(depth, height, across),
+            scratch(depth, height, across),
+            scratch(depth, height, across),
+        ]
+
+    stacked = scratch(cols, tok, width)
+    heads = 3
+    buffers = [
+        stacked,
+        scratch(cols, 32, in_width),
+        scratch(cols, 2 * rows, units),
+        scratch(cols, ring, 32, width),
+        scratch(ring, cols * rows, in_width),
+        scratch(ring, cols * rows, units),
+        scratch(ring, cols * rows, units),
+        scratch(ring, block, width),
+        scratch(cols, 2 * LANES, width),
+        scratch(8, width, kind=f32),
+        scratch(row_len, LANES, kind=f32),
+        scratch(row_len, LANES, kind=f32),
+        scratch(row_len, LANES, kind=jnp.int32),
+        scratch(heads, row_len, LANES),
+        scratch(2, row_len, LANES),
+        scratch(2, row_len, LANES),
+        scratch(heads, row_len, row_len),
+        scratch(2, row_len, LANES, kind=f32),
+        scratch(cols, tok, 2 * LANES),
+        scratch(cols, tok, 2 * LANES),
+        scratch(tok, width, kind=f32),
+        scratch(tok, width, kind=f32),
+        stacked,
+        scratch(row_len, units, kind=f32),
+        scratch(row_len, units, kind=f32),
+        scratch(row_len, units),
+        stacked,
+        stacked,
+        scratch(tok, width, kind=f32),
+        stacked,
+        scratch(row_len, units),
+        scratch(row_len, units),
+        stacked,
+        stacked,
+        scratch(tok, width, kind=f32),
+        scratch(cols, tok, 2 * LANES),
+        scratch(cols, tok, 2 * LANES),
+        scratch(2, row_len, LANES, kind=f32),
+        scratch(2, row_len, LANES, kind=f32),
+        scratch(2, row_len, LANES, kind=f32),
+        scratch(row_len, in_width),
+        stacked,
+        stacked,
+        *sums(cols * rows, in_width),
+        *sums(cols * rows, units),
+        *sums(cols * rows, units),
+        *sums(block, width),
+        scratch(cols, 2, depth, 32, width),
+        scratch(cols, 2, depth, 32, width),
+        *sums(32, width),
+        scratch(cols * rows, units, kind=f32),
+        scratch(cols, 2 * rows, units),
+        scratch(cols, 2 * rows, units),
+        scratch(cols, 32, in_width),
+        scratch(cols, 32, in_width),
+        pltpu.SemaphoreType.DMA((160,)),
+        pltpu.SemaphoreType.DMA((160,)),
+    ]
+    vmem = pl.BlockSpec(memory_space=pltpu.VMEM)
+    tokens = row_len * width
+    outputs, input_grad, g_in, g_mlp, g_out, g_down = pl.pallas_call(
+        functools.partial(fused, depth),
+        out_shape=(
+            jax.ShapeDtypeStruct((tok, width), bf16),
+            jax.ShapeDtypeStruct((tok, width), bf16),
+            jax.ShapeDtypeStruct((cols, 32, in_width), bf16),
+            jax.ShapeDtypeStruct((cols, 2 * rows, units), bf16),
+            jax.ShapeDtypeStruct((32, width), f32),
+            jax.ShapeDtypeStruct((block, width), f32),
+        ),
+        in_specs=[pl.BlockSpec(memory_space=pltpu.SMEM)] + [vmem] * 7,
+        out_specs=(vmem,) * 6,
+        scratch_shapes=buffers,
+        compiler_params=pltpu.CompilerParams(
+            collective_id=0, has_side_effects=True, vmem_limit_bytes=60 * 2**20
+        ),
+        cost_estimate=pl.CostEstimate(
+            flops=6 * tokens * (3 * units + 4 * head_width),
+            bytes_accessed=8 * 2**20,
+            transcendentals=3 * row_len * row_len,
+        ),
+        name="layer",
+    )(doc_lengths, freq, inputs[0], cotangent[0], p_in, p_mlp, p_out, down_weight)
+
+    wide_in = g_in[:, :rows].astype(f32).transpose(1, 0, 2)
+    kind_pairs = wide_in[..., : 3 * LANES].reshape(rows, cols, 3, LANES)
+    kind_singles = wide_in[..., 3 * LANES : 3 * LANES + 3 * HALF].reshape(rows, cols, 3, HALF)
+    in_grad = jnp.concatenate([kind_pairs, kind_singles], axis=-1)
+    in_grad = in_grad.transpose(0, 2, 1, 3).reshape(rows, 3 * width)
+
+    def by_column(part):
+        return (
+            part.reshape(cols, rows, ring, block)
+            .transpose(1, 2, 0, 3)
+            .reshape(rows, ff)
+            .astype(f32)
+        )
+
+    small = g_out[rows : rows + 4, :rows]
+    return (
+        outputs[None],
+        input_grad[None],
+        in_grad,
+        g_out[:rows],
+        by_column(g_mlp[:, :rows]),
+        by_column(g_mlp[:, rows:]),
+        g_down,
+        small[0],
+        small[1],
+        small[2],
+        small[3],
+    )
+
+
+def pick(sizes):
+    def chosen(*args):
+        tok, width = args[0].shape[1:]
+        ring, cols = sizes["dp"], sizes["blk"]
+        fits = (
+            ring == 8
+            and cols == 4
+            and tok == LANES
+            and HEADS == 3 * cols
+            and width == HEADS * HALF
+            and args[2].shape[0] == 24
+            and args[4].shape[1] == 4 * width
+        )
+        if fits:
+            return fast_shards(ring // 2, *args)
+        return shards(*args)
+
+    return chosen
+
+
 def solution(mesh):
     placed = (
         P("dp", "blk", None),
@@ -388,7 +1263,7 @@
         P("dp", "blk", None),
     )
     return jax.shard_map(
-        shards,
+        pick(dict(mesh.shape)),
         mesh=mesh,
         in_specs=placed,
         out_specs=(

time: 980 us -> 190 us (0.19)
  waiting for transfers between devices: 702 us -> 0 us
  Pallas kernels: 0 us -> 173 us
  blocking collectives: 86.6 us -> 0 us
  matrix products: 57.5 us -> 0 us
  loops' own time: 39.2 us -> 0 us
  local copies, waits for them, and re-layouts: 42.7 us -> 12.8 us
  other arithmetic: 32.8 us -> 3.03 us
  between operations: 16.1 us -> 0.87 us
    reduce_scatter x9 -> x0, waiting for transfers between devices: 412 us -> none  [the longest x1 99.2 us: shards(): lax.psum_scatter(up_part.astype(jnp.bfloat16), 'dp', scatter_dimension=0,...]
    all_gather x5 -> x0, waiting for transfers between devices: 181 us -> none  [the longest x1 60.9 us: shards(): lax.all_gather(up_weight, ('dp', 'blk'), axis=0, tiled=True)]
    pallas_call x0 -> x1, Pallas kernels: none -> 173 us  [fast_shards(): pl.pallas_call(functools.partial(fused, depth), out_shape=(jax.ShapeDtype...]
    unnamed x18 -> x0, waiting for transfers between devices: 108 us -> none
    unnamed x3 -> x0, blocking collectives: 69.2 us -> none
    dot_general x43 -> x0, matrix products: 57.5 us -> none  [the longest x5 14.7 us: contract_rows(): lax.dot_general(left, right, (((0,), (0,)), ((), ())), preferred_element_...]
    another operation x15 -> x0, loops' own time: 39.2 us -> none  [the longest x3 38.6 us: run_groups(): lax.scan(group_step, carried, jnp.arange(group_count, dtype=jnp.int32))]
    all_gather x2 -> x0, blocking collectives: 17.4 us -> none  [the longest x1 8.72 us: shards(): lax.all_gather(value_low, 'blk', axis=0, tiled=True)]
  transfers between devices with their start and end apart: 16 -> 0, of which waited for: 14 -> 0; matrix products, arithmetic and copies ran while one was open for 9% -> 0% of each run, Pallas kernels for 0% -> 0%
where the time goes in v1:
time: 190 us
  Pallas kernels  173 us (91%)
  local copies, waits for them, and re-layouts  12.8 us (7%)
  other arithmetic  3.03 us (2%)
    pallas_call x1, Pallas kernels, fast_shards(): pl.pallas_call(functools.partial(fused, depth), out_shape=(jax.ShapeDtype...  173 us
    unnamed x21, local copies, waits for them, and re-layouts  3.86 us

profile of v1, /device:TPU:0, one launch (start us, length us, event | category | flops | bytes accessed | tf_op | source)
XLA Modules:
  0.0 189.7 jit_solution(6518087754990435579)
XLA Ops:
  0.7 0.8 fusion.8
  1.4 1.4 pad_maximum_fusion.1.p_out
  2.8 0.2 reshape.58
  3.1 0.1 concatenate.12
  3.2 0.7 pad.8.p_in
  3.9 0.3 copy-done.4
  4.2 0.2 reshape.59
  4.4 0.2 reshape.60
  4.6 0.7 copy-done.5
  5.3 0.2 reshape.61
  5.6 0.2 reshape.62
  5.7 0.7 pad_maximum_fusion.p_mlp
  6.5 173.0 %layer.1 = (bf16[128,768]{1,0:T(8,128)(2,1)}, bf16[128,768]{1,0:T(8,128)(2,1)}, bf16[4,32,640]{2,1,0:T(8,128)(2,1)}, bf16[4,48,768]{2,1,0:T(8,128)(2,1)}, f32[32,768]{1,0:T(8,128)}, /*index=5*/f32[96,768]{1,0:T(8,128)}) custom-call(s32[1,8]{1,0:T(1,128)} %lens.1, f32[8,128]{1,0:T(8,128)} %constant.5.clone.freq, bf16[128,768]{1,0:T(8,128)(2,1)} %bitcast.64, ...), custom_call_target="tpu_custom_call" | custom-call | flops 7247757312 | bytes 8388608 | tf_op jit(solution)/shard_map/layer/pallas_call | solution.py:1176
  179.5 1.4 slice_bitcast_fusion
  180.8 1.5 slice.70
  182.4 0.1 reshape.63
  182.5 0.1 reshape.64
  182.6 0.1 maximum_bitcast_fusion
  182.7 0.2 copy.47
  182.9 0.9 reshape.65
  183.8 0.1 copy-done
  183.9 0.2 reshape.69
  184.1 0.3 copy.49
  184.4 1.1 reshape.67
  185.4 0.2 reshape.68
  185.6 0.3 copy.48
  185.9 1.1 reshape.66
  187.0 0.7 copy.71
  187.6 0.3 copy-done.2
  188.0 0.7 copy.72
  188.6 0.4 copy-done.1
  189.0 0.7 copy.73
  (23 shorter events, 0.3 us)
Async XLA Ops:
  0.6 2.2 %copy-start.6 = (bf16[24,2304]{1,0:T(8,128)(2,1)S(1)}, bf16[24,2304]{1,0:T(8,128)(2,1)}, u32[]{:S(2)}) copy-start(bf16[24,2304]{1,0:T(8,128)(2,1)} %param.15) | copy-start | bytes 331780
  3.2 1.0 copy-start.4
  4.4 0.9 copy-start.5
  179.5 2.9 %copy-start.7 = (bf16[4,32,640]{2,1,0:T(8,128)(2,1)S(1)}, bf16[4,32,640]{2,1,0:T(8,128)(2,1)}, u32[]{:S(2)}) copy-start(bf16[4,32,640]{2,1,0:T(8,128)(2,1)} %get-tuple-element.19) | copy-start | bytes 491524
  182.9 1.0 copy-start
  185.9 1.1 copy-start.3
  187.0 1.0 copy-start.2
  188.0 1.0 copy-start.1

commit v2 on v1

--- a/solution.py
+++ b/solution.py
@@ -402,38 +402,235 @@
 
 
 class Wire:
-    def __init__(self, send_sem, recv_sem):
-        self.send_sem, self.recv_sem = send_sem, recv_sem
-        self.count, self.sent = 0, []
-
-    def push(self, src, dst, peer):
-        slot = self.count
-        self.count += 1
-        copy = pltpu.make_async_remote_copy(
+    def __init__(self, send_sem, recv_sem, is_inner):
+        self.send_sem, self.recv_sem, self.is_inner = send_sem, recv_sem, is_inner
+        self.sends, self.slots = 0, 0
+        self.sent = {None: [], True: [], False: []}
+
+    def slot(self):
+        self.slots += 1
+        return self.slots - 1
+
+    def copy(self, src, dst, peer, slot):
+        self.sends += 1
+        return pltpu.make_async_remote_copy(
             src_ref=src,
             dst_ref=dst,
-            send_sem=self.send_sem.at[slot],
+            send_sem=self.send_sem.at[self.sends - 1],
             recv_sem=self.recv_sem.at[slot],
             device_id=peer,
             device_id_type=MESH_IDS,
         )
-        copy.start()
-        self.sent.append(copy)
+
+    def push(self, src, dst, peer, slot=None, inner=None):
+        slot = self.slot() if slot is None else slot
+        copy = self.copy(src, dst, peer, slot)
+        self.sent[inner].append(copy)
+        if inner is None:
+            copy.start()
+        else:
+            pl.when(self.is_inner == inner)(copy.start)
         return slot
 
     def arrive(self, slot, dst, peer):
         pltpu.make_async_remote_copy(
             src_ref=dst,
             dst_ref=dst,
-            send_sem=self.send_sem.at[slot],
+            send_sem=self.send_sem.at[0],
             recv_sem=self.recv_sem.at[slot],
             device_id=peer,
             device_id_type=MESH_IDS,
         ).wait_recv()
 
     def finish(self):
-        for copy in self.sent:
-            copy.wait_send()
+        for inner, copies in self.sent.items():
+
+            def drain(copies=copies):
+                for copy in copies:
+                    copy.wait_send()
+
+            if inner is None:
+                drain()
+            else:
+                pl.when(self.is_inner == inner)(drain)
+
+
+class Plane:
+    def __init__(self, planes):
+        dp, self.blk = lax.axis_index("dp"), lax.axis_index("blk")
+        self.z, self.x = dp // 2, dp % 2
+        self.dp = dp
+        self.partner = self.z + 1 - 2 * (self.z % 2)
+        self.other = planes // 2 - self.z // (planes // 2)
+        self.outer = (planes - 1) * (self.other - 1)
+        self.inner = ((self.z + 1) // 2) % 2
+        self.order = (self.other, self.outer, self.partner, self.z)
+        self.side = (self.z * 2 + (1 - self.x), self.blk)
+
+    def at(self, plane):
+        return (plane * 2 + self.x, self.blk)
+
+
+class Spread:
+    def __init__(self, wire, place, target, tail):
+        self.wire, self.place, self.target = wire, place, target
+        self.height, self.main = target.shape[1], target.shape[1] - tail
+
+    def block(self, plane, column):
+        return self.target.at[plane * 2 + column, 0 : self.main]
+
+    def pair(self, plane):
+        return self.target.at[pl.ds(plane * 2, 2), self.main : self.height]
+
+    def along(self, source, own, slots):
+        p = self.place
+        self.wire.push(source, own, p.at(p.partner), slots[2])
+        self.wire.push(source, own, p.at(p.other), slots[0] + (1 - p.inner))
+
+    def start(self):
+        p, wire = self.place, self.wire
+        self.z_slots = [wire.slot() for _ in range(3)]
+        own = self.block(p.z, p.x)
+        self.along(own, own, self.z_slots)
+
+    def start_side(self):
+        p, wire = self.place, self.wire
+        self.x_slots = [wire.slot() for _ in range(4)]
+        own = self.block(p.z, p.x)
+        wire.push(own, own, p.side, self.x_slots[3])
+        if self.main < self.height:
+            rest = self.target.at[p.dp, self.main : self.height]
+            self.rest_slot = wire.push(rest, rest, p.side)
+
+    def tail(self):
+        p, wire = self.place, self.wire
+        rest = self.target.at[p.z * 2 + (1 - p.x), self.main : self.height]
+        wire.arrive(self.rest_slot, rest, p.side)
+        self.t_slots = [wire.slot() for _ in range(3)]
+        self.along(self.pair(p.z), self.pair(p.z), self.t_slots)
+
+    def relay(self, j):
+        p, wire = self.place, self.wire
+        plane = p.order[j]
+        block = self.block(plane, p.x)
+        wire.arrive(self.z_slots[j], block, p.side)
+        if j < 2:
+            wire.push(block, block, p.at(p.partner), self.z_slots[j], inner=True)
+        wire.push(block, block, p.side, self.x_slots[j])
+        if self.main < self.height:
+            pair = self.pair(plane)
+            wire.arrive(self.t_slots[j], pair, p.side)
+            if j < 2:
+                wire.push(pair, pair, p.at(p.partner), self.t_slots[j], inner=True)
+
+    def settle(self):
+        p = self.place
+        for j in range(4):
+            self.wire.arrive(self.x_slots[j], self.block(p.order[j], 1 - p.x), p.side)
+
+
+class Collect:
+    def __init__(self, wire, place, buffers):
+        self.wire, self.place = wire, place
+        self.part, self.inbox, self.staged, self.landing = buffers[:4]
+        self.height, self.main = self.part.shape[2], self.inbox.shape[1]
+        self.split = self.main < self.height
+        if self.split:
+            self.t_landing, self.t_staged, self.t_cross, self.t_kept = buffers[4:]
+
+    def pair(self, plane):
+        return self.part.at[:, plane, self.main : self.height]
+
+    def send(self):
+        p, wire = self.place, self.wire
+        self.x_slots = [wire.slot() for _ in range(4)]
+        for j in (1, 0, 2, 3):
+            plane = p.order[j]
+            wire.push(
+                self.part.at[1 - p.x, plane, 0 : self.main],
+                self.inbox.at[plane],
+                p.side,
+                self.x_slots[j],
+            )
+        self.z_slots = [wire.slot() for _ in range(4)]
+        if self.split:
+            self.t_slots = [wire.slot() for _ in range(4)]
+            for j in range(3):
+                wire.push(
+                    self.pair(p.order[j]),
+                    self.t_landing.at[j],
+                    p.at(p.partner),
+                    self.t_slots[j],
+                    inner=None if j == 2 else False,
+                )
+
+    def first(self, j):
+        p, wire = self.place, self.wire
+        plane = p.order[j]
+        wire.arrive(self.x_slots[j], self.inbox.at[plane], p.side)
+        both = self.part[p.x, plane, 0 : self.main].astype(jnp.float32)
+        both = both + self.inbox[plane].astype(jnp.float32)
+        self.staged[plane] = both.astype(jnp.bfloat16)
+        wire.push(
+            self.staged.at[plane],
+            self.landing.at[j],
+            p.at(p.partner),
+            self.z_slots[j],
+            inner=None if j == 2 else False,
+        )
+
+    def second(self, j):
+        p, wire = self.place, self.wire
+        plane = p.order[j]
+        copy = wire.copy(self.staged.at[plane], self.landing.at[3], p.at(plane), self.z_slots[3])
+        wire.sent[True].append(copy)
+        if self.split:
+            t_copy = wire.copy(
+                self.t_staged.at[j], self.t_landing.at[3], p.at(plane), self.t_slots[3]
+            )
+            wire.sent[True].append(t_copy)
+
+        @pl.when(wire.is_inner)
+        def _():
+            wire.arrive(self.z_slots[j], self.landing.at[j], p.side)
+            both = self.staged[plane].astype(jnp.float32) + self.landing[j].astype(jnp.float32)
+            self.staged[plane] = both.astype(jnp.bfloat16)
+            copy.start()
+            if self.split:
+                wire.arrive(self.t_slots[j], self.t_landing.at[j], p.side)
+                rest = self.part[:, plane, self.main : self.height].astype(jnp.float32)
+                rest = rest + self.t_landing[j].astype(jnp.float32)
+                self.t_staged[j] = rest.astype(jnp.bfloat16)
+                t_copy.start()
+
+    def tail(self):
+        p, wire = self.place, self.wire
+        for j in (2, 3):
+            wire.arrive(self.t_slots[j], self.t_landing.at[j], p.side)
+
+        def rest_of(column):
+            rest = self.part[column, p.z, self.main : self.height].astype(jnp.float32)
+            for j in (2, 3):
+                rest = rest + self.t_landing[j, column].astype(jnp.float32)
+            return rest
+
+        self.t_kept[...] = rest_of(p.x)
+        self.t_cross[0] = rest_of(1 - p.x).astype(jnp.bfloat16)
+        self.cross_slot = wire.push(self.t_cross.at[0], self.t_cross.at[1], p.side)
+
+    def total(self):
+        p, wire = self.place, self.wire
+        wire.arrive(self.x_slots[3], self.inbox.at[p.z], p.side)
+        total = self.part[p.x, p.z, 0 : self.main].astype(jnp.float32)
+        total = total + self.inbox[p.z].astype(jnp.float32)
+        for j in (2, 3):
+            wire.arrive(self.z_slots[j], self.landing.at[j], p.side)
+            total = total + self.landing[j].astype(jnp.float32)
+        if not self.split:
+            return total
+        wire.arrive(self.cross_slot, self.t_cross.at[1], p.side)
+        rest = self.t_kept[...] + self.t_cross[1].astype(jnp.float32)
+        return jnp.concatenate([total, rest], axis=0)
 
 
 def fused(
@@ -480,12 +677,14 @@
     act,
     s_mix,
     r_mix,
+    t_mix,
     dres_two,
     dms,
     dgate,
     dup,
     s_dh,
     r_dh,
+    t_dh,
     dres_one,
     s_da,
     r_da,
@@ -495,28 +694,14 @@
     dj,
     s_ig,
     r_ig,
-    pr_in,
-    rx_in,
-    sz_in,
-    rz_in,
-    pr_gate,
-    rx_gate,
-    sz_gate,
-    rz_gate,
-    pr_up,
-    rx_up,
-    sz_up,
-    rz_up,
-    pr_down,
-    rx_down,
-    sz_down,
-    rz_down,
+    t_ig,
+    sum_in,
+    sum_gate,
+    sum_up,
+    sum_down,
     b_out,
     rb_out,
-    pr_out,
-    rx_out,
-    sz_out,
-    rz_out,
+    sum_out,
     f_gate,
     s_gmlp,
     r_gmlp,
@@ -528,19 +713,15 @@
     planes, cols = depth, 4
     tok = xin.shape[0]
     row_len = tok * cols
-    dp = lax.axis_index("dp")
-    blk = lax.axis_index("blk")
-    z, x = dp // 2, dp % 2
+    place = Plane(planes)
+    dp, blk = place.dp, place.blk
     bf16, f32 = jnp.bfloat16, jnp.float32
 
-    def side():
-        return (z * 2 + (1 - x), blk)
-
-    def tier(k):
-        return (((z + k) % planes) * 2 + x, blk)
-
-    def tier_from(k):
-        return (z + planes - k) % planes
+    row_of, core_of = blk // 2, blk % 2
+    near_at = row_of * 2 + (1 - core_of)
+    across_at = (1 - row_of) * 2 + core_of
+    corner_at = (1 - row_of) * 2 + (1 - core_of)
+    near, across = (dp, near_at), (dp, across_at)
 
     def lane(k):
         return (dp, (blk + k) % cols)
@@ -548,10 +729,11 @@
     def lane_from(k):
         return (blk + cols - k) % cols
 
-    tiers, lanes = range(1, planes), range(1, cols)
-    wire = Wire(send_sem, recv_sem)
+    lanes = range(1, cols)
+    wire = Wire(send_sem, recv_sem, place.inner == 1)
     barrier = pltpu.get_barrier_semaphore()
-    peers = [side()] + [tier(k) for k in tiers] + [lane(k) for k in lanes]
+    peers = [place.side] + [place.at(plane) for plane in place.order[:3]]
+    peers = peers + [lane(k) for k in lanes]
     for peer in peers:
         pl.semaphore_signal(barrier, inc=1, device_id=peer, device_id_type=MESH_IDS)
     pl.semaphore_wait(barrier, len(peers))
@@ -563,29 +745,52 @@
         for k, slot in zip(lanes, slots):
             wire.arrive(slot, target.at[lane_from(k)], lane(k))
 
-    def spread_tiers(source, target):
-        return [wire.push(source, target.at[dp], tier(k)) for k in tiers]
-
-    def from_tier(slots, target, k):
-        wire.arrive(slots[k - 1], target.at[tier_from(k) * 2 + x], tier(k))
-
-    def spread_side(source, target, plane):
-        return wire.push(source, target.at[plane * 2 + x], side())
-
-    def from_side(slot, target, plane):
-        wire.arrive(slot, target.at[plane * 2 + (1 - x)], side())
-
-    own_out = s_out.at[blk]
+    def gather_start(source, target):
+        return [
+            wire.push(source, target.at[blk], across),
+            wire.push(source, target.at[blk], near),
+        ]
+
+    def gather_relay(slots, target):
+        wire.arrive(slots[0], target.at[across_at], across)
+        slots.append(wire.push(target.at[across_at], target.at[across_at], near))
+
+    def gather_done(slots, target):
+        wire.arrive(slots[1], target.at[near_at], near)
+        wire.arrive(slots[2], target.at[corner_at], near)
+
+    def sum_start(part, inbox):
+        return [
+            wire.push(part.at[corner_at], inbox.at[0], near),
+            wire.push(part.at[near_at], inbox.at[1], near),
+        ]
+
+    def sum_relay(slots, part, inbox, staged):
+        wire.arrive(slots[0], inbox.at[0], near)
+        staged[...] = (part[across_at].astype(f32) + inbox[0].astype(f32)).astype(bf16)
+        slots.append(wire.push(staged, inbox.at[2], across))
+
+    def sum_done(slots, part, inbox):
+        wire.arrive(slots[1], inbox.at[1], near)
+        total = part[blk].astype(f32) + inbox[1].astype(f32)
+        wire.arrive(slots[2], inbox.at[2], across)
+        return total + inbox[2].astype(f32)
+
     in_slots = to_lanes(lambda to: p_in.at[to], r_in)
-    out_tiers = spread_tiers(p_out, own_out)
-    out_sides = [spread_side(p_out, own_out, z)]
-    x_slots = to_lanes(lambda to: xin, xs)
+    s_out[blk, dp] = p_out[...]
+    w_down[dp] = p_down[...]
+    tail = 0
+    out_spread = Spread(wire, place, s_out.at[blk], 0)
+    out_spread.start()
+    out_spread.start_side()
+    down_spread = Spread(wire, place, w_down, tail)
+    down_spread.start()
+    down_spread.start_side()
     mlp_slots = to_lanes(lambda to: p_mlp.at[to], r_mlp)
     xs[blk] = xin[...]
+    x_slots = gather_start(xin, xs)
     r_in[blk] = p_in[blk]
     r_mlp[blk] = p_mlp[blk]
-    s_out[blk, dp] = p_out[...]
-    w_down[dp] = p_down[...]
 
     lengths = [lens[0, j] for j in range(lens.shape[1])]
 
@@ -620,33 +825,30 @@
     w_in[dp] = jnp.concatenate(
         [r_in[j, 0:rows, :].astype(f32) for j in range(cols)], axis=0
     ).astype(bf16)
-    in_tiers = spread_tiers(w_in.at[dp], w_in)
-    in_sides = [spread_side(w_in.at[dp], w_in, z)]
+    in_spread = Spread(wire, place, w_in, tail)
+    in_spread.start()
+    in_spread.start_side()
+    for j in (2, 0, 1):
+        out_spread.relay(j)
     from_lanes(mlp_slots, r_mlp)
     mlp_own = [r_mlp[j].astype(f32) for j in range(cols)]
     w_gate[dp] = jnp.concatenate([part[0:rows] for part in mlp_own], axis=0).astype(bf16)
     w_up[dp] = jnp.concatenate([part[rows:] for part in mlp_own], axis=0).astype(bf16)
-    gate_tiers = spread_tiers(w_gate.at[dp], w_gate)
-    up_tiers = spread_tiers(w_up.at[dp], w_up)
-    down_tiers = spread_tiers(p_down, w_down)
-
-    def relay(tier_slots, side_slots, target):
-        for k in tiers:
-            from_tier(tier_slots, target, k)
-            plane = tier_from(k)
-            side_slots.append(spread_side(target.at[plane * 2 + x], target, plane))
-
-    def settle(side_slots, target):
-        for k in range(planes):
-            from_side(side_slots[k], target, tier_from(k))
-
-    relay(out_tiers, out_sides, own_out)
-    relay(in_tiers, in_sides, w_in)
-    gate_sides = [spread_side(w_gate.at[dp], w_gate, z)]
-    settle(out_sides, own_out)
-    out_lanes = to_lanes(lambda to: own_out, s_out)
-    from_lanes(x_slots, xs)
-    settle(in_sides, w_in)
+    gate_spread = Spread(wire, place, w_gate, tail)
+    up_spread = Spread(wire, place, w_up, tail)
+    gate_spread.start()
+    for j in (2, 0, 1):
+        in_spread.relay(j)
+    gate_spread.start_side()
+    up_spread.start()
+    up_spread.start_side()
+    gather_relay(x_slots, xs)
+    out_spread.settle()
+    out_lanes = gather_start(s_out.at[blk], s_out)
+    for j in (2, 0, 1):
+        down_spread.relay(j)
+    gather_done(x_slots, xs)
+    in_spread.settle()
 
     width = xin.shape[1]
     group = 2
@@ -699,13 +901,8 @@
         lax.fori_loop(0, row_len // chunk, step_fn, 0)
 
     attend(0)
-    relay(gate_tiers, gate_sides, w_gate)
-    up_sides = [spread_side(w_up.at[dp], w_up, z)]
     attend(1)
-    relay(up_tiers, up_sides, w_up)
-    down_sides = [spread_side(p_down, w_down, z)]
     attend(2)
-
     last_segment = lens.shape[1] - 1
     for j in range(cols):
         here = slice(j * tok, (j + 1) * tok)
@@ -715,7 +912,10 @@
     att_slots = to_lanes(lambda to: s_att.at[to], r_att)
     r_att[blk] = s_att[blk]
 
-    from_lanes(out_lanes, s_out)
+    gather_relay(out_lanes, s_out)
+    for j in (2, 0, 1):
+        gate_spread.relay(j)
+    gather_done(out_lanes, s_out)
     shards = planes * 2 * cols
     per_quarter = shards // cols
     head_rows = per_quarter * rows
@@ -773,11 +973,13 @@
     hidden = normal * gain_one + bias_one
     hid[...] = hidden
     hs[blk] = hidden.astype(bf16)
-    hid_slots = to_lanes(lambda to: hs.at[blk], hs)
-    relay(down_tiers, down_sides, w_down)
-    settle(gate_sides, w_gate)
-    settle(up_sides, w_up)
-    from_lanes(hid_slots, hs)
+    hid_slots = gather_start(hs.at[blk], hs)
+    gate_spread.settle()
+    gather_relay(hid_slots, hs)
+    for j in (2, 0, 1):
+        up_spread.relay(j)
+    gather_done(hid_slots, hs)
+    up_spread.settle()
 
     units = w_gate.shape[2]
     wide = 256
@@ -794,7 +996,7 @@
         return carry
 
     lax.fori_loop(0, strips, expand, 0)
-    settle(down_sides, w_down)
+    down_spread.settle()
 
     def contract(step, carry):
         here = pl.ds(pl.multiple_of(step * wide, wide), wide)
@@ -803,12 +1005,9 @@
         return carry
 
     lax.fori_loop(0, width // wide, contract, 0)
-    mix_slots = to_lanes(lambda to: s_mix.at[to], r_mix)
-    r_mix[blk] = s_mix[blk]
-    from_lanes(mix_slots, r_mix)
-    mlp_out = r_mix[0].astype(f32)
-    for j in range(1, cols):
-        mlp_out = mlp_out + r_mix[j].astype(f32)
+    mix_slots = sum_start(s_mix, r_mix)
+    sum_relay(mix_slots, s_mix, r_mix, t_mix)
+    mlp_out = sum_done(mix_slots, s_mix, r_mix)
     normal, spread_two = normalize(hid[...] + mlp_out)
     outputs[...] = (normal * gain_two + bias_two).astype(bf16)
     grad = cot[...].astype(f32)
@@ -817,30 +1016,15 @@
     d_two = normalize_back(grad, normal, spread_two, gain_two)
     dres_two[...] = d_two
     dms[blk] = d_two.astype(bf16)
-    dm_slots = to_lanes(lambda to: dms.at[blk], dms)
-    from_lanes(dm_slots, dms)
-
-    def send_side(part, inbox):
-        order = [(z + k) % planes for k in list(tiers) + [0]]
-        return [wire.push(part.at[1 - x, to], inbox.at[to], side()) for to in order]
-
-    def pass_on(part, inbox, staged, landing, side_slots):
-        tier_slots = []
-        for k in tiers:
-            to = (z + k) % planes
-            wire.arrive(side_slots[k - 1], inbox.at[to], side())
-            staged[to] = (part[x, to].astype(f32) + inbox[to].astype(f32)).astype(bf16)
-            tier_slots.append(wire.push(staged.at[to], landing.at[k], tier(k)))
-        wire.arrive(side_slots[planes - 1], inbox.at[z], side())
-        return tier_slots
-
-    def total_of(part, inbox, landing, tier_slots):
-        total = part[x, z].astype(f32) + inbox[z].astype(f32)
-        for k in tiers:
-            wire.arrive(tier_slots[k - 1], landing.at[k], tier(k))
-            total = total + landing[k].astype(f32)
-        return total
-
+    dm_slots = gather_start(dms.at[blk], dms)
+    gather_relay(dm_slots, dms)
+    gather_done(dm_slots, dms)
+
+    down_sum = Collect(wire, place, sum_down)
+    gate_sum = Collect(wire, place, sum_gate)
+    up_sum = Collect(wire, place, sum_up)
+    in_sum = Collect(wire, place, sum_in)
+    out_sum = Collect(wire, place, sum_out)
     half = 4
 
     def fill_parts(part, left_of, right):
@@ -857,8 +1041,8 @@
 
         lax.fori_loop(0, planes * 2 // half, step_fn, 0)
 
-    fill_parts(pr_down, lambda here: act[:, here], lambda: dms[...].reshape(row_len, width))
-    down_x = send_side(pr_down, rx_down)
+    fill_parts(down_sum.part, lambda here: act[:, here], lambda: dms[...].reshape(row_len, width))
+    down_sum.send()
 
     block = w_down.shape[1]
 
@@ -887,21 +1071,21 @@
         return carry
 
     lax.fori_loop(0, planes * 2 // half, hidden_grads, 0)
-    dh_slots = to_lanes(lambda to: s_dh.at[to], r_dh)
-    r_dh[blk] = s_dh[blk]
+    dh_slots = sum_start(s_dh, r_dh)
 
     def hidden_rows(here):
         return hs[:, :, here].reshape(row_len, half * block)
 
-    fill_parts(pr_gate, hidden_rows, lambda: dgate[...])
-    gate_x = send_side(pr_gate, rx_gate)
-    fill_parts(pr_up, hidden_rows, lambda: dup[...])
-    up_x = send_side(pr_up, rx_up)
-
-    from_lanes(dh_slots, r_dh)
-    d_hidden = dres_two[...]
-    for j in range(cols):
-        d_hidden = d_hidden + r_dh[j].astype(f32)
+    fill_parts(gate_sum.part, hidden_rows, lambda: dgate[...])
+    gate_sum.send()
+    sum_relay(dh_slots, s_dh, r_dh, t_dh)
+    fill_parts(up_sum.part, hidden_rows, lambda: dup[...])
+    up_sum.send()
+    down_sum.first(1)
+    down_sum.first(0)
+    d_hidden = dres_two[...] + sum_done(dh_slots, s_dh, r_dh)
+    down_sum.second(1)
+    down_sum.first(2)
     normal = norm_one[...]
     first_gain = column_sum(d_hidden * normal)
     first_bias = column_sum(d_hidden)
@@ -936,9 +1120,8 @@
     out_blk = to_lanes(lambda to: b_out.at[to], rb_out)
     rb_out[blk] = b_out[blk]
 
-    down_z = pass_on(pr_down, rx_down, sz_down, rz_down, down_x)
+    down_sum.second(0)
     from_lanes(da_slots, r_da)
-
     def attend_back(head):
         window = head // 2
         fresh = head != 1
@@ -981,6 +1164,7 @@
         lax.fori_loop(0, row_len // chunk, step_fn, 0)
 
     attend_back(0)
+    gate_sum.first(1)
     attend_back(1)
     attend_back(2)
 
@@ -996,50 +1180,59 @@
     dj[:, 3 * LANES : 4 * LANES] = rotate_back(acc_q[1] + pltpu.roll(acc_k[1], HALF, 1))
     dj[:, 4 * LANES : 5 * LANES] = acc_v[1].astype(bf16)
 
+    gate_sum.first(0)
+    fill_parts(in_sum.part, lambda here: xs[:, :, here].reshape(row_len, half * block), lambda: dj[...])
+
+    def input_grads(step, carry):
+        here = pl.ds(pl.multiple_of(step * half * block, LANES), half * block)
+        mixed = mt(dj[...], w_in[pl.ds(step * half, half)].reshape(half * block, w_in.shape[2]))
+        s_ig[:, :, here] = mixed.reshape(cols, tok, half * block).astype(bf16)
+        return carry
+
+    lax.fori_loop(0, planes * 2 // half, input_grads, 0)
+    ig_slots = sum_start(s_ig, r_ig)
+
+    gate_sum.second(1)
+    gate_sum.first(2)
+    sum_relay(ig_slots, s_ig, r_ig, t_ig)
+    g_down[...] = down_sum.total()
+    gate_sum.second(0)
+    up_sum.first(1)
     from_lanes(out_blk, rb_out)
     for side_at in range(2):
         gathered = rb_out[0, side_at].astype(f32)
         for j in range(1, cols):
             gathered = gathered + rb_out[j, side_at].astype(f32)
-        pr_out[side_at] = gathered.astype(bf16)
-    out_x = send_side(pr_out, rx_out)
-
-    fill_parts(pr_in, lambda here: xs[:, :, here].reshape(row_len, half * block), lambda: dj[...])
-    in_x = send_side(pr_in, rx_in)
-
-    def input_grads(step, carry):
-        here = pl.ds(pl.multiple_of(step * half * block, LANES), half * block)
-        mixed = mt(dj[...], w_in[pl.ds(step * half, half)].reshape(half * block, w_in.shape[2]))
-        s_ig[:, :, here] = mixed.reshape(cols, tok, half * block).astype(bf16)
-        return carry
-
-    lax.fori_loop(0, planes * 2 // half, input_grads, 0)
-    ig_slots = to_lanes(lambda to: s_ig.at[to], r_ig)
-    r_ig[blk] = s_ig[blk]
-
-    gate_z = pass_on(pr_gate, rx_gate, sz_gate, rz_gate, gate_x)
-    g_down[...] = total_of(pr_down, rx_down, rz_down, down_z)
-    up_z = pass_on(pr_up, rx_up, sz_up, rz_up, up_x)
-    gate_total = total_of(pr_gate, rx_gate, rz_gate, gate_z)
-    f_gate[...] = gate_total
-    out_z = pass_on(pr_out, rx_out, sz_out, rz_out, out_x)
-    from_lanes(ig_slots, r_ig)
-    grad_in = dres_one[...]
-    for j in range(cols):
-        grad_in = grad_in + r_ig[j].astype(f32)
+        out_sum.part[side_at] = gathered.astype(bf16)
+    out_sum.send()
+    in_sum.send()
+    up_sum.first(0)
+    up_sum.second(1)
+    up_sum.first(2)
+    f_gate[...] = gate_sum.total()
+    up_sum.second(0)
+    grad_in = dres_one[...] + sum_done(ig_slots, s_ig, r_ig)
     input_grad[...] = grad_in.astype(bf16)
-    up_total = total_of(pr_up, rx_up, rz_up, up_z)
+    for j in (1, 0, 2):
+        out_sum.first(j)
+    in_sum.first(1)
+    up_total = up_sum.total()
     gate_total = f_gate[...]
     for j in range(cols):
         here = slice(j * rows, (j + 1) * rows)
         s_gmlp[j] = jnp.concatenate([gate_total[here], up_total[here]], axis=0).astype(bf16)
     gmlp_slots = to_lanes(lambda to: s_gmlp.at[to], r_gmlp)
     r_gmlp[blk] = s_gmlp[blk]
-    in_z = pass_on(pr_in, rx_in, sz_in, rz_in, in_x)
-    g_out[...] = total_of(pr_out, rx_out, rz_out, out_z)
+    in_sum.first(0)
+    out_sum.second(1)
+    out_sum.second(0)
+    in_sum.second(1)
+    in_sum.first(2)
+    in_sum.second(0)
+    g_out[...] = out_sum.total()
     from_lanes(gmlp_slots, r_gmlp)
     g_mlp[...] = r_gmlp[...]
-    in_total = total_of(pr_in, rx_in, rz_in, in_z)
+    in_total = in_sum.total()
     for j in range(cols):
         s_gin[j] = jnp.concatenate(
             [in_total[j * rows : (j + 1) * rows], jnp.zeros((8, in_total.shape[1]), f32)], axis=0
@@ -1102,13 +1295,22 @@
     def scratch(*shape, kind=bf16):
         return pltpu.VMEM(shape, kind)
 
-    def sums(height, across):
-        return [
+    def sums(height, across, tail=0):
+        main = height - tail
+        buffers = [
             scratch(2, depth, height, across),
-            scratch(depth, height, across),
-            scratch(depth, height, across),
-            scratch(depth, height, across),
+            scratch(depth, main, across),
+            scratch(depth, main, across),
+            scratch(4, main, across),
         ]
+        if tail:
+            buffers = buffers + [
+                scratch(4, 2, tail, across),
+                scratch(2, 2, tail, across),
+                scratch(2, tail, across),
+                scratch(tail, across, kind=f32),
+            ]
+        return tuple(buffers)
 
     stacked = scratch(cols, tok, width)
     heads = 3
@@ -1140,13 +1342,15 @@
         scratch(row_len, units, kind=f32),
         scratch(row_len, units),
         stacked,
-        stacked,
+        scratch(3, tok, width),
+        scratch(tok, width),
         scratch(tok, width, kind=f32),
         stacked,
         scratch(row_len, units),
         scratch(row_len, units),
         stacked,
-        stacked,
+        scratch(3, tok, width),
+        scratch(tok, width),
         scratch(tok, width, kind=f32),
         scratch(cols, tok, 2 * LANES),
         scratch(cols, tok, 2 * LANES),
@@ -1155,21 +1359,22 @@
         scratch(2, row_len, LANES, kind=f32),
         scratch(row_len, in_width),
         stacked,
-        stacked,
-        *sums(cols * rows, in_width),
-        *sums(cols * rows, units),
-        *sums(cols * rows, units),
-        *sums(block, width),
+        scratch(3, tok, width),
+        scratch(tok, width),
+        sums(cols * rows, in_width),
+        sums(cols * rows, units),
+        sums(cols * rows, units),
+        sums(block, width),
         scratch(cols, 2, depth, 32, width),
         scratch(cols, 2, depth, 32, width),
-        *sums(32, width),
+        sums(32, width, 0),
         scratch(cols * rows, units, kind=f32),
         scratch(cols, 2 * rows, units),
         scratch(cols, 2 * rows, units),
         scratch(cols, 32, in_width),
         scratch(cols, 32, in_width),
-        pltpu.SemaphoreType.DMA((160,)),
-        pltpu.SemaphoreType.DMA((160,)),
+        pltpu.SemaphoreType.DMA((240,)),
+        pltpu.SemaphoreType.DMA((240,)),
     ]
     vmem = pl.BlockSpec(memory_space=pltpu.VMEM)
     tokens = row_len * width

time: 190 us -> 168 us (0.88)
  Pallas kernels: 173 us -> 151 us
    pallas_call x1, Pallas kernels: 173 us -> 151 us  [fast_shards(): pl.pallas_call(functools.partial(fused, depth), out_shape=(jax.ShapeDtype...]
where the time goes in v2:
time: 168 us; the launch traced here: 167 us
  Pallas kernels  151 us (90%)
  local copies, waits for them, and re-layouts  12.8 us (8%)
  other arithmetic  3.03 us (2%)
    pallas_call x1, Pallas kernels, fast_shards(): pl.pallas_call(functools.partial(fused, depth), out_shape=(jax.ShapeDtype...  151 us
    unnamed x21, local copies, waits for them, and re-layouts  3.86 us

profile of v2, /device:TPU:0, one launch (start us, length us, event | category | flops | bytes accessed | tf_op | source)
XLA Modules:
  0.0 167.5 jit_solution(5921478244406015552)
XLA Ops:
  0.7 0.8 fusion.8
  1.4 1.4 pad_maximum_fusion.1.p_out
  2.8 0.2 reshape.58
  3.1 0.1 concatenate.12
  3.2 0.7 pad.8.p_in
  3.9 0.3 copy-done.4
  4.2 0.2 reshape.59
  4.4 0.2 reshape.60
  4.6 0.7 copy-done.5
  5.3 0.2 reshape.61
  5.6 0.2 reshape.62
  5.7 0.7 pad_maximum_fusion.p_mlp
  6.5 150.7 %layer.1 = (bf16[128,768]{1,0:T(8,128)(2,1)}, bf16[128,768]{1,0:T(8,128)(2,1)}, bf16[4,32,640]{2,1,0:T(8,128)(2,1)}, bf16[4,48,768]{2,1,0:T(8,128)(2,1)}, f32[32,768]{1,0:T(8,128)}, /*index=5*/f32[96,768]{1,0:T(8,128)}) custom-call(s32[1,8]{1,0:T(1,128)} %lens.1, f32[8,128]{1,0:T(8,128)} %constant.5.clone.freq, bf16[128,768]{1,0:T(8,128)(2,1)} %bitcast.64, ...), custom_call_target="tpu_custom_call" | custom-call | flops 7247757312 | bytes 8388608 | tf_op jit(solution)/shard_map/layer/pallas_call | solution.py:1381
  157.2 1.4 slice_bitcast_fusion
  158.6 1.5 slice.70
  160.2 0.1 reshape.63
  160.2 0.1 reshape.64
  160.4 0.1 maximum_bitcast_fusion
  160.5 0.2 copy.47
  160.7 0.9 reshape.65
  161.5 0.1 copy-done
  161.7 0.2 reshape.69
  161.9 0.3 copy.49
  162.1 1.1 reshape.67
  163.2 0.2 reshape.68
  163.4 0.3 copy.48
  163.7 1.1 reshape.66
  164.7 0.7 copy.71
  165.4 0.3 copy-done.2
  165.7 0.7 copy.72
  166.4 0.4 copy-done.1
  166.8 0.7 copy.73
  (23 shorter events, 0.3 us)
Async XLA Ops:
  0.6 2.2 %copy-start.6 = (bf16[24,2304]{1,0:T(8,128)(2,1)S(1)}, bf16[24,2304]{1,0:T(8,128)(2,1)}, u32[]{:S(2)}) copy-start(bf16[24,2304]{1,0:T(8,128)(2,1)} %param.15) | copy-start | bytes 331780
  3.2 1.0 copy-start.4
  4.4 0.9 copy-start.5
  157.2 2.9 %copy-start.7 = (bf16[4,32,640]{2,1,0:T(8,128)(2,1)S(1)}, bf16[4,32,640]{2,1,0:T(8,128)(2,1)}, u32[]{:S(2)}) copy-start(bf16[4,32,640]{2,1,0:T(8,128)(2,1)} %get-tuple-element.19) | copy-start | bytes 491524
  160.7 1.0 copy-start
  163.7 1.1 copy-start.3
  164.7 1.0 copy-start.2
  165.7 1.0 copy-start.1

commit v3 on v2

--- a/solution.py
+++ b/solution.py
@@ -381,6 +381,7 @@
 LANES = 128
 HALF = 64
 QUART = 32
+DT = 48
 
 
 def mm(left, right):
@@ -399,6 +400,25 @@
     return lax.dot_general(
         left, right, (((0,), (0,)), ((), ())), preferred_element_type=jnp.float32
     )
+
+
+def window_at(value, start):
+    aligned = min(max(start // LANES * LANES, 0), value.shape[1] - LANES)
+    if aligned == start:
+        return value[:, aligned : aligned + LANES]
+    aligned = min(aligned, value.shape[1] - 2 * LANES)
+    two = value[:, aligned : aligned + 2 * LANES]
+    return pltpu.roll(two, (aligned - start) % (2 * LANES), 1)[:, :LANES]
+
+
+def gather_lanes(value, block, first, source):
+    lanes = lax.broadcasted_iota(jnp.int32, (1, LANES), 1)
+    result = None
+    for number in range(first // block, (first + LANES - 1) // block + 1):
+        piece = window_at(value, source(number, first))
+        begin = number * block - first
+        result = piece if result is None else jnp.where(lanes < begin, result, piece)
+    return result
 
 
 class Wire:
@@ -482,16 +502,23 @@
     def pair(self, plane):
         return self.target.at[pl.ds(plane * 2, 2), self.main : self.height]
 
-    def along(self, source, own, slots):
+    def along(self, own, slots):
         p = self.place
-        self.wire.push(source, own, p.at(p.partner), slots[2])
-        self.wire.push(source, own, p.at(p.other), slots[0] + (1 - p.inner))
+        self.wire.push(own, own, p.at(p.partner), slots[2], inner=False)
+        self.wire.push(own, own, p.at(p.other), slots[0] + (1 - p.inner))
+
+    def outward(self, own, slots):
+        p = self.place
+        self.wire.push(own, own, p.at(p.partner), slots[2], inner=True)
 
     def start(self):
         p, wire = self.place, self.wire
         self.z_slots = [wire.slot() for _ in range(3)]
-        own = self.block(p.z, p.x)
-        self.along(own, own, self.z_slots)
+        self.along(self.block(p.z, p.x), self.z_slots)
+
+    def start_out(self):
+        p = self.place
+        self.outward(self.block(p.z, p.x), self.z_slots)
 
     def start_side(self):
         p, wire = self.place, self.wire
@@ -507,7 +534,10 @@
         rest = self.target.at[p.z * 2 + (1 - p.x), self.main : self.height]
         wire.arrive(self.rest_slot, rest, p.side)
         self.t_slots = [wire.slot() for _ in range(3)]
-        self.along(self.pair(p.z), self.pair(p.z), self.t_slots)
+        self.along(self.pair(p.z), self.t_slots)
+
+    def tail_out(self):
+        self.outward(self.pair(self.place.z), self.t_slots)
 
     def relay(self, j):
         p, wire = self.place, self.wire
@@ -517,11 +547,25 @@
         if j < 2:
             wire.push(block, block, p.at(p.partner), self.z_slots[j], inner=True)
         wire.push(block, block, p.side, self.x_slots[j])
-        if self.main < self.height:
-            pair = self.pair(plane)
+    def pass_tail(self, j):
+        p, wire = self.place, self.wire
+        pair = self.pair(p.order[j])
+        copy = wire.copy(pair, pair, p.at(p.partner), self.t_slots[j])
+        wire.sent[True].append(copy)
+
+        @pl.when(wire.is_inner)
+        def _():
             wire.arrive(self.t_slots[j], pair, p.side)
-            if j < 2:
-                wire.push(pair, pair, p.at(p.partner), self.t_slots[j], inner=True)
+            copy.start()
+
+    def settle_tail(self):
+        p, wire = self.place, self.wire
+        wire.arrive(self.t_slots[2], self.pair(p.order[2]), p.side)
+
+        @pl.when(jnp.logical_not(wire.is_inner))
+        def _():
+            for j in range(2):
+                wire.arrive(self.t_slots[j], self.pair(p.order[j]), p.side)
 
     def settle(self):
         p = self.place
@@ -555,7 +599,7 @@
         self.z_slots = [wire.slot() for _ in range(4)]
         if self.split:
             self.t_slots = [wire.slot() for _ in range(4)]
-            for j in range(3):
+            for j in (1, 0, 2):
                 wire.push(
                     self.pair(p.order[j]),
                     self.t_landing.at[j],
@@ -584,11 +628,6 @@
         plane = p.order[j]
         copy = wire.copy(self.staged.at[plane], self.landing.at[3], p.at(plane), self.z_slots[3])
         wire.sent[True].append(copy)
-        if self.split:
-            t_copy = wire.copy(
-                self.t_staged.at[j], self.t_landing.at[3], p.at(plane), self.t_slots[3]
-            )
-            wire.sent[True].append(t_copy)
 
         @pl.when(wire.is_inner)
         def _():
@@ -596,12 +635,20 @@
             both = self.staged[plane].astype(jnp.float32) + self.landing[j].astype(jnp.float32)
             self.staged[plane] = both.astype(jnp.bfloat16)
             copy.start()
-            if self.split:
-                wire.arrive(self.t_slots[j], self.t_landing.at[j], p.side)
-                rest = self.part[:, plane, self.main : self.height].astype(jnp.float32)
-                rest = rest + self.t_landing[j].astype(jnp.float32)
-                self.t_staged[j] = rest.astype(jnp.bfloat16)
-                t_copy.start()
+
+    def second_tail(self, j):
+        p, wire = self.place, self.wire
+        plane = p.order[j]
+        copy = wire.copy(self.t_staged.at[j], self.t_landing.at[3], p.at(plane), self.t_slots[3])
+        wire.sent[True].append(copy)
+
+        @pl.when(wire.is_inner)
+        def _():
+            wire.arrive(self.t_slots[j], self.t_landing.at[j], p.side)
+            rest = self.part[:, plane, self.main : self.height].astype(jnp.float32)
+            rest = rest + self.t_landing[j].astype(jnp.float32)
+            self.t_staged[j] = rest.astype(jnp.bfloat16)
+            copy.start()
 
     def tail(self):
         p, wire = self.place, self.wire
@@ -639,10 +686,15 @@
     freq,
     xin,
     cot,
-    p_in,
-    p_mlp,
-    p_out,
+    in_rows,
+    gate_rows,
+    up_rows,
+    out_rows,
     p_down,
+    gain_a,
+    bias_a,
+    gain_b,
+    bias_b,
     outputs,
     input_grad,
     g_in,
@@ -650,6 +702,9 @@
     g_out,
     g_down,
     xs,
+    p_in,
+    p_mlp,
+    vectors_tab,
     r_in,
     r_mlp,
     s_out,
@@ -701,6 +756,7 @@
     sum_down,
     b_out,
     rb_out,
+    tb_out,
     sum_out,
     f_gate,
     s_gmlp,
@@ -736,6 +792,33 @@
     peers = peers + [lane(k) for k in lanes]
     for peer in peers:
         pl.semaphore_signal(barrier, inc=1, device_id=peer, device_id_type=MESH_IDS)
+
+    rows = 24
+    width = xin.shape[1]
+    lane_ids = lax.broadcasted_iota(jnp.int32, (1, LANES), 1)
+    low_half = lane_ids < HALF
+    head_width = width // cols
+    joined_rows = in_rows[...].astype(f32)
+    for j in range(cols):
+        starts = [kind * width + j * head_width for kind in range(3)]
+        windows = [window_at(joined_rows, start) for start in starts]
+        windows.append(
+            jnp.where(
+                low_half,
+                window_at(joined_rows, starts[0] + LANES),
+                window_at(joined_rows, starts[1] + LANES - HALF),
+            )
+        )
+        windows.append(jnp.where(low_half, window_at(joined_rows, starts[2] + LANES), 0.0))
+        packed = jnp.concatenate(windows, axis=1)
+        p_in[j] = jnp.concatenate(
+            [packed, jnp.zeros((8, packed.shape[1]), f32)], axis=0
+        ).astype(bf16)
+    vectors_tab[...] = jnp.zeros_like(vectors_tab)
+    for number, vector in enumerate((gain_a, bias_a, gain_b, bias_b)):
+        vectors_tab[number : number + 1, 0:rows] = vector[...].astype(f32)
+    lower = jnp.concatenate([vectors_tab[...], jnp.zeros((8, width - LANES), f32)], axis=1)
+    s_out[blk, dp] = jnp.concatenate([out_rows[...].astype(f32), lower], axis=0).astype(bf16)
     pl.semaphore_wait(barrier, len(peers))
 
     def to_lanes(source_of, target):
@@ -777,15 +860,34 @@
         return total + inbox[2].astype(f32)
 
     in_slots = to_lanes(lambda to: p_in.at[to], r_in)
-    s_out[blk, dp] = p_out[...]
     w_down[dp] = p_down[...]
     tail = 0
     out_spread = Spread(wire, place, s_out.at[blk], 0)
     out_spread.start()
+    out_spread.start_out()
     out_spread.start_side()
-    down_spread = Spread(wire, place, w_down, tail)
+    down_spread = Spread(wire, place, w_down, DT)
     down_spread.start()
+    down_spread.start_out()
     down_spread.start_side()
+    units = gate_rows.shape[1] // cols
+    unit_block = units // (planes * 2)
+    for at, weight in ((0, gate_rows), (rows, up_rows)):
+        whole = weight[...].astype(f32)
+        for j in range(cols):
+            packed = jnp.concatenate(
+                [
+                    gather_lanes(
+                        whole,
+                        unit_block,
+                        n * LANES,
+                        lambda ring_at, lane: lane + (cols - 1) * unit_block * ring_at + unit_block * j,
+                    )
+                    for n in range(units // LANES)
+                ],
+                axis=1,
+            )
+            p_mlp[j, at : at + rows] = packed.astype(bf16)
     mlp_slots = to_lanes(lambda to: p_mlp.at[to], r_mlp)
     xs[blk] = xin[...]
     x_slots = gather_start(xin, xs)
@@ -808,8 +910,6 @@
     seg_rows, offsets = layout(lax.broadcasted_iota(jnp.int32, (row_len, LANES), 0))
     seg_tab[...] = seg_rows
     seg_key = layout(lax.broadcasted_iota(jnp.int32, (8, row_len), 1))[0][0:1]
-    lane_ids = lax.broadcasted_iota(jnp.int32, (1, LANES), 1)
-    low_half = lane_ids < HALF
     front = lane_ids % HALF < QUART
     angles = offsets.astype(f32) * freq[0:1]
     cos_tab[...] = jnp.cos(angles)
@@ -821,15 +921,13 @@
         )
 
     from_lanes(in_slots, r_in)
-    rows = 24
     w_in[dp] = jnp.concatenate(
         [r_in[j, 0:rows, :].astype(f32) for j in range(cols)], axis=0
     ).astype(bf16)
     in_spread = Spread(wire, place, w_in, tail)
     in_spread.start()
+    in_spread.start_out()
     in_spread.start_side()
-    for j in (2, 0, 1):
-        out_spread.relay(j)
     from_lanes(mlp_slots, r_mlp)
     mlp_own = [r_mlp[j].astype(f32) for j in range(cols)]
     w_gate[dp] = jnp.concatenate([part[0:rows] for part in mlp_own], axis=0).astype(bf16)
@@ -837,20 +935,27 @@
     gate_spread = Spread(wire, place, w_gate, tail)
     up_spread = Spread(wire, place, w_up, tail)
     gate_spread.start()
+    gate_spread.start_side()
+    up_spread.start_side()
+    up_spread.start()
     for j in (2, 0, 1):
-        in_spread.relay(j)
-    gate_spread.start_side()
-    up_spread.start()
-    up_spread.start_side()
+        out_spread.relay(j)
+    in_spread.relay(2)
+    in_spread.relay(0)
+    down_spread.relay(2)
+    in_spread.relay(1)
+    down_spread.relay(0)
+    down_spread.relay(1)
+    gate_spread.start_out()
+    up_spread.start_out()
+    down_spread.tail()
     gather_relay(x_slots, xs)
     out_spread.settle()
     out_lanes = gather_start(s_out.at[blk], s_out)
-    for j in (2, 0, 1):
-        down_spread.relay(j)
+    gate_spread.relay(2)
     gather_done(x_slots, xs)
     in_spread.settle()
 
-    width = xin.shape[1]
     group = 2
     chunk = group * tok
 
@@ -913,8 +1018,9 @@
     r_att[blk] = s_att[blk]
 
     gather_relay(out_lanes, s_out)
-    for j in (2, 0, 1):
-        gate_spread.relay(j)
+    gate_spread.relay(0)
+    up_spread.relay(2)
+    gate_spread.relay(1)
     gather_done(out_lanes, s_out)
     shards = planes * 2 * cols
     per_quarter = shards // cols
@@ -974,14 +1080,16 @@
     hid[...] = hidden
     hs[blk] = hidden.astype(bf16)
     hid_slots = gather_start(hs.at[blk], hs)
+    up_spread.relay(0)
+    up_spread.relay(1)
+    down_spread.tail_out()
+    for j in range(2):
+        down_spread.pass_tail(j)
+    gather_relay(hid_slots, hs)
     gate_spread.settle()
-    gather_relay(hid_slots, hs)
-    for j in (2, 0, 1):
-        up_spread.relay(j)
     gather_done(hid_slots, hs)
     up_spread.settle()
 
-    units = w_gate.shape[2]
     wide = 256
     strips = units // wide
 
@@ -997,6 +1105,7 @@
 
     lax.fori_loop(0, strips, expand, 0)
     down_spread.settle()
+    down_spread.settle_tail()
 
     def contract(step, carry):
         here = pl.ds(pl.multiple_of(step * wide, wide), wide)
@@ -1084,7 +1193,6 @@
     down_sum.first(1)
     down_sum.first(0)
     d_hidden = dres_two[...] + sum_done(dh_slots, s_dh, r_dh)
-    down_sum.second(1)
     down_sum.first(2)
     normal = norm_one[...]
     first_gain = column_sum(d_hidden * normal)
@@ -1117,10 +1225,11 @@
             b_out[s % cols, owner_dp % 2, owner_dp // 2] = jnp.concatenate(
                 [product[t * rows : (t + 1) * rows], lower], axis=0
             ).astype(bf16)
-    out_blk = to_lanes(lambda to: b_out.at[to], rb_out)
-    rb_out[blk] = b_out[blk]
-
-    down_sum.second(0)
+    out_blk = sum_start(b_out, rb_out)
+
+    sum_relay(out_blk, b_out, rb_out, tb_out)
+    down_sum.second_tail(1)
+    down_sum.second(1)
     from_lanes(da_slots, r_da)
     def attend_back(head):
         window = head // 2
@@ -1165,6 +1274,8 @@
 
     attend_back(0)
     gate_sum.first(1)
+    down_sum.second_tail(0)
+    down_sum.second(0)
     attend_back(1)
     attend_back(2)
 
@@ -1181,6 +1292,7 @@
     dj[:, 4 * LANES : 5 * LANES] = acc_v[1].astype(bf16)
 
     gate_sum.first(0)
+    down_sum.tail()
     fill_parts(in_sum.part, lambda here: xs[:, :, here].reshape(row_len, half * block), lambda: dj[...])
 
     def input_grads(step, carry):
@@ -1195,26 +1307,19 @@
     gate_sum.second(1)
     gate_sum.first(2)
     sum_relay(ig_slots, s_ig, r_ig, t_ig)
-    g_down[...] = down_sum.total()
     gate_sum.second(0)
     up_sum.first(1)
-    from_lanes(out_blk, rb_out)
-    for side_at in range(2):
-        gathered = rb_out[0, side_at].astype(f32)
-        for j in range(1, cols):
-            gathered = gathered + rb_out[j, side_at].astype(f32)
-        out_sum.part[side_at] = gathered.astype(bf16)
+    out_sum.part[...] = sum_done(out_blk, b_out, rb_out).astype(bf16)
+    in_sum.send()
     out_sum.send()
-    in_sum.send()
     up_sum.first(0)
     up_sum.second(1)
     up_sum.first(2)
     f_gate[...] = gate_sum.total()
     up_sum.second(0)
+    g_down[...] = down_sum.total()
     grad_in = dres_one[...] + sum_done(ig_slots, s_ig, r_ig)
     input_grad[...] = grad_in.astype(bf16)
-    for j in (1, 0, 2):
-        out_sum.first(j)
     in_sum.first(1)
     up_total = up_sum.total()
     gate_total = f_gate[...]
@@ -1224,12 +1329,13 @@
     gmlp_slots = to_lanes(lambda to: s_gmlp.at[to], r_gmlp)
     r_gmlp[blk] = s_gmlp[blk]
     in_sum.first(0)
-    out_sum.second(1)
-    out_sum.second(0)
     in_sum.second(1)
     in_sum.first(2)
     in_sum.second(0)
-    g_out[...] = out_sum.total()
+    for j in (1, 0, 2):
+        out_sum.first(j)
+    out_sum.second(1)
+    out_sum.second(0)
     from_lanes(gmlp_slots, r_gmlp)
     g_mlp[...] = r_gmlp[...]
     in_total = in_sum.total()
@@ -1239,9 +1345,68 @@
         ).astype(bf16)
     gin_slots = to_lanes(lambda to: s_gin.at[to], r_gin)
     r_gin[blk] = s_gin[blk]
+    g_out[...] = out_sum.total()
     from_lanes(gin_slots, r_gin)
     g_in[...] = r_gin[...]
     wire.finish()
+
+
+def unpack(
+    rows,
+    block,
+    outputs,
+    input_grad,
+    g_in,
+    g_mlp,
+    g_out,
+    g_down,
+    outputs_to,
+    input_grad_to,
+    in_to,
+    out_to,
+    gate_to,
+    up_to,
+    down_to,
+    *vectors_to,
+):
+    f32 = jnp.float32
+    cols = g_in.shape[0]
+    width = outputs.shape[1]
+    outputs_to[0] = outputs[...]
+    input_grad_to[0] = input_grad[...]
+    down_to[...] = g_down[...]
+    out_to[...] = g_out[0:rows, :]
+    for number, vector_to in enumerate(vectors_to):
+        vector_to[...] = g_out[rows + number, 0:rows]
+    low_half = lax.broadcasted_iota(jnp.int32, (1, LANES), 1) < HALF
+    joined = [g_in[j].astype(f32)[0:rows] for j in range(cols)]
+    single_at = ((3, 0), (3, 1), (4, 0))
+
+    def half(kind, number, want):
+        owner, part = number // 3, number % 3
+        window, at = (kind, part) if part < 2 else single_at[kind]
+        value = joined[owner][:, window * LANES : (window + 1) * LANES]
+        return value if at == want else pltpu.roll(value, HALF, 1)
+
+    for kind in range(3):
+        for n in range(width // LANES):
+            at = kind * width + n * LANES
+            in_to[:, at : at + LANES] = jnp.where(
+                low_half, half(kind, 2 * n, 0), half(kind, 2 * n + 1, 1)
+            )
+    lanes = lax.broadcasted_iota(jnp.int32, (1, LANES), 1)
+    mlp = [g_mlp[j].astype(f32) for j in range(cols)]
+    for first_row, target in ((0, gate_to), (rows, up_to)):
+        parts = [part[first_row : first_row + rows] for part in mlp]
+        for n in range(target.shape[1] // LANES):
+            first = n * LANES
+            result = None
+            for number in range(first // block, (first + LANES - 1) // block + 1):
+                ring_at, owner = number // cols, number % cols
+                piece = window_at(parts[owner], ring_at * block + first - number * block)
+                begin = number * block - first
+                result = piece if result is None else jnp.where(lanes < begin, result, piece)
+            target[:, first : first + LANES] = result
 
 
 def fast_shards(
@@ -1271,22 +1436,6 @@
     in_width = 5 * LANES
     bf16, f32 = jnp.bfloat16, jnp.float32
 
-    kinds = project_in.reshape(rows, 3, cols, head_width)
-    pairs, singles = kinds[..., :LANES], kinds[..., LANES:]
-    p_in = jnp.concatenate(
-        [pairs[:, 0], pairs[:, 1], pairs[:, 2], singles[:, 0], singles[:, 1], singles[:, 2]],
-        axis=-1,
-    ).transpose(1, 0, 2)
-    p_in = jnp.pad(p_in, ((0, 0), (0, 32 - rows), (0, in_width - p_in.shape[2])))
-
-    def by_owner(weight):
-        return weight.reshape(rows, ring, cols, block).transpose(2, 0, 1, 3).reshape(cols, rows, units)
-
-    p_mlp = jnp.concatenate([by_owner(gate_weight), by_owner(up_weight)], axis=1)
-    vectors = jnp.stack([first_gain, first_bias, second_gain, second_bias])
-    p_out = jnp.concatenate(
-        [project_out, jnp.pad(vectors, ((0, 4), (0, width - rows)))], axis=0
-    )
     lane_ids = np.arange(LANES) % QUART
     freq = jnp.asarray(
         np.broadcast_to(BASE ** (-2.0 * lane_ids / HALF), (8, LANES)).astype(np.float32)
@@ -1316,6 +1465,9 @@
     heads = 3
     buffers = [
         stacked,
+        scratch(cols, 32, in_width),
+        scratch(cols, 2 * rows, units),
+        scratch(8, LANES, kind=f32),
         scratch(cols, 32, in_width),
         scratch(cols, 2 * rows, units),
         scratch(cols, ring, 32, width),
@@ -1364,9 +1516,10 @@
         sums(cols * rows, in_width),
         sums(cols * rows, units),
         sums(cols * rows, units),
-        sums(block, width),
+        sums(block, width, DT),
         scratch(cols, 2, depth, 32, width),
-        scratch(cols, 2, depth, 32, width),
+        scratch(3, 2, depth, 32, width),
+        scratch(2, depth, 32, width),
         sums(32, width, 0),
         scratch(cols * rows, units, kind=f32),
         scratch(cols, 2 * rows, units),
@@ -1388,7 +1541,7 @@
             jax.ShapeDtypeStruct((32, width), f32),
             jax.ShapeDtypeStruct((block, width), f32),
         ),
-        in_specs=[pl.BlockSpec(memory_space=pltpu.SMEM)] + [vmem] * 7,
+        in_specs=[pl.BlockSpec(memory_space=pltpu.SMEM)] + [vmem] * 12,
         out_specs=(vmem,) * 6,
         scratch_shapes=buffers,
         compiler_params=pltpu.CompilerParams(
@@ -1400,36 +1553,42 @@
             transcendentals=3 * row_len * row_len,
         ),
         name="layer",
-    )(doc_lengths, freq, inputs[0], cotangent[0], p_in, p_mlp, p_out, down_weight)
-
-    wide_in = g_in[:, :rows].astype(f32).transpose(1, 0, 2)
-    kind_pairs = wide_in[..., : 3 * LANES].reshape(rows, cols, 3, LANES)
-    kind_singles = wide_in[..., 3 * LANES : 3 * LANES + 3 * HALF].reshape(rows, cols, 3, HALF)
-    in_grad = jnp.concatenate([kind_pairs, kind_singles], axis=-1)
-    in_grad = in_grad.transpose(0, 2, 1, 3).reshape(rows, 3 * width)
-
-    def by_column(part):
-        return (
-            part.reshape(cols, rows, ring, block)
-            .transpose(1, 2, 0, 3)
-            .reshape(rows, ff)
-            .astype(f32)
-        )
-
-    small = g_out[rows : rows + 4, :rows]
-    return (
-        outputs[None],
-        input_grad[None],
-        in_grad,
-        g_out[:rows],
-        by_column(g_mlp[:, :rows]),
-        by_column(g_mlp[:, rows:]),
-        g_down,
-        small[0],
-        small[1],
-        small[2],
-        small[3],
-    )
+    )(
+        doc_lengths,
+        freq,
+        inputs[0],
+        cotangent[0],
+        project_in,
+        gate_weight,
+        up_weight,
+        project_out,
+        down_weight,
+        first_gain[None],
+        first_bias[None],
+        second_gain[None],
+        second_bias[None],
+    )
+
+    vector = jax.ShapeDtypeStruct((rows,), f32)
+    return pl.pallas_call(
+        functools.partial(unpack, rows, block),
+        out_shape=(
+            jax.ShapeDtypeStruct((1, tok, width), bf16),
+            jax.ShapeDtypeStruct((1, tok, width), bf16),
+            jax.ShapeDtypeStruct((rows, 3 * width), f32),
+            jax.ShapeDtypeStruct((rows, width), f32),
+            jax.ShapeDtypeStruct((rows, ff), f32),
+            jax.ShapeDtypeStruct((rows, ff), f32),
+            jax.ShapeDtypeStruct((block, width), f32),
+            vector,
+            vector,
+            vector,
+            vector,
+        ),
+        in_specs=[vmem] * 6,
+        out_specs=(vmem,) * 11,
+        name="unpack",
+    )(outputs, input_grad, g_in, g_mlp, g_out, g_down)
 
 
 def pick(sizes):

time: 168 us -> 140 us (0.83)
  local copies, waits for them, and re-layouts: 12.8 us -> 0 us
  Pallas kernels: 151 us -> 139 us
  other arithmetic: 3.03 us -> 0 us
    pallas_call x1, Pallas kernels: 151 us -> 136 us  [fast_shards(): pl.pallas_call(functools.partial(fused, depth), out_shape=(jax.ShapeDtype...]
    unnamed x21 -> x0, local copies, waits for them, and re-layouts: 3.86 us -> none
    convert_element_type x6 -> x0, local copies, waits for them, and re-layouts: 3.03 us -> none  [by_column(): return part.reshape(cols, rows, ring, block).transpose(1, 2, 0, 3).reshap...]
    pallas_call x0 -> x1, Pallas kernels: none -> 2.7 us  [fast_shards(): pl.pallas_call(functools.partial(unpack, rows, block), out_shape=(jax.Sha...]
    concatenate x2 -> x0, other arithmetic: 2.13 us -> none  [the longest x1 1.39 us: fast_shards(): jnp.concatenate([project_out, jnp.pad(vectors, ((0, 4), (0, width - rows)...]
    reshape x10 -> x0, local copies, waits for them, and re-layouts: 1.98 us -> none  [the longest x1 0.88 us: fast_shards(): in_grad = in_grad.transpose(0, 2, 1, 3).reshape(rows, 3 * width)]
where the time goes in v3:
time: 140 us
  Pallas kernels  139 us (99%)
    pallas_call x1, Pallas kernels, fast_shards(): pl.pallas_call(functools.partial(fused, depth), out_shape=(jax.ShapeDtype...  136 us

profile of v3, /device:TPU:0, one launch (start us, length us, event | category | flops | bytes accessed | tf_op | source)
XLA Modules:
  0.0 139.6 jit_solution(8686426548564178791)
XLA Ops:
  0.6 136.3 %layer.1 = (bf16[128,768]{1,0:T(8,128)(2,1)}, bf16[128,768]{1,0:T(8,128)(2,1)}, bf16[4,32,640]{2,1,0:T(8,128)(2,1)}, bf16[4,48,768]{2,1,0:T(8,128)(2,1)}, f32[32,768]{1,0:T(8,128)}, /*index=5*/f32[96,768]{1,0:T(8,128)}) custom-call(s32[1,8]{1,0:T(1,128)} %lens.1, f32[8,128]{1,0:T(8,128)} %constant.2.clone.freq, bf16[128,768]{1,0:T(8,128)(2,1)} %bitcast.6, ...), custom_call_target="tpu_custom_call" | custom-call | flops 7247757312 | bytes 8388608 | tf_op jit(solution)/shard_map/layer/pallas_call | solution.py:1534
  136.9 2.7 %unpack.1 = (bf16[1,128,768]{2,1,0:T(8,128)(2,1)}, bf16[1,128,768]{2,1,0:T(8,128)(2,1)}, f32[24,2304]{1,0:T(8,128)}, f32[24,768]{1,0:T(8,128)}, f32[24,3072]{1,0...) custom-call(bf16[128,768]{1,0:T(8,128)(2,1)} %get-tuple-element.17.o, ...), custom_call_target="tpu_custom_call" | custom-call | tf_op jit(solution)/shard_map/unpack/pallas_call | solution.py:1573

commit v4 on v3

--- a/solution.py
+++ b/solution.py
@@ -381,7 +381,8 @@
 LANES = 128
 HALF = 64
 QUART = 32
-DT = 48
+DTF = 48
+DTB = 64
 
 
 def mm(left, right):
@@ -539,14 +540,30 @@
     def tail_out(self):
         self.outward(self.pair(self.place.z), self.t_slots)
 
-    def relay(self, j):
+    def relay(self, j, inner=None):
         p, wire = self.place, self.wire
-        plane = p.order[j]
-        block = self.block(plane, p.x)
-        wire.arrive(self.z_slots[j], block, p.side)
-        if j < 2:
-            wire.push(block, block, p.at(p.partner), self.z_slots[j], inner=True)
-        wire.push(block, block, p.side, self.x_slots[j])
+        block = self.block(p.order[j], p.x)
+        onward = wire.copy(block, block, p.side, self.x_slots[j])
+        wire.sent[inner].append(onward)
+        outward = None
+        if j < 2 and inner is not False:
+            outward = wire.copy(block, block, p.at(p.partner), self.z_slots[j])
+            wire.sent[True].append(outward)
+
+        def run():
+            wire.arrive(self.z_slots[j], block, p.side)
+            if outward is not None:
+                if inner:
+                    outward.start()
+                else:
+                    pl.when(wire.is_inner)(outward.start)
+            onward.start()
+
+        if inner is None:
+            run()
+        else:
+            pl.when(wire.is_inner == inner)(run)
+
     def pass_tail(self, j):
         p, wire = self.place, self.wire
         pair = self.pair(p.order[j])
@@ -585,17 +602,21 @@
     def pair(self, plane):
         return self.part.at[:, plane, self.main : self.height]
 
-    def send(self):
+    def send_side(self, j):
+        p = self.place
+        plane = p.order[j]
+        self.wire.push(
+            self.part.at[1 - p.x, plane, 0 : self.main],
+            self.inbox.at[plane],
+            p.side,
+            self.x_slots[j],
+        )
+
+    def send(self, order=(1, 0, 2, 3)):
         p, wire = self.place, self.wire
         self.x_slots = [wire.slot() for _ in range(4)]
-        for j in (1, 0, 2, 3):
-            plane = p.order[j]
-            wire.push(
-                self.part.at[1 - p.x, plane, 0 : self.main],
-                self.inbox.at[plane],
-                p.side,
-                self.x_slots[j],
-            )
+        for j in order:
+            self.send_side(j)
         self.z_slots = [wire.slot() for _ in range(4)]
         if self.split:
             self.t_slots = [wire.slot() for _ in range(4)]
@@ -828,36 +849,40 @@
         for k, slot in zip(lanes, slots):
             wire.arrive(slot, target.at[lane_from(k)], lane(k))
 
-    def gather_start(source, target):
+    every = pl.ds(0, tok)
+
+    def gather_start(own, target, cut=every):
         return [
-            wire.push(source, target.at[blk], across),
-            wire.push(source, target.at[blk], near),
+            wire.push(own.at[cut], target.at[blk, cut], across),
+            wire.push(own.at[cut], target.at[blk, cut], near),
         ]
 
-    def gather_relay(slots, target):
-        wire.arrive(slots[0], target.at[across_at], across)
-        slots.append(wire.push(target.at[across_at], target.at[across_at], near))
-
-    def gather_done(slots, target):
-        wire.arrive(slots[1], target.at[near_at], near)
-        wire.arrive(slots[2], target.at[corner_at], near)
-
-    def sum_start(part, inbox):
+    def gather_relay(slots, target, cut=every):
+        came = target.at[across_at, cut]
+        wire.arrive(slots[0], came, across)
+        slots.append(wire.push(came, came, near))
+
+    def gather_done(slots, target, cut=every):
+        wire.arrive(slots[1], target.at[near_at, cut], near)
+        wire.arrive(slots[2], target.at[corner_at, cut], near)
+
+    def sum_start(part, inbox, cut=every):
         return [
-            wire.push(part.at[corner_at], inbox.at[0], near),
-            wire.push(part.at[near_at], inbox.at[1], near),
+            wire.push(part.at[corner_at, cut], inbox.at[0, cut], near),
+            wire.push(part.at[near_at, cut], inbox.at[1, cut], near),
         ]
 
-    def sum_relay(slots, part, inbox, staged):
-        wire.arrive(slots[0], inbox.at[0], near)
-        staged[...] = (part[across_at].astype(f32) + inbox[0].astype(f32)).astype(bf16)
-        slots.append(wire.push(staged, inbox.at[2], across))
-
-    def sum_done(slots, part, inbox):
-        wire.arrive(slots[1], inbox.at[1], near)
-        total = part[blk].astype(f32) + inbox[1].astype(f32)
-        wire.arrive(slots[2], inbox.at[2], across)
-        return total + inbox[2].astype(f32)
+    def sum_relay(slots, part, inbox, staged, cut=every):
+        wire.arrive(slots[0], inbox.at[0, cut], near)
+        both = part[across_at, cut].astype(f32) + inbox[0, cut].astype(f32)
+        staged[cut] = both.astype(bf16)
+        slots.append(wire.push(staged.at[cut], inbox.at[2, cut], across))
+
+    def sum_done(slots, part, inbox, cut=every):
+        wire.arrive(slots[1], inbox.at[1, cut], near)
+        total = part[blk, cut].astype(f32) + inbox[1, cut].astype(f32)
+        wire.arrive(slots[2], inbox.at[2, cut], across)
+        return total + inbox[2, cut].astype(f32)
 
     in_slots = to_lanes(lambda to: p_in.at[to], r_in)
     w_down[dp] = p_down[...]
@@ -866,7 +891,7 @@
     out_spread.start()
     out_spread.start_out()
     out_spread.start_side()
-    down_spread = Spread(wire, place, w_down, DT)
+    down_spread = Spread(wire, place, w_down, DTF)
     down_spread.start()
     down_spread.start_out()
     down_spread.start_side()
@@ -936,7 +961,6 @@
     up_spread = Spread(wire, place, w_up, tail)
     gate_spread.start()
     gate_spread.start_side()
-    up_spread.start_side()
     up_spread.start()
     for j in (2, 0, 1):
         out_spread.relay(j)
@@ -944,14 +968,16 @@
     in_spread.relay(0)
     down_spread.relay(2)
     in_spread.relay(1)
-    down_spread.relay(0)
-    down_spread.relay(1)
+    up_spread.start_side()
     gate_spread.start_out()
     up_spread.start_out()
     down_spread.tail()
+    gate_spread.relay(0, inner=True)
+    gate_spread.relay(1, inner=True)
     gather_relay(x_slots, xs)
     out_spread.settle()
-    out_lanes = gather_start(s_out.at[blk], s_out)
+    shards_here = pl.ds(0, planes * 2)
+    out_lanes = gather_start(s_out.at[blk], s_out, shards_here)
     gate_spread.relay(2)
     gather_done(x_slots, xs)
     in_spread.settle()
@@ -1005,8 +1031,10 @@
 
         lax.fori_loop(0, row_len // chunk, step_fn, 0)
 
+    up_spread.relay(0, inner=True)
     attend(0)
     attend(1)
+    up_spread.relay(1, inner=True)
     attend(2)
     last_segment = lens.shape[1] - 1
     for j in range(cols):
@@ -1017,11 +1045,16 @@
     att_slots = to_lanes(lambda to: s_att.at[to], r_att)
     r_att[blk] = s_att[blk]
 
-    gather_relay(out_lanes, s_out)
-    gate_spread.relay(0)
+    down_spread.tail_out()
     up_spread.relay(2)
-    gate_spread.relay(1)
-    gather_done(out_lanes, s_out)
+    gather_relay(out_lanes, s_out, shards_here)
+    gate_spread.relay(0, inner=False)
+    gate_spread.relay(1, inner=False)
+    down_spread.relay(0, inner=True)
+    down_spread.relay(1, inner=True)
+    for j in range(2):
+        down_spread.pass_tail(j)
+    gather_done(out_lanes, s_out, shards_here)
     shards = planes * 2 * cols
     per_quarter = shards // cols
     head_rows = per_quarter * rows
@@ -1080,30 +1113,38 @@
     hid[...] = hidden
     hs[blk] = hidden.astype(bf16)
     hid_slots = gather_start(hs.at[blk], hs)
-    up_spread.relay(0)
-    up_spread.relay(1)
-    down_spread.tail_out()
-    for j in range(2):
-        down_spread.pass_tail(j)
+    up_spread.relay(0, inner=False)
+    up_spread.relay(1, inner=False)
+    down_spread.relay(0, inner=False)
+    down_spread.relay(1, inner=False)
     gather_relay(hid_slots, hs)
     gate_spread.settle()
     gather_done(hid_slots, hs)
-    up_spread.settle()
 
     wide = 256
     strips = units // wide
 
-    def expand(step, carry):
-        here = pl.ds(pl.multiple_of(step * wide, wide), wide)
+    def each_strip(body):
+        def step_fn(step, carry):
+            body(pl.ds(pl.multiple_of(step * wide, wide), wide))
+            return carry
+
+        lax.fori_loop(0, strips, step_fn, 0)
+
+    def expand_gate(here):
         tokens = hs[...].reshape(row_len, width)
-        gate = mm(tokens, w_gate[:, :, here].reshape(width, wide))
+        gate_pre[:, here] = mm(tokens, w_gate[:, :, here].reshape(width, wide))
+
+    def expand_up(here):
+        tokens = hs[...].reshape(row_len, width)
         up = mm(tokens, w_up[:, :, here].reshape(width, wide))
-        gate_pre[:, here] = gate
+        gate = gate_pre[:, here]
         up_pre[:, here] = up
         act[:, here] = (gate / (1.0 + jnp.exp(-gate)) * up).astype(bf16)
-        return carry
-
-    lax.fori_loop(0, strips, expand, 0)
+
+    each_strip(expand_gate)
+    up_spread.settle()
+    each_strip(expand_up)
     down_spread.settle()
     down_spread.settle_tail()
 
@@ -1114,20 +1155,26 @@
         return carry
 
     lax.fori_loop(0, width // wide, contract, 0)
-    mix_slots = sum_start(s_mix, r_mix)
-    sum_relay(mix_slots, s_mix, r_mix, t_mix)
-    mlp_out = sum_done(mix_slots, s_mix, r_mix)
-    normal, spread_two = normalize(hid[...] + mlp_out)
-    outputs[...] = (normal * gain_two + bias_two).astype(bf16)
-    grad = cot[...].astype(f32)
-    second_gain = column_sum(grad * normal)
-    second_bias = column_sum(grad)
-    d_two = normalize_back(grad, normal, spread_two, gain_two)
-    dres_two[...] = d_two
-    dms[blk] = d_two.astype(bf16)
-    dm_slots = gather_start(dms.at[blk], dms)
-    gather_relay(dm_slots, dms)
-    gather_done(dm_slots, dms)
+    halves = [pl.ds(0, tok // 2), pl.ds(tok // 2, tok // 2)]
+    mix_slots = [sum_start(s_mix, r_mix, cut) for cut in halves]
+    for slots, cut in zip(mix_slots, halves):
+        sum_relay(slots, s_mix, r_mix, t_mix, cut)
+    second_gain, second_bias, dm_slots = 0.0, 0.0, []
+    for slots, cut in zip(mix_slots, halves):
+        mlp_out = sum_done(slots, s_mix, r_mix, cut)
+        normal, spread_two = normalize(hid[cut, :] + mlp_out)
+        outputs[cut, :] = (normal * gain_two + bias_two).astype(bf16)
+        grad = cot[cut, :].astype(f32)
+        second_gain = second_gain + column_sum(grad * normal)
+        second_bias = second_bias + column_sum(grad)
+        d_two = normalize_back(grad, normal, spread_two, gain_two)
+        dres_two[cut, :] = d_two
+        dms[blk, cut] = d_two.astype(bf16)
+        dm_slots.append(gather_start(dms.at[blk], dms, cut))
+    for slots, cut in zip(dm_slots, halves):
+        gather_relay(slots, dms, cut)
+    for slots, cut in zip(dm_slots, halves):
+        gather_done(slots, dms, cut)
 
     down_sum = Collect(wire, place, sum_down)
     gate_sum = Collect(wire, place, sum_gate)
@@ -1170,6 +1217,11 @@
     lax.fori_loop(0, planes * 2 // half, active_grads, 0)
     block = w_gate.shape[1]
 
+    def hidden_rows(here):
+        return hs[:, :, here].reshape(row_len, half * block)
+
+    fill_parts(gate_sum.part, hidden_rows, lambda: dgate[...])
+    gate_sum.send()
     def hidden_grads(step, carry):
         here = pl.ds(pl.multiple_of(step * half * block, LANES), half * block)
         those = pl.ds(step * half, half)
@@ -1182,11 +1234,6 @@
     lax.fori_loop(0, planes * 2 // half, hidden_grads, 0)
     dh_slots = sum_start(s_dh, r_dh)
 
-    def hidden_rows(here):
-        return hs[:, :, here].reshape(row_len, half * block)
-
-    fill_parts(gate_sum.part, hidden_rows, lambda: dgate[...])
-    gate_sum.send()
     sum_relay(dh_slots, s_dh, r_dh, t_dh)
     fill_parts(up_sum.part, hidden_rows, lambda: dup[...])
     up_sum.send()
@@ -1225,9 +1272,10 @@
             b_out[s % cols, owner_dp % 2, owner_dp // 2] = jnp.concatenate(
                 [product[t * rows : (t + 1) * rows], lower], axis=0
             ).astype(bf16)
-    out_blk = sum_start(b_out, rb_out)
-
-    sum_relay(out_blk, b_out, rb_out, tb_out)
+    both_sides = pl.ds(0, 2)
+    out_blk = sum_start(b_out, rb_out, both_sides)
+
+    sum_relay(out_blk, b_out, rb_out, tb_out, both_sides)
     down_sum.second_tail(1)
     down_sum.second(1)
     from_lanes(da_slots, r_da)
@@ -1309,9 +1357,11 @@
     sum_relay(ig_slots, s_ig, r_ig, t_ig)
     gate_sum.second(0)
     up_sum.first(1)
-    out_sum.part[...] = sum_done(out_blk, b_out, rb_out).astype(bf16)
-    in_sum.send()
+    out_sum.part[...] = sum_done(out_blk, b_out, rb_out, both_sides).astype(bf16)
+    in_sum.send((1, 0))
     out_sum.send()
+    in_sum.send_side(2)
+    in_sum.send_side(3)
     up_sum.first(0)
     up_sum.second(1)
     up_sum.first(2)
@@ -1321,6 +1371,7 @@
     grad_in = dres_one[...] + sum_done(ig_slots, s_ig, r_ig)
     input_grad[...] = grad_in.astype(bf16)
     in_sum.first(1)
+    in_sum.first(0)
     up_total = up_sum.total()
     gate_total = f_gate[...]
     for j in range(cols):
@@ -1328,12 +1379,11 @@
         s_gmlp[j] = jnp.concatenate([gate_total[here], up_total[here]], axis=0).astype(bf16)
     gmlp_slots = to_lanes(lambda to: s_gmlp.at[to], r_gmlp)
     r_gmlp[blk] = s_gmlp[blk]
-    in_sum.first(0)
     in_sum.second(1)
-    in_sum.first(2)
-    in_sum.second(0)
     for j in (1, 0, 2):
         out_sum.first(j)
+    in_sum.second(0)
+    in_sum.first(2)
     out_sum.second(1)
     out_sum.second(0)
     from_lanes(gmlp_slots, r_gmlp)
@@ -1516,7 +1566,7 @@
         sums(cols * rows, in_width),
         sums(cols * rows, units),
         sums(cols * rows, units),
-        sums(block, width, DT),
+        sums(block, width, DTB),
         scratch(cols, 2, depth, 32, width),
         scratch(3, 2, depth, 32, width),
         scratch(2, depth, 32, width),

time: 140 us -> 134 us (0.957)
  Pallas kernels: 139 us -> 133 us
    pallas_call x1, Pallas kernels: 136 us -> 131 us  [fast_shards(): pl.pallas_call(functools.partial(fused, depth), out_shape=(jax.ShapeDtype...]
where the time goes in v4:
time: 134 us
  Pallas kernels  133 us (99%)
    pallas_call x1, Pallas kernels, fast_shards(): pl.pallas_call(functools.partial(fused, depth), out_shape=(jax.ShapeDtype...  131 us
    pallas_call x1, Pallas kernels, fast_shards(): pl.pallas_call(functools.partial(unpack, rows, block), out_shape=(jax.Sha...  2.7 us

profile of v4, /device:TPU:0, one launch (start us, length us, event | category | flops | bytes accessed | tf_op | source)
XLA Modules:
  0.0 134.1 jit_solution(14475515523506394169)
XLA Ops:
  0.6 130.8 %layer.1 = (bf16[128,768]{1,0:T(8,128)(2,1)}, bf16[128,768]{1,0:T(8,128)(2,1)}, bf16[4,32,640]{2,1,0:T(8,128)(2,1)}, bf16[4,48,768]{2,1,0:T(8,128)(2,1)}, f32[32,768]{1,0:T(8,128)}, /*index=5*/f32[96,768]{1,0:T(8,128)}) custom-call(s32[1,8]{1,0:T(1,128)} %lens.1, f32[8,128]{1,0:T(8,128)} %constant.2.clone.freq, bf16[128,768]{1,0:T(8,128)(2,1)} %bitcast.6, ...), custom_call_target="tpu_custom_call" | custom-call | flops 7247757312 | bytes 8388608 | tf_op jit(solution)/shard_map/layer/pallas_call | solution.py:1584
  131.4 2.7 %unpack.1 = (bf16[1,128,768]{2,1,0:T(8,128)(2,1)}, bf16[1,128,768]{2,1,0:T(8,128)(2,1)}, f32[24,2304]{1,0:T(8,128)}, f32[24,768]{1,0:T(8,128)}, f32[24,3072]{1,0...) custom-call(bf16[128,768]{1,0:T(8,128)(2,1)} %get-tuple-element.17.o, ...), custom_call_target="tpu_custom_call" | custom-call | tf_op jit(solution)/shard_map/unpack/pallas_call | solution.py:1623

commit v5 on v4

--- a/solution.py
+++ b/solution.py
@@ -809,16 +809,30 @@
     lanes = range(1, cols)
     wire = Wire(send_sem, recv_sem, place.inner == 1)
     barrier = pltpu.get_barrier_semaphore()
-    peers = [place.side] + [place.at(plane) for plane in place.order[:3]]
+    peers = [place.side, place.at(place.partner), place.at(place.other)]
     peers = peers + [lane(k) for k in lanes]
     for peer in peers:
         pl.semaphore_signal(barrier, inc=1, device_id=peer, device_id_type=MESH_IDS)
+    far = place.at(place.outer)
+
+    @pl.when(place.inner == 1)
+    def _():
+        pl.semaphore_signal(barrier, inc=1, device_id=far, device_id_type=MESH_IDS)
+
 
     rows = 24
     width = xin.shape[1]
     lane_ids = lax.broadcasted_iota(jnp.int32, (1, LANES), 1)
     low_half = lane_ids < HALF
     head_width = width // cols
+    vectors_tab[...] = jnp.zeros_like(vectors_tab)
+    for number, vector in enumerate((gain_a, bias_a, gain_b, bias_b)):
+        vectors_tab[number : number + 1, 0:rows] = vector[...].astype(f32)
+    free_lane = lax.broadcasted_iota(jnp.int32, (8, LANES), 0) + HALF
+    to_lane = jnp.where(
+        free_lane == lax.broadcasted_iota(jnp.int32, (8, LANES), 1), 1.0, 0.0
+    ).astype(bf16)
+    vector_columns = tm(vectors_tab[...].astype(bf16), to_lane)[0:rows]
     joined_rows = in_rows[...].astype(f32)
     for j in range(cols):
         starts = [kind * width + j * head_width for kind in range(3)]
@@ -830,17 +844,16 @@
                 window_at(joined_rows, starts[1] + LANES - HALF),
             )
         )
-        windows.append(jnp.where(low_half, window_at(joined_rows, starts[2] + LANES), 0.0))
+        windows.append(
+            jnp.where(low_half, window_at(joined_rows, starts[2] + LANES), vector_columns)
+        )
         packed = jnp.concatenate(windows, axis=1)
         p_in[j] = jnp.concatenate(
             [packed, jnp.zeros((8, packed.shape[1]), f32)], axis=0
         ).astype(bf16)
-    vectors_tab[...] = jnp.zeros_like(vectors_tab)
-    for number, vector in enumerate((gain_a, bias_a, gain_b, bias_b)):
-        vectors_tab[number : number + 1, 0:rows] = vector[...].astype(f32)
-    lower = jnp.concatenate([vectors_tab[...], jnp.zeros((8, width - LANES), f32)], axis=1)
-    s_out[blk, dp] = jnp.concatenate([out_rows[...].astype(f32), lower], axis=0).astype(bf16)
-    pl.semaphore_wait(barrier, len(peers))
+    halved = [out_rows[:, n * width // 2 : (n + 1) * width // 2].astype(f32) for n in range(2)]
+    s_out[blk, dp] = jnp.concatenate(halved, axis=0).astype(bf16)
+    pl.semaphore_wait(barrier, len(peers) + place.inner)
 
     def to_lanes(source_of, target):
         return [wire.push(source_of((blk + k) % cols), target.at[blk], lane(k)) for k in lanes]
@@ -979,6 +992,7 @@
     shards_here = pl.ds(0, planes * 2)
     out_lanes = gather_start(s_out.at[blk], s_out, shards_here)
     gate_spread.relay(2)
+    up_spread.relay(2)
     gather_done(x_slots, xs)
     in_spread.settle()
 
@@ -1046,7 +1060,6 @@
     r_att[blk] = s_att[blk]
 
     down_spread.tail_out()
-    up_spread.relay(2)
     gather_relay(out_lanes, s_out, shards_here)
     gate_spread.relay(0, inner=False)
     gate_spread.relay(1, inner=False)
@@ -1059,32 +1072,22 @@
     per_quarter = shards // cols
     head_rows = per_quarter * rows
     for quarter in range(cols):
+        slots = [
+            s_out[s % cols, s // cols].astype(f32)
+            for s in range(quarter * per_quarter, (quarter + 1) * per_quarter)
+        ]
         w_out[quarter, 0:head_rows, :] = jnp.concatenate(
             [
-                s_out[s % cols, s // cols, 0:rows, :].astype(f32)
-                for s in range(quarter * per_quarter, (quarter + 1) * per_quarter)
+                jnp.concatenate([slot[n * rows : (n + 1) * rows] for slot in slots], axis=0)
+                for n in range(2)
             ],
-            axis=0,
+            axis=1,
         ).astype(bf16)
         w_out[quarter, head_rows:, :] = jnp.zeros(
             (w_out.shape[1] - head_rows, width), bf16
         )
-    column = lax.broadcasted_iota(jnp.int32, (LANES, width), 1).astype(f32)
-    owner = jnp.floor((column + 0.5) * (1.0 / rows))
-    inside = column - owner * rows
-    unit = (
-        inside == lax.broadcasted_iota(jnp.int32, (LANES, width), 0).astype(f32)
-    ).astype(bf16)
-    tails = jnp.concatenate(
-        [
-            s_out[s % cols, s // cols, rows : rows + 8, 0:LANES].astype(f32)
-            for s in range(shards)
-        ],
-        axis=0,
-    ).astype(bf16)
-    shard_ids = lax.broadcasted_iota(jnp.int32, (shards, 8, width), 0).astype(f32)
-    shard_hit = (shard_ids == owner[0:1].reshape(1, 1, width)).astype(f32)
-    params[...] = jnp.sum(mm(tails, unit).reshape(shards, 8, width) * shard_hit, axis=0)
+    last_window = w_in[:, :, 4 * LANES : 5 * LANES].reshape(width, LANES)
+    params[...] = mt(to_lane, last_window)
     gain_one, bias_one = params[0:1, :], params[1:2, :]
     gain_two, bias_two = params[2:3, :], params[3:4, :]
 
@@ -1155,7 +1158,8 @@
         return carry
 
     lax.fori_loop(0, width // wide, contract, 0)
-    halves = [pl.ds(0, tok // 2), pl.ds(tok // 2, tok // 2)]
+    pieces = 4
+    halves = [pl.ds(n * tok // pieces, tok // pieces) for n in range(pieces)]
     mix_slots = [sum_start(s_mix, r_mix, cut) for cut in halves]
     for slots, cut in zip(mix_slots, halves):
         sum_relay(slots, s_mix, r_mix, t_mix, cut)
@@ -1183,12 +1187,12 @@
     out_sum = Collect(wire, place, sum_out)
     half = 4
 
-    def fill_parts(part, left_of, right):
+    def fill_parts(part, left_of, right, more=lambda product, here: product):
         height = part.shape[2]
 
         def step_fn(step, carry):
             here = pl.ds(pl.multiple_of(step * half * height, LANES), half * height)
-            product = tm(left_of(here), right())
+            product = more(tm(left_of(here), right()), here)
             for j in range(half):
                 part[j % 2, step * (half // 2) + j // 2] = product[
                     j * height : (j + 1) * height
@@ -1255,29 +1259,27 @@
     da_slots = to_lanes(lambda to: s_da.at[to], r_da)
     r_da[blk] = s_da[blk]
 
-    vectors = jnp.concatenate(
+    params[...] = jnp.concatenate(
         [first_gain, first_bias, second_gain, second_bias, jnp.zeros((4, width), f32)], axis=0
-    )
-    tails = mt(
-        (shard_hit * vectors.reshape(1, 8, width)).reshape(shards * 8, width).astype(bf16), unit
     )
     for quarter in range(cols):
         product = tm(r_att[quarter], d_branch)
         for t in range(per_quarter):
             s = quarter * per_quarter + t
             owner_dp = s // cols
-            lower = jnp.concatenate(
-                [tails[s * 8 : s * 8 + 8], jnp.zeros((8, width - LANES), f32)], axis=1
-            )
+            mine_rows = product[t * rows : (t + 1) * rows]
+            halved = [mine_rows[:, n * width // 2 : (n + 1) * width // 2] for n in range(2)]
             b_out[s % cols, owner_dp % 2, owner_dp // 2] = jnp.concatenate(
-                [product[t * rows : (t + 1) * rows], lower], axis=0
+                halved, axis=0
             ).astype(bf16)
     both_sides = pl.ds(0, 2)
     out_blk = sum_start(b_out, rb_out, both_sides)
 
+    gate_sum.first(1)
     sum_relay(out_blk, b_out, rb_out, tb_out, both_sides)
     down_sum.second_tail(1)
     down_sum.second(1)
+    gate_sum.first(0)
     from_lanes(da_slots, r_da)
     def attend_back(head):
         window = head // 2
@@ -1321,7 +1323,7 @@
         lax.fori_loop(0, row_len // chunk, step_fn, 0)
 
     attend_back(0)
-    gate_sum.first(1)
+    gate_sum.first(2)
     down_sum.second_tail(0)
     down_sum.second(0)
     attend_back(1)
@@ -1339,9 +1341,19 @@
     dj[:, 3 * LANES : 4 * LANES] = rotate_back(acc_q[1] + pltpu.roll(acc_k[1], HALF, 1))
     dj[:, 4 * LANES : 5 * LANES] = acc_v[1].astype(bf16)
 
-    gate_sum.first(0)
-    down_sum.tail()
-    fill_parts(in_sum.part, lambda here: xs[:, :, here].reshape(row_len, half * block), lambda: dj[...])
+    up_sum.first(1)
+
+    def with_vectors(product, here):
+        columns = tm(params[:, here].astype(bf16), to_lane)
+        last = product[:, 4 * LANES :] + columns
+        return jnp.concatenate([product[:, : 4 * LANES], last], axis=1)
+
+    fill_parts(
+        in_sum.part,
+        lambda here: xs[:, :, here].reshape(row_len, half * block),
+        lambda: dj[...],
+        with_vectors,
+    )
 
     def input_grads(step, carry):
         here = pl.ds(pl.multiple_of(step * half * block, LANES), half * block)
@@ -1353,21 +1365,19 @@
     ig_slots = sum_start(s_ig, r_ig)
 
     gate_sum.second(1)
-    gate_sum.first(2)
     sum_relay(ig_slots, s_ig, r_ig, t_ig)
+    up_sum.first(0)
     gate_sum.second(0)
-    up_sum.first(1)
     out_sum.part[...] = sum_done(out_blk, b_out, rb_out, both_sides).astype(bf16)
-    in_sum.send((1, 0))
-    out_sum.send()
-    in_sum.send_side(2)
+    in_sum.send((1, 0, 2))
+    out_sum.send((1, 0, 2))
     in_sum.send_side(3)
-    up_sum.first(0)
+    out_sum.send_side(3)
+    down_sum.tail()
     up_sum.second(1)
     up_sum.first(2)
     f_gate[...] = gate_sum.total()
     up_sum.second(0)
-    g_down[...] = down_sum.total()
     grad_in = dres_one[...] + sum_done(ig_slots, s_ig, r_ig)
     input_grad[...] = grad_in.astype(bf16)
     in_sum.first(1)
@@ -1380,10 +1390,10 @@
     gmlp_slots = to_lanes(lambda to: s_gmlp.at[to], r_gmlp)
     r_gmlp[blk] = s_gmlp[blk]
     in_sum.second(1)
+    in_sum.first(2)
+    in_sum.second(0)
     for j in (1, 0, 2):
         out_sum.first(j)
-    in_sum.second(0)
-    in_sum.first(2)
     out_sum.second(1)
     out_sum.second(0)
     from_lanes(gmlp_slots, r_gmlp)
@@ -1396,6 +1406,7 @@
     gin_slots = to_lanes(lambda to: s_gin.at[to], r_gin)
     r_gin[blk] = s_gin[blk]
     g_out[...] = out_sum.total()
+    g_down[...] = down_sum.total()
     from_lanes(gin_slots, r_gin)
     g_in[...] = r_gin[...]
     wire.finish()
@@ -1425,11 +1436,16 @@
     outputs_to[0] = outputs[...]
     input_grad_to[0] = input_grad[...]
     down_to[...] = g_down[...]
-    out_to[...] = g_out[0:rows, :]
-    for number, vector_to in enumerate(vectors_to):
-        vector_to[...] = g_out[rows + number, 0:rows]
+    for n in range(2):
+        out_to[:, n * width // 2 : (n + 1) * width // 2] = g_out[n * rows : (n + 1) * rows, :]
     low_half = lax.broadcasted_iota(jnp.int32, (1, LANES), 1) < HALF
     joined = [g_in[j].astype(f32)[0:rows] for j in range(cols)]
+    vectors = joined[0][:, 4 * LANES :]
+    for j in range(1, cols):
+        vectors = vectors + joined[j][:, 4 * LANES :]
+    vectors = jnp.concatenate([vectors, jnp.zeros((LANES - rows, LANES), f32)], axis=0).T
+    for number, vector_to in enumerate(vectors_to):
+        vector_to[...] = vectors[HALF + number, 0:rows]
     single_at = ((3, 0), (3, 1), (4, 0))
 
     def half(kind, number, want):
@@ -1520,7 +1536,7 @@
         scratch(8, LANES, kind=f32),
         scratch(cols, 32, in_width),
         scratch(cols, 2 * rows, units),
-        scratch(cols, ring, 32, width),
+        scratch(cols, ring, 2 * rows, width // 2),
         scratch(ring, cols * rows, in_width),
         scratch(ring, cols * rows, units),
         scratch(ring, cols * rows, units),
@@ -1567,10 +1583,10 @@
         sums(cols * rows, units),
         sums(cols * rows, units),
         sums(block, width, DTB),
-        scratch(cols, 2, depth, 32, width),
-        scratch(3, 2, depth, 32, width),
-        scratch(2, depth, 32, width),
-        sums(32, width, 0),
+        scratch(cols, 2, depth, 2 * rows, width // 2),
+        scratch(3, 2, depth, 2 * rows, width // 2),
+        scratch(2, depth, 2 * rows, width // 2),
+        sums(2 * rows, width // 2, 0),
         scratch(cols * rows, units, kind=f32),
         scratch(cols, 2 * rows, units),
         scratch(cols, 2 * rows, units),
@@ -1588,7 +1604,7 @@
             jax.ShapeDtypeStruct((tok, width), bf16),
             jax.ShapeDtypeStruct((cols, 32, in_width), bf16),
             jax.ShapeDtypeStruct((cols, 2 * rows, units), bf16),
-            jax.ShapeDtypeStruct((32, width), f32),
+            jax.ShapeDtypeStruct((2 * rows, width // 2), f32),
             jax.ShapeDtypeStruct((block, width), f32),
         ),
         in_specs=[pl.BlockSpec(memory_space=pltpu.SMEM)] + [vmem] * 12,

time: 134 us -> 128 us (0.955)
  Pallas kernels: 133 us -> 127 us
    pallas_call x1, Pallas kernels: 131 us -> 125 us  [fast_shards(): pl.pallas_call(functools.partial(fused, depth), out_shape=(jax.ShapeDtype...]
where the time goes in v5:
time: 128 us
  Pallas kernels  127 us (99%)
    pallas_call x1, Pallas kernels, fast_shards(): pl.pallas_call(functools.partial(fused, depth), out_shape=(jax.ShapeDtype...  125 us
    pallas_call x1, Pallas kernels, fast_shards(): pl.pallas_call(functools.partial(unpack, rows, block), out_shape=(jax.Sha...  2.7 us

profile of v5, /device:TPU:0, one launch (start us, length us, event | category | flops | bytes accessed | tf_op | source)
XLA Modules:
  0.0 128.1 jit_solution(3394206671576657870)
XLA Ops:
  0.6 124.8 %layer.1 = (bf16[128,768]{1,0:T(8,128)(2,1)}, bf16[128,768]{1,0:T(8,128)(2,1)}, bf16[4,32,640]{2,1,0:T(8,128)(2,1)}, bf16[4,48,768]{2,1,0:T(8,128)(2,1)}, f32[48,384]{1,0:T(8,128)}, /*index=5*/f32[96,768]{1,0:T(8,128)}) custom-call(s32[1,8]{1,0:T(1,128)} %lens.1, f32[8,128]{1,0:T(8,128)} %constant.2.clone.freq, bf16[128,768]{1,0:T(8,128)(2,1)} %bitcast.6, ...), custom_call_target="tpu_custom_call" | custom-call | flops 7247757312 | bytes 8388608 | tf_op jit(solution)/shard_map/layer/pallas_call | solution.py:1600
  125.4 2.7 %unpack.1 = (bf16[1,128,768]{2,1,0:T(8,128)(2,1)}, bf16[1,128,768]{2,1,0:T(8,128)(2,1)}, f32[24,2304]{1,0:T(8,128)}, f32[24,768]{1,0:T(8,128)}, f32[24,3072]{1,0...) custom-call(bf16[128,768]{1,0:T(8,128)(2,1)} %get-tuple-element.17.o, ...), custom_call_target="tpu_custom_call" | custom-call | tf_op jit(solution)/shard_map/unpack/pallas_call | solution.py:1639

commit v6 on v5

--- a/solution.py
+++ b/solution.py
@@ -381,7 +381,7 @@
 LANES = 128
 HALF = 64
 QUART = 32
-DTF = 48
+DTF = 64
 DTB = 64
 
 
@@ -705,23 +705,33 @@
     depth,
     lens,
     freq,
-    xin,
+    xin_at,
+    cot_at,
+    in_at,
+    gate_at,
+    up_at,
+    out_at,
+    down_at,
+    gain_a,
+    bias_a,
+    gain_b,
+    bias_b,
+    outputs_to,
+    input_grad_to,
+    g_in_to,
+    g_mlp_to,
+    g_out_to,
+    g_down_to,
     cot,
     in_rows,
     gate_rows,
     up_rows,
     out_rows,
-    p_down,
-    gain_a,
-    bias_a,
-    gain_b,
-    bias_b,
     outputs,
     input_grad,
-    g_in,
-    g_mlp,
     g_out,
     g_down,
+    local_sem,
     xs,
     p_in,
     p_mlp,
@@ -788,7 +798,7 @@
     recv_sem,
 ):
     planes, cols = depth, 4
-    tok = xin.shape[0]
+    tok = xin_at.shape[0]
     row_len = tok * cols
     place = Plane(planes)
     dp, blk = place.dp, place.blk
@@ -807,6 +817,22 @@
         return (blk + cols - k) % cols
 
     lanes = range(1, cols)
+    local = []
+
+    def move(source, target):
+        copy = pltpu.make_async_copy(source, target, local_sem.at[len(local)])
+        local.append(copy)
+        copy.start()
+        return copy
+
+    xin = xs.at[blk]
+    in_load = move(in_at, in_rows)
+    out_load = move(out_at, out_rows)
+    down_load = move(down_at, w_down.at[dp])
+    x_load = move(xin_at, xin)
+    gate_load = move(gate_at, gate_rows)
+    up_load = move(up_at, up_rows)
+    cot_load = move(cot_at, cot)
     wire = Wire(send_sem, recv_sem, place.inner == 1)
     barrier = pltpu.get_barrier_semaphore()
     peers = [place.side, place.at(place.partner), place.at(place.other)]
@@ -821,7 +847,7 @@
 
 
     rows = 24
-    width = xin.shape[1]
+    width = xin_at.shape[1]
     lane_ids = lax.broadcasted_iota(jnp.int32, (1, LANES), 1)
     low_half = lane_ids < HALF
     head_width = width // cols
@@ -833,6 +859,7 @@
         free_lane == lax.broadcasted_iota(jnp.int32, (8, LANES), 1), 1.0, 0.0
     ).astype(bf16)
     vector_columns = tm(vectors_tab[...].astype(bf16), to_lane)[0:rows]
+    in_load.wait()
     joined_rows = in_rows[...].astype(f32)
     for j in range(cols):
         starts = [kind * width + j * head_width for kind in range(3)]
@@ -851,6 +878,7 @@
         p_in[j] = jnp.concatenate(
             [packed, jnp.zeros((8, packed.shape[1]), f32)], axis=0
         ).astype(bf16)
+    out_load.wait()
     halved = [out_rows[:, n * width // 2 : (n + 1) * width // 2].astype(f32) for n in range(2)]
     s_out[blk, dp] = jnp.concatenate(halved, axis=0).astype(bf16)
     pl.semaphore_wait(barrier, len(peers) + place.inner)
@@ -898,7 +926,7 @@
         return total + inbox[2, cut].astype(f32)
 
     in_slots = to_lanes(lambda to: p_in.at[to], r_in)
-    w_down[dp] = p_down[...]
+    down_load.wait()
     tail = 0
     out_spread = Spread(wire, place, s_out.at[blk], 0)
     out_spread.start()
@@ -908,6 +936,8 @@
     down_spread.start()
     down_spread.start_out()
     down_spread.start_side()
+    gate_load.wait()
+    up_load.wait()
     units = gate_rows.shape[1] // cols
     unit_block = units // (planes * 2)
     for at, weight in ((0, gate_rows), (rows, up_rows)):
@@ -927,7 +957,7 @@
             )
             p_mlp[j, at : at + rows] = packed.astype(bf16)
     mlp_slots = to_lanes(lambda to: p_mlp.at[to], r_mlp)
-    xs[blk] = xin[...]
+    x_load.wait()
     x_slots = gather_start(xin, xs)
     r_in[blk] = p_in[blk]
     r_mlp[blk] = p_mlp[blk]
@@ -975,9 +1005,13 @@
     gate_spread.start()
     gate_spread.start_side()
     up_spread.start()
-    for j in (2, 0, 1):
-        out_spread.relay(j)
+    out_spread.relay(2)
+    for spread in (out_spread, down_spread):
+        spread.relay(0, inner=True)
+        spread.relay(1, inner=True)
     in_spread.relay(2)
+    out_spread.relay(0, inner=False)
+    out_spread.relay(1, inner=False)
     in_spread.relay(0)
     down_spread.relay(2)
     in_spread.relay(1)
@@ -1063,8 +1097,6 @@
     gather_relay(out_lanes, s_out, shards_here)
     gate_spread.relay(0, inner=False)
     gate_spread.relay(1, inner=False)
-    down_spread.relay(0, inner=True)
-    down_spread.relay(1, inner=True)
     for j in range(2):
         down_spread.pass_tail(j)
     gather_done(out_lanes, s_out, shards_here)
@@ -1159,6 +1191,7 @@
 
     lax.fori_loop(0, width // wide, contract, 0)
     pieces = 4
+    cot_load.wait()
     halves = [pl.ds(n * tok // pieces, tok // pieces) for n in range(pieces)]
     mix_slots = [sum_start(s_mix, r_mix, cut) for cut in halves]
     for slots, cut in zip(mix_slots, halves):
@@ -1175,6 +1208,7 @@
         dres_two[cut, :] = d_two
         dms[blk, cut] = d_two.astype(bf16)
         dm_slots.append(gather_start(dms.at[blk], dms, cut))
+    writes = [move(outputs, outputs_to)]
     for slots, cut in zip(dm_slots, halves):
         gather_relay(slots, dms, cut)
     for slots, cut in zip(dm_slots, halves):
@@ -1380,6 +1414,7 @@
     up_sum.second(0)
     grad_in = dres_one[...] + sum_done(ig_slots, s_ig, r_ig)
     input_grad[...] = grad_in.astype(bf16)
+    writes.append(move(input_grad, input_grad_to))
     in_sum.first(1)
     in_sum.first(0)
     up_total = up_sum.total()
@@ -1397,7 +1432,7 @@
     out_sum.second(1)
     out_sum.second(0)
     from_lanes(gmlp_slots, r_gmlp)
-    g_mlp[...] = r_gmlp[...]
+    writes.append(move(r_gmlp, g_mlp_to))
     in_total = in_sum.total()
     for j in range(cols):
         s_gin[j] = jnp.concatenate(
@@ -1406,10 +1441,14 @@
     gin_slots = to_lanes(lambda to: s_gin.at[to], r_gin)
     r_gin[blk] = s_gin[blk]
     g_out[...] = out_sum.total()
+    writes.append(move(g_out, g_out_to))
     g_down[...] = down_sum.total()
+    writes.append(move(g_down, g_down_to))
     from_lanes(gin_slots, r_gin)
-    g_in[...] = r_gin[...]
+    writes.append(move(r_gin, g_in_to))
     wire.finish()
+    for write in writes:
+        write.wait()
 
 
 def unpack(
@@ -1530,6 +1569,16 @@
     stacked = scratch(cols, tok, width)
     heads = 3
     buffers = [
+        scratch(tok, width),
+        scratch(rows, 3 * width),
+        scratch(rows, ff),
+        scratch(rows, ff),
+        scratch(rows, width),
+        scratch(tok, width),
+        scratch(tok, width),
+        scratch(2 * rows, width // 2, kind=f32),
+        scratch(block, width, kind=f32),
+        pltpu.SemaphoreType.DMA((16,)),
         stacked,
         scratch(cols, 32, in_width),
         scratch(cols, 2 * rows, units),
@@ -1596,6 +1645,7 @@
         pltpu.SemaphoreType.DMA((240,)),
     ]
     vmem = pl.BlockSpec(memory_space=pltpu.VMEM)
+    anywhere = pl.BlockSpec(memory_space=pl.ANY)
     tokens = row_len * width
     outputs, input_grad, g_in, g_mlp, g_out, g_down = pl.pallas_call(
         functools.partial(fused, depth),
@@ -1607,8 +1657,8 @@
             jax.ShapeDtypeStruct((2 * rows, width // 2), f32),
             jax.ShapeDtypeStruct((block, width), f32),
         ),
-        in_specs=[pl.BlockSpec(memory_space=pltpu.SMEM)] + [vmem] * 12,
-        out_specs=(vmem,) * 6,
+        in_specs=[pl.BlockSpec(memory_space=pltpu.SMEM), vmem] + [anywhere] * 7 + [vmem] * 4,
+        out_specs=(anywhere,) * 6,
         scratch_shapes=buffers,
         compiler_params=pltpu.CompilerParams(
             collective_id=0, has_side_effects=True, vmem_limit_bytes=60 * 2**20

time: 128 us -> 127 us (level)
  no operation moved by 1% of the time
where the time goes in v6:
time: 127 us
  Pallas kernels  126 us (99%)
    pallas_call x1, Pallas kernels, fast_shards(): pl.pallas_call(functools.partial(fused, depth), out_shape=(jax.ShapeDtype...  124 us
    pallas_call x1, Pallas kernels, fast_shards(): pl.pallas_call(functools.partial(unpack, rows, block), out_shape=(jax.Sha...  2.7 us

profile of v6, /device:TPU:0, one launch (start us, length us, event | category | flops | bytes accessed | tf_op | source)
XLA Modules:
  0.0 127.0 jit_solution(13271188221608906279)
XLA Ops:
  0.6 123.7 %layer.1 = (bf16[128,768]{1,0:T(8,128)(2,1)}, bf16[128,768]{1,0:T(8,128)(2,1)}, bf16[4,32,640]{2,1,0:T(8,128)(2,1)}, bf16[4,48,768]{2,1,0:T(8,128)(2,1)}, f32[48,384]{1,0:T(8,128)}, /*index=5*/f32[96,768]{1,0:T(8,128)}) custom-call(s32[1,8]{1,0:T(1,128)} %lens.1, f32[8,128]{1,0:T(8,128)} %constant.2.clone.freq, bf16[128,768]{1,0:T(8,128)(2,1)} %bitcast.6, ...), custom_call_target="tpu_custom_call" | custom-call | flops 7247757312 | bytes 8388608 | tf_op jit(solution)/shard_map/layer/pallas_call | solution.py:1650
  124.3 2.7 %unpack.1 = (bf16[1,128,768]{2,1,0:T(8,128)(2,1)}, bf16[1,128,768]{2,1,0:T(8,128)(2,1)}, f32[24,2304]{1,0:T(8,128)}, f32[24,768]{1,0:T(8,128)}, f32[24,3072]{1,0...) custom-call(bf16[128,768]{1,0:T(8,128)(2,1)} %get-tuple-element.17.o, ...), custom_call_target="tpu_custom_call" | custom-call | tf_op jit(solution)/shard_map/unpack/pallas_call | solution.py:1689

commit v7 on v6

--- a/solution.py
+++ b/solution.py
@@ -527,8 +527,8 @@
         own = self.block(p.z, p.x)
         wire.push(own, own, p.side, self.x_slots[3])
         if self.main < self.height:
-            rest = self.target.at[p.dp, self.main : self.height]
-            self.rest_slot = wire.push(rest, rest, p.side)
+            self.out_slots = []
+            self.rest_slot = wire.push(self.rest(p.x), self.rest(p.x), p.side)
 
     def tail(self):
         p, wire = self.place, self.wire
@@ -537,8 +537,14 @@
         self.t_slots = [wire.slot() for _ in range(3)]
         self.along(self.pair(p.z), self.t_slots)
 
-    def tail_out(self):
-        self.outward(self.pair(self.place.z), self.t_slots)
+    def rest(self, column):
+        p = self.place
+        return self.target.at[p.z * 2 + column, self.main : self.height]
+
+    def tail_out(self, own):
+        p, wire = self.place, self.wire
+        rest = self.rest(p.x if own else 1 - p.x)
+        self.out_slots.append(wire.push(rest, rest, p.at(p.partner), inner=True))
 
     def relay(self, j, inner=None):
         p, wire = self.place, self.wire
@@ -577,12 +583,18 @@
 
     def settle_tail(self):
         p, wire = self.place, self.wire
-        wire.arrive(self.t_slots[2], self.pair(p.order[2]), p.side)
+
+        @pl.when(wire.is_inner)
+        def _():
+            wire.arrive(self.t_slots[2], self.pair(p.order[2]), p.side)
 
         @pl.when(jnp.logical_not(wire.is_inner))
         def _():
             for j in range(2):
                 wire.arrive(self.t_slots[j], self.pair(p.order[j]), p.side)
+            for slot, column in zip(self.out_slots, (p.x, 1 - p.x)):
+                came = self.target.at[p.partner * 2 + column, self.main : self.height]
+                wire.arrive(slot, came, p.side)
 
     def settle(self):
         p = self.place
@@ -740,6 +752,7 @@
     r_mlp,
     s_out,
     w_in,
+    w_value,
     w_gate,
     w_up,
     w_down,
@@ -936,6 +949,7 @@
     down_spread.start()
     down_spread.start_out()
     down_spread.start_side()
+    down_spread.tail_out(True)
     gate_load.wait()
     up_load.wait()
     units = gate_rows.shape[1] // cols
@@ -989,8 +1003,27 @@
         )
 
     from_lanes(in_slots, r_in)
+    own_rows = cols * rows
+    fold_rows = own_rows // 2
+    heads_width = 4 * LANES
+
+    def folded(last, tile):
+        fold = jnp.where(low_half, last[0:fold_rows], pltpu.roll(last[fold_rows:], HALF, 1))
+        chunks = [fold[n * 16 : (n + 1) * 16] for n in range(3)]
+        chunks.append(jnp.concatenate([tile, jnp.zeros((8, LANES), f32)], axis=0))
+        return jnp.concatenate(chunks, axis=1)
+
+    def unfolded(below):
+        fold = jnp.concatenate([below[:, n * LANES : (n + 1) * LANES] for n in range(3)], axis=0)
+        return jnp.concatenate([fold, pltpu.roll(fold, HALF, 1)], axis=0), below[0:8, 3 * LANES :]
+
+    gathered = jnp.concatenate(
+        [r_in[j, 0:rows, :].astype(f32) for j in range(cols)], axis=0
+    )
+    last = gathered[:, heads_width:]
+    padded = jnp.concatenate([last, jnp.zeros((LANES - own_rows, LANES), f32)], axis=0)
     w_in[dp] = jnp.concatenate(
-        [r_in[j, 0:rows, :].astype(f32) for j in range(cols)], axis=0
+        [gathered[:, :heads_width], folded(last, mt(to_lane, padded.astype(bf16)))], axis=0
     ).astype(bf16)
     in_spread = Spread(wire, place, w_in, tail)
     in_spread.start()
@@ -1033,11 +1066,17 @@
     group = 2
     chunk = group * tok
 
+    tiles = []
+    for d in range(planes * 2):
+        values, tile = unfolded(w_in[d, own_rows:, :].astype(f32))
+        w_value[d] = jnp.where(low_half, values, 0.0).astype(bf16)
+        tiles.append(tile)
+
     def project(step, carry):
         start = pl.multiple_of(step * chunk, chunk)
         here = pl.ds(start, chunk)
         tokens = xs[pl.ds(step * group, group)].reshape(chunk, width)
-        joined = mm(tokens, w_in[...].reshape(width, w_in.shape[2]))
+        joined = mm(tokens, w_in[:, 0:own_rows, :].reshape(width, heads_width))
         cosine, sine = cos_tab[here, :], sin_tab[here, :]
 
         def rotate(number):
@@ -1053,7 +1092,7 @@
         both = rotate(3)
         qm[2, here, :] = jnp.where(low_half, both.astype(bf16).astype(f32) * scale, 0.0).astype(bf16)
         kw[1, here, :] = jnp.where(low_half, pltpu.roll(both, HALF, 1), 0.0).astype(bf16)
-        vw[1, here, :] = joined[:, 4 * LANES : 5 * LANES].astype(bf16)
+        vw[1, here, :] = mm(tokens, w_value[...].reshape(width, LANES)).astype(bf16)
         return carry
 
     lax.fori_loop(0, cols // group, project, 0)
@@ -1093,7 +1132,7 @@
     att_slots = to_lanes(lambda to: s_att.at[to], r_att)
     r_att[blk] = s_att[blk]
 
-    down_spread.tail_out()
+    down_spread.tail_out(False)
     gather_relay(out_lanes, s_out, shards_here)
     gate_spread.relay(0, inner=False)
     gate_spread.relay(1, inner=False)
@@ -1118,8 +1157,14 @@
         w_out[quarter, head_rows:, :] = jnp.zeros(
             (w_out.shape[1] - head_rows, width), bf16
         )
-    last_window = w_in[:, :, 4 * LANES : 5 * LANES].reshape(width, LANES)
-    params[...] = mt(to_lane, last_window)
+    for n in range(width // LANES):
+        first = n * LANES
+        result = None
+        for d in range(first // own_rows, (first + LANES - 1) // own_rows + 1):
+            begin = d * own_rows - first
+            piece = pltpu.roll(tiles[d], begin % LANES, 1)
+            result = piece if result is None else jnp.where(lane_ids < begin, result, piece)
+        params[:, first : first + LANES] = result
     gain_one, bias_one = params[0:1, :], params[1:2, :]
     gain_two, bias_two = params[2:3, :], params[3:4, :]
 
@@ -1377,21 +1422,25 @@
 
     up_sum.first(1)
 
-    def with_vectors(product, here):
-        columns = tm(params[:, here].astype(bf16), to_lane)
-        last = product[:, 4 * LANES :] + columns
-        return jnp.concatenate([product[:, : 4 * LANES], last], axis=1)
-
-    fill_parts(
-        in_sum.part,
-        lambda here: xs[:, :, here].reshape(row_len, half * block),
-        lambda: dj[...],
-        with_vectors,
-    )
+    def input_parts(step, carry):
+        here = pl.ds(pl.multiple_of(step * half * own_rows, LANES), half * own_rows)
+        product = tm(xs[:, :, here].reshape(row_len, half * own_rows), dj[...])
+        vectors = params[:, here]
+        for j in range(half):
+            mine_rows = product[j * own_rows : (j + 1) * own_rows]
+            tile = jnp.where(lane_ids < own_rows, window_at(vectors, j * own_rows), 0.0)
+            in_sum.part[j % 2, step * (half // 2) + j // 2] = jnp.concatenate(
+                [mine_rows[:, :heads_width], folded(mine_rows[:, heads_width:], tile)], axis=0
+            ).astype(bf16)
+        return carry
+
+    lax.fori_loop(0, planes * 2 // half, input_parts, 0)
 
     def input_grads(step, carry):
         here = pl.ds(pl.multiple_of(step * half * block, LANES), half * block)
-        mixed = mt(dj[...], w_in[pl.ds(step * half, half)].reshape(half * block, w_in.shape[2]))
+        those = pl.ds(step * half, half)
+        mixed = mt(dj[:, 0:heads_width], w_in[those, 0:own_rows].reshape(half * block, heads_width))
+        mixed = mixed + mt(dj[:, heads_width:], w_value[those].reshape(half * block, LANES))
         s_ig[:, :, here] = mixed.reshape(cols, tok, half * block).astype(bf16)
         return carry
 
@@ -1404,8 +1453,8 @@
     gate_sum.second(0)
     out_sum.part[...] = sum_done(out_blk, b_out, rb_out, both_sides).astype(bf16)
     in_sum.send((1, 0, 2))
+    in_sum.send_side(3)
     out_sum.send((1, 0, 2))
-    in_sum.send_side(3)
     out_sum.send_side(3)
     down_sum.tail()
     up_sum.second(1)
@@ -1434,6 +1483,11 @@
     from_lanes(gmlp_slots, r_gmlp)
     writes.append(move(r_gmlp, g_mlp_to))
     in_total = in_sum.total()
+    values, tile = unfolded(in_total[own_rows:])
+    columns = tm(tile.astype(bf16), to_lane)[0:own_rows]
+    in_total = jnp.concatenate(
+        [in_total[0:own_rows], jnp.where(low_half, values, columns)], axis=1
+    )
     for j in range(cols):
         s_gin[j] = jnp.concatenate(
             [in_total[j * rows : (j + 1) * rows], jnp.zeros((8, in_total.shape[1]), f32)], axis=0
@@ -1586,7 +1640,8 @@
         scratch(cols, 32, in_width),
         scratch(cols, 2 * rows, units),
         scratch(cols, ring, 2 * rows, width // 2),
-        scratch(ring, cols * rows, in_width),
+        scratch(ring, cols * rows + 16, 4 * LANES),
+        scratch(ring, cols * rows, LANES),
         scratch(ring, cols * rows, units),
         scratch(ring, cols * rows, units),
         scratch(ring, block, width),
@@ -1628,7 +1683,7 @@
         stacked,
         scratch(3, tok, width),
         scratch(tok, width),
-        sums(cols * rows, in_width),
+        sums(cols * rows + 16, 4 * LANES),
         sums(cols * rows, units),
         sums(cols * rows, units),
         sums(block, width, DTB),

time: 127 us -> 126 us (level)
    pallas_call x1, Pallas kernels: 124 us -> 122 us  [fast_shards(): pl.pallas_call(functools.partial(fused, depth), out_shape=(jax.ShapeDtype...]
where the time goes in v7:
time: 126 us; the launch traced here: 125 us
  Pallas kernels  125 us (99%)
    pallas_call x1, Pallas kernels, fast_shards(): pl.pallas_call(functools.partial(fused, depth), out_shape=(jax.ShapeDtype...  122 us
    pallas_call x1, Pallas kernels, fast_shards(): pl.pallas_call(functools.partial(unpack, rows, block), out_shape=(jax.Sha...  2.7 us

profile of v7, /device:TPU:0, one launch (start us, length us, event | category | flops | bytes accessed | tf_op | source)
XLA Modules:
  0.0 125.5 jit_solution(3973722424058924957)
XLA Ops:
  0.6 122.1 %layer.1 = (bf16[128,768]{1,0:T(8,128)(2,1)}, bf16[128,768]{1,0:T(8,128)(2,1)}, bf16[4,32,640]{2,1,0:T(8,128)(2,1)}, bf16[4,48,768]{2,1,0:T(8,128)(2,1)}, f32[48,384]{1,0:T(8,128)}, /*index=5*/f32[96,768]{1,0:T(8,128)}) custom-call(s32[1,8]{1,0:T(1,128)} %lens.1, f32[8,128]{1,0:T(8,128)} %constant.2.clone.freq, bf16[128,768]{1,0:T(8,128)(2,1)} %bitcast.6, ...), custom_call_target="tpu_custom_call" | custom-call | flops 7247757312 | bytes 8388608 | tf_op jit(solution)/shard_map/layer/pallas_call | solution.py:1705
  122.8 2.7 %unpack.1 = (bf16[1,128,768]{2,1,0:T(8,128)(2,1)}, bf16[1,128,768]{2,1,0:T(8,128)(2,1)}, f32[24,2304]{1,0:T(8,128)}, f32[24,768]{1,0:T(8,128)}, f32[24,3072]{1,0...) custom-call(bf16[128,768]{1,0:T(8,128)(2,1)} %get-tuple-element.17.o, ...), custom_call_target="tpu_custom_call" | custom-call | tf_op jit(solution)/shard_map/unpack/pallas_call | solution.py:1744

commit v8 on v7

--- a/solution.py
+++ b/solution.py
@@ -608,8 +608,11 @@
         self.part, self.inbox, self.staged, self.landing = buffers[:4]
         self.height, self.main = self.part.shape[2], self.inbox.shape[1]
         self.split = self.main < self.height
+        self.x_slots = [wire.slot() for _ in range(4)]
+        self.z_slots = [wire.slot() for _ in range(4)]
         if self.split:
             self.t_landing, self.t_staged, self.t_cross, self.t_kept = buffers[4:]
+            self.t_slots = [wire.slot() for _ in range(4)]
 
     def pair(self, plane):
         return self.part.at[:, plane, self.main : self.height]
@@ -625,21 +628,19 @@
         )
 
     def send(self, order=(1, 0, 2, 3)):
-        p, wire = self.place, self.wire
-        self.x_slots = [wire.slot() for _ in range(4)]
         for j in order:
             self.send_side(j)
-        self.z_slots = [wire.slot() for _ in range(4)]
-        if self.split:
-            self.t_slots = [wire.slot() for _ in range(4)]
-            for j in (1, 0, 2):
-                wire.push(
-                    self.pair(p.order[j]),
-                    self.t_landing.at[j],
-                    p.at(p.partner),
-                    self.t_slots[j],
-                    inner=None if j == 2 else False,
-                )
+
+    def send_tails(self):
+        p = self.place
+        for j in (1, 0, 2):
+            self.wire.push(
+                self.pair(p.order[j]),
+                self.t_landing.at[j],
+                p.at(p.partner),
+                self.t_slots[j],
+                inner=None if j == 2 else False,
+            )
 
     def first(self, j):
         p, wire = self.place, self.wire
@@ -774,6 +775,8 @@
     gate_pre,
     up_pre,
     act,
+    act_t,
+    hs_t,
     s_mix,
     r_mix,
     t_mix,
@@ -1223,6 +1226,7 @@
         act[:, here] = (gate / (1.0 + jnp.exp(-gate)) * up).astype(bf16)
 
     each_strip(expand_gate)
+    hs_t[...] = hs[...].reshape(row_len, width).T
     up_spread.settle()
     each_strip(expand_up)
     down_spread.settle()
@@ -1241,6 +1245,7 @@
     mix_slots = [sum_start(s_mix, r_mix, cut) for cut in halves]
     for slots, cut in zip(mix_slots, halves):
         sum_relay(slots, s_mix, r_mix, t_mix, cut)
+    act_t[...] = act[...].T
     second_gain, second_bias, dm_slots = 0.0, 0.0, []
     for slots, cut in zip(mix_slots, halves):
         mlp_out = sum_done(slots, s_mix, r_mix, cut)
@@ -1271,7 +1276,7 @@
 
         def step_fn(step, carry):
             here = pl.ds(pl.multiple_of(step * half * height, LANES), half * height)
-            product = more(tm(left_of(here), right()), here)
+            product = more(mm(left_of(here), right()), here)
             for j in range(half):
                 part[j % 2, step * (half // 2) + j // 2] = product[
                     j * height : (j + 1) * height
@@ -1280,8 +1285,9 @@
 
         lax.fori_loop(0, planes * 2 // half, step_fn, 0)
 
-    fill_parts(down_sum.part, lambda here: act[:, here], lambda: dms[...].reshape(row_len, width))
-    down_sum.send()
+    fill_parts(down_sum.part, lambda here: act_t[here, :], lambda: dms[...].reshape(row_len, width))
+    down_sum.send((1, 0,))
+    down_sum.send_tails()
 
     block = w_down.shape[1]
 
@@ -1301,7 +1307,7 @@
     block = w_gate.shape[1]
 
     def hidden_rows(here):
-        return hs[:, :, here].reshape(row_len, half * block)
+        return hs_t[here, :]
 
     fill_parts(gate_sum.part, hidden_rows, lambda: dgate[...])
     gate_sum.send()
@@ -1319,11 +1325,10 @@
 
     sum_relay(dh_slots, s_dh, r_dh, t_dh)
     fill_parts(up_sum.part, hidden_rows, lambda: dup[...])
-    up_sum.send()
+    up_sum.send((1, 0))
     down_sum.first(1)
     down_sum.first(0)
     d_hidden = dres_two[...] + sum_done(dh_slots, s_dh, r_dh)
-    down_sum.first(2)
     normal = norm_one[...]
     first_gain = column_sum(d_hidden * normal)
     first_bias = column_sum(d_hidden)
@@ -1420,7 +1425,6 @@
     dj[:, 3 * LANES : 4 * LANES] = rotate_back(acc_q[1] + pltpu.roll(acc_k[1], HALF, 1))
     dj[:, 4 * LANES : 5 * LANES] = acc_v[1].astype(bf16)
 
-    up_sum.first(1)
 
     def input_parts(step, carry):
         here = pl.ds(pl.multiple_of(step * half * own_rows, LANES), half * own_rows)
@@ -1436,6 +1440,7 @@
 
     lax.fori_loop(0, planes * 2 // half, input_parts, 0)
 
+    in_sum.send((1, 0))
     def input_grads(step, carry):
         here = pl.ds(pl.multiple_of(step * half * block, LANES), half * block)
         those = pl.ds(step * half, half)
@@ -1447,25 +1452,38 @@
     lax.fori_loop(0, planes * 2 // half, input_grads, 0)
     ig_slots = sum_start(s_ig, r_ig)
 
+    up_sum.first(1)
     gate_sum.second(1)
     sum_relay(ig_slots, s_ig, r_ig, t_ig)
+    out_sum.part[...] = sum_done(out_blk, b_out, rb_out, both_sides).astype(bf16)
+    out_sum.send((1, 0,))
+    up_sum.send((2,))
+    in_sum.send((2,))
+    up_sum.send((3,))
+    in_sum.send((3,))
+    down_sum.send((2,))
+    out_sum.send((2,))
+    out_sum.send((3,))
+    down_sum.send((3,))
+    down_sum.tail()
     up_sum.first(0)
     gate_sum.second(0)
-    out_sum.part[...] = sum_done(out_blk, b_out, rb_out, both_sides).astype(bf16)
-    in_sum.send((1, 0, 2))
-    in_sum.send_side(3)
-    out_sum.send((1, 0, 2))
-    out_sum.send_side(3)
-    down_sum.tail()
+    in_sum.first(1)
     up_sum.second(1)
+    in_sum.first(0)
+    out_sum.first(1)
+    out_sum.first(0)
+    up_sum.second(0)
+    f_gate[...] = gate_sum.total()
+    in_sum.second(1)
     up_sum.first(2)
-    f_gate[...] = gate_sum.total()
-    up_sum.second(0)
     grad_in = dres_one[...] + sum_done(ig_slots, s_ig, r_ig)
     input_grad[...] = grad_in.astype(bf16)
     writes.append(move(input_grad, input_grad_to))
-    in_sum.first(1)
-    in_sum.first(0)
+    in_sum.second(0)
+    out_sum.second(1)
+    out_sum.second(0)
+    in_sum.first(2)
     up_total = up_sum.total()
     gate_total = f_gate[...]
     for j in range(cols):
@@ -1473,15 +1491,8 @@
         s_gmlp[j] = jnp.concatenate([gate_total[here], up_total[here]], axis=0).astype(bf16)
     gmlp_slots = to_lanes(lambda to: s_gmlp.at[to], r_gmlp)
     r_gmlp[blk] = s_gmlp[blk]
-    in_sum.second(1)
-    in_sum.first(2)
-    in_sum.second(0)
-    for j in (1, 0, 2):
-        out_sum.first(j)
-    out_sum.second(1)
-    out_sum.second(0)
-    from_lanes(gmlp_slots, r_gmlp)
-    writes.append(move(r_gmlp, g_mlp_to))
+    out_sum.first(2)
+    down_sum.first(2)
     in_total = in_sum.total()
     values, tile = unfolded(in_total[own_rows:])
     columns = tm(tile.astype(bf16), to_lane)[0:own_rows]
@@ -1498,6 +1509,8 @@
     writes.append(move(g_out, g_out_to))
     g_down[...] = down_sum.total()
     writes.append(move(g_down, g_down_to))
+    from_lanes(gmlp_slots, r_gmlp)
+    writes.append(move(r_gmlp, g_mlp_to))
     from_lanes(gin_slots, r_gin)
     writes.append(move(r_gin, g_in_to))
     wire.finish()
@@ -1663,6 +1676,8 @@
         scratch(row_len, units, kind=f32),
         scratch(row_len, units, kind=f32),
         scratch(row_len, units),
+        scratch(units, row_len),
+        scratch(width, row_len),
         stacked,
         scratch(3, tok, width),
         scratch(tok, width),

time: 126 us -> 124 us (0.984)
  Pallas kernels: 125 us -> 123 us
    pallas_call x1, Pallas kernels: 122 us -> 121 us  [fast_shards(): pl.pallas_call(functools.partial(fused, depth), out_shape=(jax.ShapeDtype...]
where the time goes in v8:
time: 124 us
  Pallas kernels  123 us (99%)
    pallas_call x1, Pallas kernels, fast_shards(): pl.pallas_call(functools.partial(fused, depth), out_shape=(jax.ShapeDtype...  121 us
    pallas_call x1, Pallas kernels, fast_shards(): pl.pallas_call(functools.partial(unpack, rows, block), out_shape=(jax.Sha...  2.7 us

profile of v8, /device:TPU:0, one launch (start us, length us, event | category | flops | bytes accessed | tf_op | source)
XLA Modules:
  0.0 124.1 jit_solution(8538153558511371859)
XLA Ops:
  0.6 120.8 %layer.1 = (bf16[128,768]{1,0:T(8,128)(2,1)}, bf16[128,768]{1,0:T(8,128)(2,1)}, bf16[4,32,640]{2,1,0:T(8,128)(2,1)}, bf16[4,48,768]{2,1,0:T(8,128)(2,1)}, f32[48,384]{1,0:T(8,128)}, /*index=5*/f32[96,768]{1,0:T(8,128)}) custom-call(s32[1,8]{1,0:T(1,128)} %lens.1, f32[8,128]{1,0:T(8,128)} %constant.2.clone.freq, bf16[128,768]{1,0:T(8,128)(2,1)} %bitcast.6, ...), custom_call_target="tpu_custom_call" | custom-call | flops 7247757312 | bytes 8388608 | tf_op jit(solution)/shard_map/layer/pallas_call | solution.py:1720
  121.4 2.7 %unpack.1 = (bf16[1,128,768]{2,1,0:T(8,128)(2,1)}, bf16[1,128,768]{2,1,0:T(8,128)(2,1)}, f32[24,2304]{1,0:T(8,128)}, f32[24,768]{1,0:T(8,128)}, f32[24,3072]{1,0...) custom-call(bf16[128,768]{1,0:T(8,128)(2,1)} %get-tuple-element.17.o, ...), custom_call_target="tpu_custom_call" | custom-call | tf_op jit(solution)/shard_map/unpack/pallas_call | solution.py:1759

commit v9 on v8

--- a/solution.py
+++ b/solution.py
@@ -1191,11 +1191,11 @@
     for quarter in range(1, cols):
         branch = branch + mm(r_att[quarter], w_out[quarter])
     normal, spread_one = normalize(xin[...].astype(f32) + branch)
-    norm_one[...] = normal
     hidden = normal * gain_one + bias_one
-    hid[...] = hidden
     hs[blk] = hidden.astype(bf16)
     hid_slots = gather_start(hs.at[blk], hs)
+    norm_one[...] = normal
+    hid[...] = hidden
     up_spread.relay(0, inner=False)
     up_spread.relay(1, inner=False)
     down_spread.relay(0, inner=False)
@@ -1250,14 +1250,14 @@
     for slots, cut in zip(mix_slots, halves):
         mlp_out = sum_done(slots, s_mix, r_mix, cut)
         normal, spread_two = normalize(hid[cut, :] + mlp_out)
+        grad = cot[cut, :].astype(f32)
+        d_two = normalize_back(grad, normal, spread_two, gain_two)
+        dms[blk, cut] = d_two.astype(bf16)
+        dm_slots.append(gather_start(dms.at[blk], dms, cut))
+        dres_two[cut, :] = d_two
         outputs[cut, :] = (normal * gain_two + bias_two).astype(bf16)
-        grad = cot[cut, :].astype(f32)
         second_gain = second_gain + column_sum(grad * normal)
         second_bias = second_bias + column_sum(grad)
-        d_two = normalize_back(grad, normal, spread_two, gain_two)
-        dres_two[cut, :] = d_two
-        dms[blk, cut] = d_two.astype(bf16)
-        dm_slots.append(gather_start(dms.at[blk], dms, cut))
     writes = [move(outputs, outputs_to)]
     for slots, cut in zip(dm_slots, halves):
         gather_relay(slots, dms, cut)
@@ -1474,7 +1474,6 @@
     out_sum.first(1)
     out_sum.first(0)
     up_sum.second(0)
-    f_gate[...] = gate_sum.total()
     in_sum.second(1)
     up_sum.first(2)
     grad_in = dres_one[...] + sum_done(ig_slots, s_ig, r_ig)
@@ -1484,6 +1483,7 @@
     out_sum.second(1)
     out_sum.second(0)
     in_sum.first(2)
+    f_gate[...] = gate_sum.total()
     up_total = up_sum.total()
     gate_total = f_gate[...]
     for j in range(cols):

time: 124 us -> 124 us (level)
  no operation moved by 1% of the time
where the time goes in v9:
time: 124 us
  Pallas kernels  123 us (99%)
    pallas_call x1, Pallas kernels, fast_shards(): pl.pallas_call(functools.partial(fused, depth), out_shape=(jax.ShapeDtype...  121 us
    pallas_call x1, Pallas kernels, fast_shards(): pl.pallas_call(functools.partial(unpack, rows, block), out_shape=(jax.Sha...  2.7 us

profile of v9, /device:TPU:0, one launch (start us, length us, event | category | flops | bytes accessed | tf_op | source)
XLA Modules:
  0.0 124.1 jit_solution(11724608811241796620)
XLA Ops:
  0.6 120.8 %layer.1 = (bf16[128,768]{1,0:T(8,128)(2,1)}, bf16[128,768]{1,0:T(8,128)(2,1)}, bf16[4,32,640]{2,1,0:T(8,128)(2,1)}, bf16[4,48,768]{2,1,0:T(8,128)(2,1)}, f32[48,384]{1,0:T(8,128)}, /*index=5*/f32[96,768]{1,0:T(8,128)}) custom-call(s32[1,8]{1,0:T(1,128)} %lens.1, f32[8,128]{1,0:T(8,128)} %constant.2.clone.freq, bf16[128,768]{1,0:T(8,128)(2,1)} %bitcast.6, ...), custom_call_target="tpu_custom_call" | custom-call | flops 7247757312 | bytes 8388608 | tf_op jit(solution)/shard_map/layer/pallas_call | solution.py:1720
  121.4 2.7 %unpack.1 = (bf16[1,128,768]{2,1,0:T(8,128)(2,1)}, bf16[1,128,768]{2,1,0:T(8,128)(2,1)}, f32[24,2304]{1,0:T(8,128)}, f32[24,768]{1,0:T(8,128)}, f32[24,3072]{1,0...) custom-call(bf16[128,768]{1,0:T(8,128)(2,1)} %get-tuple-element.17.o, ...), custom_call_target="tpu_custom_call" | custom-call | tf_op jit(solution)/shard_map/unpack/pallas_call | solution.py:1759

commit v10 on v9

--- a/solution.py
+++ b/solution.py
@@ -1286,8 +1286,8 @@
         lax.fori_loop(0, planes * 2 // half, step_fn, 0)
 
     fill_parts(down_sum.part, lambda here: act_t[here, :], lambda: dms[...].reshape(row_len, width))
-    down_sum.send((1, 0,))
     down_sum.send_tails()
+    down_sum.send((1, 0))
 
     block = w_down.shape[1]
 

time: 124 us -> 124 us (level)
  no operation moved by 1% of the time
where the time goes in v10:
time: 124 us
  Pallas kernels  123 us (99%)
    pallas_call x1, Pallas kernels, fast_shards(): pl.pallas_call(functools.partial(fused, depth), out_shape=(jax.ShapeDtype...  121 us
    pallas_call x1, Pallas kernels, fast_shards(): pl.pallas_call(functools.partial(unpack, rows, block), out_shape=(jax.Sha...  2.7 us

profile of v10, /device:TPU:0, one launch (start us, length us, event | category | flops | bytes accessed | tf_op | source)
XLA Modules:
  0.0 124.1 jit_solution(17492869464558699883)
XLA Ops:
  0.6 120.8 %layer.1 = (bf16[128,768]{1,0:T(8,128)(2,1)}, bf16[128,768]{1,0:T(8,128)(2,1)}, bf16[4,32,640]{2,1,0:T(8,128)(2,1)}, bf16[4,48,768]{2,1,0:T(8,128)(2,1)}, f32[48,384]{1,0:T(8,128)}, /*index=5*/f32[96,768]{1,0:T(8,128)}) custom-call(s32[1,8]{1,0:T(1,128)} %lens.1, f32[8,128]{1,0:T(8,128)} %constant.2.clone.freq, bf16[128,768]{1,0:T(8,128)(2,1)} %bitcast.6, ...), custom_call_target="tpu_custom_call" | custom-call | flops 7247757312 | bytes 8388608 | tf_op jit(solution)/shard_map/layer/pallas_call | solution.py:1720
  121.4 2.7 %unpack.1 = (bf16[1,128,768]{2,1,0:T(8,128)(2,1)}, bf16[1,128,768]{2,1,0:T(8,128)(2,1)}, f32[24,2304]{1,0:T(8,128)}, f32[24,768]{1,0:T(8,128)}, f32[24,3072]{1,0...) custom-call(bf16[128,768]{1,0:T(8,128)(2,1)} %get-tuple-element.17.o, ...), custom_call_target="tpu_custom_call" | custom-call | tf_op jit(solution)/shard_map/unpack/pallas_call | solution.py:1759
